TPU v7x, 128 devices: a whole 4x4x4 slice. The times are simulated.
128 devices in a mesh: gx: 16 (over z, y), gy: 8 (over x, core).
Axes of the slice: x: 4, y: 4, z: 4, core: 2. Of those that a mesh axis runs over, the one named last changes fastest.
Arguments:
- sky_bottom_quantities: bfloat16 [2048, 8, 256], P(('gx', 'gy')), may hold values from -6 to 6
- link_weight_array: bfloat16 [2048, 256, 256], P(('gx', 'gy')), as said below
- link_sky_block: int32 [2048], P(('gx', 'gy')), may hold values from 0 to 15
- link_target_device: int32 [2048, 1], P(('gx', 'gy')), may hold values from 0 to 127, as said below
- link_sea_block: int32 [2048], P(('gx', 'gy')), may hold values from 0 to 15
- sea_warmth_anomaly: float32 [2048, 256], P(('gx', 'gy')), may hold values from -6 to 6
- marine_indicator: int32 [2048, 256], P(('gx', 'gy')), may hold values 0 or 1
Outputs:
- sea_top_forcings: float32 [2048, 4, 256], P(('gx', 'gy'))
- atm_back: float32 [2048, 5, 256], P(('gx', 'gy'))
Inputs may be any that keep to these rules, and one draw needn't show every extreme that they name: `link_target_device`: devices are numbered gx-major (index along gx times 8 plus index along gy). Among the pairs of one device at most 2 name the same owner. Exactly 2 pairs of each device name each of these three: the device whose number is its own plus 128 // 2, its own plus 1, and its own minus 1, all taken modulo 128. `link_weight_array`: entries are nonnegative and zero unless the atmosphere cell and the ocean cell lie within 4 of each other modulo 256.
All inputs are finite; a program needn't handle non-finite values. No bound on the sum of `marine_indicator` on one device may be relied on, other than what follows from the above.
Results may differ from a plain program's by a relative error of at most 0.0026.
Values may be sent and summed in bfloat16 or wider, within the bound.
No kernel may reach another device: no remote copies, remote signals or barrier semaphores. Data moves between devices by JAX's collectives and lax.ppermute only.
A program may use at most 64 MiB of HBM per device.

v0:
```python
import jax
import jax.numpy as jnp
from jax import lax
from jax.sharding import PartitionSpec as P


def bulk_exchange_rates(regridded_quantities, sea_warmth_anomaly, marine_indicator):
    marine_points = marine_indicator.astype(jnp.float32)
    wind_u = regridded_quantities[:, 0]
    wind_v = regridded_quantities[:, 1]
    lower_layer_warmth = regridded_quantities[:, 2]
    vapour_moisture = regridded_quantities[:, 3]
    solar_radiation = regridded_quantities[:, 4]
    infrared_radiation = regridded_quantities[:, 5]
    precip = regridded_quantities[:, 6]
    bottom_barometric_load = regridded_quantities[:, 7]
    wind_speed = jnp.sqrt(wind_u * wind_u + wind_v * wind_v + 0.25)
    warmth_contrast = sea_warmth_anomaly - lower_layer_warmth
    moisture_contrast = 0.4 * sea_warmth_anomaly - vapour_moisture + 0.3 * bottom_barometric_load
    upward_lift = warmth_contrast + 0.5 * moisture_contrast
    steadiness_scaling = jnp.zeros_like(sea_warmth_anomaly)
    for iteration in range(3):
        coeff = 1.0 + 0.5 * jnp.tanh(steadiness_scaling)
        steadiness_scaling = 2.0 * upward_lift / (1.0 + coeff * wind_speed * wind_speed)
    coeff = 1.0 + 0.5 * jnp.tanh(steadiness_scaling)
    exchange_coefficient = coeff * wind_speed
    eastward_drag = exchange_coefficient * wind_u * marine_points
    northward_drag = exchange_coefficient * wind_v * marine_points
    warming_balance = (
        0.5 * solar_radiation
        + 0.3 * infrared_radiation
        - exchange_coefficient * warmth_contrast
        - exchange_coefficient * moisture_contrast
    ) * marine_points
    rainfall_minus_evaporation = (
        precip - 0.5 * exchange_coefficient * moisture_contrast
    ) * marine_points
    transfer_result = jnp.stack(
        [eastward_drag, northward_drag, warming_balance, rainfall_minus_evaporation], axis=1
    )
    delivered_quantities = jnp.stack(
        [
            eastward_drag,
            northward_drag,
            warming_balance,
            rainfall_minus_evaporation,
            sea_warmth_anomaly * marine_points,
        ],
        axis=1,
    ).astype(jnp.bfloat16)
    return (transfer_result, delivered_quantities)


def on_device(
    sky_bottom_quantities,
    link_weight_array,
    link_sky_block,
    link_target_device,
    link_sea_block,
    sea_warmth_anomaly,
    marine_indicator,
):
    devices = lax.axis_size(("gx", "gy"))
    pair_count = link_sky_block.shape[0]
    tile_count = sky_bottom_quantities.shape[0]
    field_count = sky_bottom_quantities.shape[1]
    tile_cells = sky_bottom_quantities.shape[2]
    back_count = 5
    capacity = max(2, pair_count // 8)
    slot_count = devices * capacity
    contrib = jnp.einsum(
        "pfa,pat->pft",
        sky_bottom_quantities[link_sky_block],
        link_weight_array,
        preferred_element_type=jnp.float32,
    )
    target = link_target_device[:, 0]
    dest_hits = (target[:, None] == jnp.arange(devices, dtype=jnp.int32)[None, :]).astype(jnp.int32)
    before = jnp.cumsum(dest_hits, axis=0) - dest_hits
    slot_of = target * capacity + jnp.sum(before * dest_hits, axis=1)
    outgoing = (
        jnp.zeros((slot_count, field_count, tile_cells), jnp.float32).at[slot_of].set(contrib)
    )
    labels = jnp.full((slot_count,), -1, jnp.int32).at[slot_of].set(link_sea_block)
    arrived, slot_tiles = (
        lax.all_to_all(
            outgoing.reshape(devices, capacity, field_count, tile_cells),
            ("gx", "gy"),
            split_axis=0,
            concat_axis=0,
            tiled=True,
        ),
        lax.all_to_all(
            labels.reshape(devices, capacity), ("gx", "gy"), split_axis=0, concat_axis=0, tiled=True
        ),
    )
    arrived = arrived.reshape(slot_count, field_count, tile_cells)
    slot_tiles = slot_tiles.reshape(slot_count)
    select = (slot_tiles[:, None] == jnp.arange(tile_count, dtype=jnp.int32)[None, :]).astype(
        jnp.float32
    )
    regridded_quantities = jnp.einsum(
        "sq,sft->qft", select, arrived, precision=lax.Precision.HIGHEST
    )
    transfer_result, delivered_quantities = bulk_exchange_rates(
        regridded_quantities, sea_warmth_anomaly, marine_indicator
    )
    live_slot = (slot_tiles >= 0).astype(jnp.bfloat16)
    picked = (
        delivered_quantities[jnp.clip(slot_tiles, 0, tile_count - 1)] * live_slot[:, None, None]
    )
    returned = lax.all_to_all(
        picked.reshape(devices, capacity, back_count, tile_cells),
        ("gx", "gy"),
        split_axis=0,
        concat_axis=0,
        tiled=True,
    )
    values = returned.reshape(slot_count, back_count, tile_cells)[slot_of]
    back_terms = jnp.einsum(
        "pft,pat->pfa", values, link_weight_array, preferred_element_type=jnp.float32
    )
    tile_select = (
        link_sky_block[:, None] == jnp.arange(tile_count, dtype=jnp.int32)[None, :]
    ).astype(jnp.float32)
    atm_back = jnp.einsum("pq,pfa->qfa", tile_select, back_terms, precision=lax.Precision.HIGHEST)
    return (transfer_result, atm_back)


def solution(mesh):
    placed = (
        P(("gx", "gy"), None, None),
        P(("gx", "gy"), None, None),
        P(("gx", "gy")),
        P(("gx", "gy"), None),
        P(("gx", "gy")),
        P(("gx", "gy"), None),
        P(("gx", "gy"), None),
    )
    return jax.shard_map(
        on_device,
        mesh=mesh,
        in_specs=placed,
        out_specs=(P(("gx", "gy"), None, None), P(("gx", "gy"), None, None)),
        check_vma=False,
    )
```

profile of v0, /device:TPU:1, one launch (start us, length us, event | category | flops | bytes accessed | tf_op | source)
XLA Modules:
  0.0 107.4 jit_solution(11301414742246661377)
XLA Ops:
  0.6 0.9 fusion.25
  1.6 0.8 select_reduce_fusion
  3.1 0.8 scatter_custom_fusion
  3.8 0.8 all_to_all.12
  4.6 11.5 %all-to-all-start = ((s32[128,1,2]{2,1,0:T(1,128)}), s32[128,1,2]{2,1,0:T(1,128)S(1)}, u32[]{:S(2)}, u32[]{:S(2)}) async-start(s32[128,1,2]{2,1,0:T(1,128)} %bitcast.3), calls=%async_computation | async-start | bytes 131072 | tf_op jit(solution)/shard_map/all_to_all | solution.py:93
  16.8 8.9 %all-to-all-done = s32[128,1,2]{2,1,0:T(1,128)S(1)} async-done(((s32[128,1,2]{2,1,0:T(1,128)}), s32[128,1,2]{2,1,0:T(1,128)S(1)}, u32[]{:S(2)}, u32[]{:S(2)}) %all-to-all-start) | async-done | bytes 1056 | tf_op jit(solution)/shard_map/all_to_all | solution.py:93
  26.0 1.4 %gather_fusion = bf16[16,8,256]{2,1,0:T(8,128)(2,1)S(1)} fusion(bf16[16,8,256]{2,1,0:T(8,128)(2,1)} %param.7, s32[1024]{0:T(1024)S(1)} %get-tuple-element.22), kind=kCustom, calls=%fused_computation | custom fusion | bytes 131136 | tf_op jit(solution)/shard_map/gather | solution.py:73
  27.8 1.5 %broadcast_in_dim.7 = f32[256,8,256]{2,1,0:T(8,128)} broadcast(f32[]{:T(128)} %constant.3.clone.1), dimensions={} | broadcast | bytes 2097156 | tf_op jit(solution)/shard_map/broadcast_in_dim | solution.py:82
  29.3 2.2 %scatter_fusion = f32[256,8,256]{2,1,0:T(8,128)} fusion(f32[256,8,256]{2,1,0:T(8,128)} %broadcast_in_dim.7, s32[16]{0:T(128)S(1)} %fusion.30, f32[16,8,256]{2,1,0:T(8,128)S(1)} %fusion.35), kind=kCustom, calls=%fused_computation.4 | custom fusion | bytes 393280 | tf_op jit(solution)/shard_map/scatter | solution.py:82
  31.5 4.0 %copy.32 = f32[128,2,8,256]{3,1,2,0:T(2,128)} copy(f32[128,2,8,256]{3,2,1,0:T(8,128)} %bitcast.121) | data formatting | bytes 4194304 | tf_op jit(solution)/shard_map/reshape | solution.py:87
  35.4 5.3 %all-to-all-start.1 = ((f32[128,2,8,256]{3,1,2,0:T(2,128)}), f32[128,2,8,256]{3,1,2,0:T(2,128)}, u32[]{:S(2)}, u32[]{:S(2)}) async-start(f32[128,2,8,256]{3,1,2,0:T(2,128)} %copy.32), calls=%async_computation.1 | async-start | bytes 4194304 | tf_op jit(solution)/shard_map/all_to_all | solution.py:86
  41.2 0.8 reduce.3
  42.3 28.7 %all-to-all-done.1 = f32[128,2,8,256]{3,1,2,0:T(2,128)} async-done(((f32[128,2,8,256]{3,1,2,0:T(2,128)}), f32[128,2,8,256]{3,1,2,0:T(2,128)}, u32[]{:S(2)}, u32[]{:S(2)}) %all-to-all-start.1) | async-done | bytes 2097184 | tf_op jit(solution)/shard_map/all_to_all | solution.py:86
  71.0 3.7 %copy.33 = f32[128,2,8,256]{3,1,0,2:T(2,128)} copy(f32[128,2,8,256]{3,1,2,0:T(2,128)} %all-to-all-done.1) | data formatting | bytes 4194304 | tf_op jit(solution)/shard_map/all_to_all | solution.py:86
  74.7 3.7 %reshape.68 = f32[256,8,256]{2,0,1:T(8,128)} reshape(f32[128,2,8,256]{3,1,0,2:T(2,128)} %copy.33) | data formatting | bytes 4194304 | tf_op jit(solution)/shard_map/reshape | solution.py:97
  78.4 2.4 %fusion.21 = f32[16,8,256]{2,0,1:T(8,128)S(1)} fusion(f32[256,8,256]{2,0,1:T(8,128)} %reshape.68, s32[256]{0:T(256)S(1)} %eq.47), kind=kOutput, calls=%fused_computation.43 | convolution fusion | flops 100667392 | bytes 2229248 | tf_op jit(solution)/shard_map/sq,sft->qft/dot_general | solution.py:102
  81.0 0.8 gather_fusion.1
  81.7 1.6 %copy_multiply_fusion = bf16[128,2,5,256]{3,1,2,0:T(2,128)(2,1)} fusion(bf16[128,2,5,256]{3,2,1,0:T(8,128)(2,1)S(1)} %bitcast.122, bf16[128,2]{1,0:T(8,128)(2,1)S(1)} %copy.38), kind=kLoop, calls=%fused_computation.5 | loop fusion | flops 327680 | bytes 1311232 | tf_op jit(solution)/shard_map/mul | solution.py:110
  83.3 4.3 %all-to-all-start.2 = ((bf16[128,2,5,256]{3,1,2,0:T(2,128)(2,1)}), bf16[128,2,5,256]{3,1,2,0:T(2,128)(2,1)S(1)}, u32[]{:S(2)}, u32[]{:S(2)}) async-start(bf16[128,2,5,256]{3,1,2,0:T(2,128)(2,1)} %copy_multiply_fusion), calls=%async_computation.2 | async-start | bytes 1310720 | tf_op jit(solution)/shard_map/all_to_all | solution.py:112
  87.7 0.7 copy.42
  88.4 14.6 %all-to-all-done.2 = bf16[128,2,5,256]{3,1,2,0:T(2,128)(2,1)S(1)} async-done(((bf16[128,2,5,256]{3,1,2,0:T(2,128)(2,1)}), bf16[128,2,5,256]{3,1,2,0:T(2,128)(2,1)S(1)}, u32[]{:S(2)}, u32[]{:S(2)}) %all-to-all-start.2) | async-done | bytes 655392 | tf_op jit(solution)/shard_map/all_to_all | solution.py:112
  102.9 1.2 %copy.40 = bf16[128,2,5,256]{3,2,1,0:T(8,128)(2,1)} copy(bf16[128,2,5,256]{3,1,2,0:T(2,128)(2,1)S(1)} %all-to-all-done.2) | data formatting | bytes 1310720 | tf_op jit(solution)/shard_map/all_to_all | solution.py:112
  104.1 1.8 %gather_fusion.2 = bf16[16,5,256]{2,1,0:T(8,128)(2,1)S(1)} fusion(bf16[256,5,256]{2,1,0:T(8,128)(2,1)} %bitcast.123, s32[1024]{0:T(1024)S(1)} %pad_clamp_fusion), kind=kCustom, calls=%fused_computation.2 | custom fusion | bytes 81984 | tf_op jit(solution)/shard_map/gather | solution.py:119
  106.5 0.8 fusion
  (31 shorter events, 3.7 us)
Async XLA Ops:
  0.6 26.8 %copy-start = (bf16[16,256,256]{2,1,0:T(8,128)(2,1)S(1)}, bf16[16,256,256]{2,1,0:T(8,128)(2,1)}, u32[]{:S(2)}) copy-start(bf16[16,256,256]{2,1,0:T(8,128)(2,1)} %param.8) | copy-start | bytes 6291460
  4.6 21.0 %all-to-all-start = ((s32[128,1,2]{2,1,0:T(1,128)}), s32[128,1,2]{2,1,0:T(1,128)S(1)}, u32[]{:S(2)}, u32[]{:S(2)}) async-start(s32[128,1,2]{2,1,0:T(1,128)} %bitcast.3), calls=%async_computation | async-start | bytes 131072 | tf_op jit(solution)/shard_map/all_to_all | solution.py:93
  35.4 35.6 %all-to-all-start.1 = ((f32[128,2,8,256]{3,1,2,0:T(2,128)}), f32[128,2,8,256]{3,1,2,0:T(2,128)}, u32[]{:S(2)}, u32[]{:S(2)}) async-start(f32[128,2,8,256]{3,1,2,0:T(2,128)} %copy.32), calls=%async_computation.1 | async-start | bytes 4194304 | tf_op jit(solution)/shard_map/all_to_all | solution.py:86
  78.4 2.4 %copy-start.1 = (s32[16,256]{1,0:T(8,128)S(1)}, s32[16,256]{1,0:T(8,128)}, u32[]{:S(2)}) copy-start(s32[16,256]{1,0:T(8,128)} %param.13) | copy-start | bytes 49156
  78.4 2.4 %copy-start.2 = (f32[16,256]{1,0:T(8,128)S(1)}, f32[16,256]{1,0:T(8,128)}, u32[]{:S(2)}) copy-start(f32[16,256]{1,0:T(8,128)} %param.12) | copy-start | bytes 49156
  83.3 19.6 %all-to-all-start.2 = ((bf16[128,2,5,256]{3,1,2,0:T(2,128)(2,1)}), bf16[128,2,5,256]{3,1,2,0:T(2,128)(2,1)S(1)}, u32[]{:S(2)}, u32[]{:S(2)}) async-start(bf16[128,2,5,256]{3,1,2,0:T(2,128)(2,1)} %copy_multiply_fusion), calls=%async_computation.2 | async-start | bytes 1310720 | tf_op jit(solution)/shard_map/all_to_all | solution.py:112
  88.4 18.2 %copy-start.3 = (s32[16]{0:T(128)S(1)}, s32[16]{0:T(128)}, u32[]{:S(2)}) copy-start(s32[16]{0:T(128)} %param.9) | copy-start | bytes 196
where the time goes:
time: 108 us; the launch traced here: 107 us
  waiting for transfers between devices  52.1 us (48%)
  local copies, waits for them, and re-layouts  23.5 us (22%)
  starting transfers between devices  21.1 us (20%)
  other arithmetic  5.62 us (5%)
  matrix products  4.24 us (4%)
    all_to_all x1, waiting for transfers between devices, on_device(): lax.all_to_all(outgoing.reshape(devices, capacity, field_count, tile_cell...  28.7 us
    all_to_all x1, waiting for transfers between devices, on_device(): lax.all_to_all(picked.reshape(devices, capacity, back_count, tile_cells),...  14.6 us
    all_to_all x1, starting transfers between devices, on_device(): lax.all_to_all(labels.reshape(devices, capacity), ('gx', 'gy'), split_axi...  11.5 us
    all_to_all x1, waiting for transfers between devices, on_device(): lax.all_to_all(labels.reshape(devices, capacity), ('gx', 'gy'), split_axi...  8.87 us
    all_to_all x1, starting transfers between devices, on_device(): lax.all_to_all(outgoing.reshape(devices, capacity, field_count, tile_cell...  5.26 us
    all_to_all x1, starting transfers between devices, on_device(): lax.all_to_all(picked.reshape(devices, capacity, back_count, tile_cells),...  4.35 us
    reshape x1, local copies, waits for them, and re-layouts, on_device(): outgoing.reshape(devices, capacity, field_count, tile_cells)  3.98 us
    reshape x1, local copies, waits for them, and re-layouts, on_device(): arrived = arrived.reshape(slot_count, field_count, tile_cells)  3.7 us
  transfers between devices with their start and end apart: 3, of which 3 were waited for; matrix products, arithmetic and copies ran while one was open for 3% of the time, Pallas kernels for 0%

commit v1 on v0

v1 whole, which is shorter than its diff:
```python
import jax
import jax.numpy as jnp
from jax import lax
from jax.experimental import pallas as pl
from jax.experimental.pallas import tpu as pltpu
from jax.sharding import PartitionSpec as P

PAIRS = 16
TILES = 16
FIELDS = 8
CELLS = 256
HALF = 128
SLOTS = 2
SENT = 7
BACK = 5
ROWS_DEST = 2 * SLOTS
BF = jnp.bfloat16
F32 = jnp.float32
VMEM_LIMIT = 24 * 1024 * 1024


def iota(shape, dim):
    return lax.broadcasted_iota(jnp.int32, shape, dim)


def halves_to_rows(plane):
    return jnp.concatenate([plane[:, :HALF], plane[:, HALF:]], axis=0)


def field_rows(scratch, f):
    parts = [scratch[h, pl.ds(f, PAIRS, stride=FIELDS), :] for h in range(2)]
    return jnp.concatenate(parts, axis=0)


def slot_column(target_row):
    row = target_row.astype(F32)
    later, other = iota((PAIRS, PAIRS), 0), iota((PAIRS, PAIRS), 1)
    column = jnp.sum(jnp.where(later == other, row, 0.0), axis=1, keepdims=True)
    earlier = jnp.where((column == row) & (other < later), 1.0, 0.0)
    return SLOTS * column + jnp.sum(earlier, axis=1, keepdims=True)


def contribute(src, target, sea, sky, weights, out, scratch):
    rows = out.shape[0]
    for p in range(PAIRS):
        term = jnp.dot(sky[src[p]], weights[p], preferred_element_type=F32)
        for h in range(2):
            scratch[h, p * FIELDS : (p + 1) * FIELDS, :] = term[:, h * HALF : (h + 1) * HALF]
    u, v, ta, qa, sw, lw, pr, ps = (field_rows(scratch, f) for f in range(FIELDS))
    sent = [x.astype(BF) for x in (u, v, ta, qa - 0.3 * ps, 0.5 * sw + 0.3 * lw, pr)]
    both = 2 * PAIRS
    mine = (iota((both, PAIRS), 0) % PAIRS) == iota((both, PAIRS), 1)
    tile = jnp.sum(jnp.where(mine, sea[...].astype(F32), 0.0), axis=1, keepdims=True)
    label = tile + (iota((both, 1), 0) // PAIRS * TILES + 1).astype(F32)
    rest = u - sent[0].astype(F32)
    sent.append(jnp.where(iota((both, HALF), 1) == 0, label, rest).astype(BF))
    slot = slot_column(target[...])
    pair = iota((PAIRS, both), 1) % PAIRS == iota((PAIRS, both), 0)
    place = 2.0 * jnp.sum(jnp.where(pair, slot, 0.0), axis=0, keepdims=True)
    place = place.astype(jnp.int32) + iota((1, both), 1) // PAIRS
    chosen = jnp.where(iota((rows, both), 0) == place, 1.0, 0.0).astype(BF)
    out[...] = jnp.dot(chosen, jnp.concatenate(sent, axis=1), preferred_element_type=F32).astype(BF)


def exchange(arrived, sst, marine, fluxes, out):
    rows = arrived.shape[0]
    both = 2 * TILES
    label = arrived[:, (SENT - 1) * HALF :].astype(F32)[:, :1].astype(jnp.int32)
    chosen = jnp.where(label == iota((rows, both), 1) + 1, 1.0, 0.0).astype(BF)
    total = lax.dot_general(
        chosen, arrived[...], (((0,), (0,)), ((), ())), preferred_element_type=F32
    )
    u, v, ta, q, rad, pr, rest = (total[:, f * HALF : (f + 1) * HALF] for f in range(SENT))
    u = u + jnp.where(iota((both, HALF), 1) == 0, 0.0, rest)
    sst_rows = halves_to_rows(sst[...])
    w = halves_to_rows(marine[...].astype(F32))
    square = u * u + v * v + 0.25
    speed = jnp.sqrt(square)
    dth = sst_rows - ta
    dq = 0.4 * sst_rows - q
    lift = 2.0 * (dth + 0.5 * dq)
    c = jnp.ones_like(speed)
    for _ in range(3):
        c = 1.0 + 0.5 * jnp.tanh(lift / (1.0 + c * speed * speed))
    k = c * speed
    found = (k * u * w, k * v * w, (rad - k * dth - k * dq) * w, (pr - 0.5 * k * dq) * w)
    for f, x in enumerate(found):
        fluxes[f, :, :HALF] = x[:TILES]
        fluxes[f, :, HALF:] = x[TILES:]
    back = jnp.concatenate([x.astype(BF) for x in found + (sst_rows * w,)], axis=1)
    out[...] = jnp.dot(chosen, back, preferred_element_type=F32).astype(BF)


def deliver(src, target, returned, weights, out, values, sums):
    rows = returned.shape[0]
    both = 2 * PAIRS
    slot = slot_column(target[...])
    place = jnp.concatenate([2.0 * slot, 2.0 * slot + 1.0], axis=0).astype(jnp.int32)
    chosen = jnp.where(iota((both, rows), 1) == place, 1.0, 0.0).astype(BF)
    picked = jnp.dot(chosen, returned[...], preferred_element_type=F32)
    values[...] = jnp.zeros_like(values)
    for f in range(BACK):
        for h in range(2):
            part = picked[h * PAIRS : (h + 1) * PAIRS, f * HALF : (f + 1) * HALF]
            values[h, pl.ds(f, PAIRS, stride=FIELDS), :] = part
    sums[...] = jnp.zeros_like(sums)
    for p in range(PAIRS):
        block = pl.ds(p * FIELDS, FIELDS)
        term = lax.dot_general(
            jnp.concatenate([values[h, block, :] for h in range(2)], axis=1).astype(BF),
            weights[p],
            (((1,), (1,)), ((), ())),
            preferred_element_type=F32,
        )
        at = pl.ds(pl.multiple_of(src[p] * FIELDS, FIELDS), FIELDS)
        for h in range(2):
            sums[h, at, :] += term[:, h * HALF : (h + 1) * HALF]
    for f in range(BACK):
        for h in range(2):
            out[f, :, h * HALF : (h + 1) * HALF] = sums[h, pl.ds(f, TILES, stride=FIELDS), :]


SMEM = pl.BlockSpec(memory_space=pltpu.SMEM)
VMEM = pl.BlockSpec(memory_space=pltpu.VMEM)


def on_device(sky, weights, sky_block, target_device, sea_block, sst, marine):
    devices = lax.axis_size(("gx", "gy"))
    rows = devices * ROWS_DEST
    params = pltpu.CompilerParams(vmem_limit_bytes=VMEM_LIMIT)
    target = target_device.reshape(1, PAIRS)
    sea = sea_block.reshape(1, PAIRS)

    def swap(x):
        width = x.shape[1]
        y = lax.all_to_all(
            x.reshape(devices, ROWS_DEST, width),
            ("gx", "gy"),
            split_axis=0,
            concat_axis=0,
            tiled=True,
        )
        return y.reshape(rows, width)

    outgoing = pl.pallas_call(
        contribute,
        out_shape=jax.ShapeDtypeStruct((rows, SENT * HALF), BF),
        in_specs=[SMEM] + [VMEM] * 4,
        out_specs=VMEM,
        scratch_shapes=[pltpu.VMEM((2, PAIRS * FIELDS, HALF), F32)],
        compiler_params=params,
    )(sky_block, target, sea, sky, weights)
    fluxes, back = pl.pallas_call(
        exchange,
        out_shape=(
            jax.ShapeDtypeStruct((4, TILES, CELLS), F32),
            jax.ShapeDtypeStruct((rows, BACK * HALF), BF),
        ),
        in_specs=[VMEM] * 3,
        out_specs=(VMEM, VMEM),
        compiler_params=params,
    )(swap(outgoing), sst, marine)
    atm_back = pl.pallas_call(
        deliver,
        out_shape=jax.ShapeDtypeStruct((BACK, TILES, CELLS), F32),
        in_specs=[SMEM] + [VMEM] * 3,
        out_specs=VMEM,
        scratch_shapes=[
            pltpu.VMEM((2, PAIRS * FIELDS, HALF), F32),
            pltpu.VMEM((2, TILES * FIELDS, HALF), F32),
        ],
        compiler_params=params,
    )(sky_block, target, swap(back), weights)
    return jnp.transpose(fluxes, (1, 0, 2)), jnp.transpose(atm_back, (1, 0, 2))


def solution(mesh):
    tiles = P(("gx", "gy"), None, None)
    cells = P(("gx", "gy"), None)
    flat = P(("gx", "gy"))
    return jax.shard_map(
        on_device,
        mesh=mesh,
        in_specs=(tiles, tiles, flat, cells, flat, cells, cells),
        out_specs=(tiles, tiles),
        check_vma=False,
    )
```

time: 108 us -> 60.3 us (0.56)
  waiting for transfers between devices: 52.1 us -> 14.5 us
  blocking collectives: 0 us -> 29.2 us
  local copies, waits for them, and re-layouts: 23.5 us -> 6.66 us
  starting transfers between devices: 21.1 us -> 4.38 us
  other arithmetic: 5.62 us -> 0 us
  Pallas kernels: 0 us -> 4.41 us
  matrix products: 4.24 us -> 0 us
    all_to_all x3 -> x1, waiting for transfers between devices: 52.1 us -> 14.5 us  [swap(): lax.all_to_all(x.reshape(devices, ROWS_DEST, width), ('gx', 'gy'), split_...]
    all_to_all x0 -> x1, blocking collectives: none -> 29.2 us  [swap(): lax.all_to_all(x.reshape(devices, ROWS_DEST, width), ('gx', 'gy'), split_...]
    all_to_all x3 -> x1, starting transfers between devices: 21.1 us -> 4.38 us  [swap(): lax.all_to_all(x.reshape(devices, ROWS_DEST, width), ('gx', 'gy'), split_...]
    all_to_all x5 -> x0, local copies, waits for them, and re-layouts: 6.19 us -> none  [the longest x1 3.66 us: on_device(): lax.all_to_all(outgoing.reshape(devices, capacity, field_count, tile_cell...]
    reshape x2 -> x4, local copies, waits for them, and re-layouts: 7.67 us -> 1.56 us  [the longest x2 1.2 us: swap(): x.reshape(devices, ROWS_DEST, width)]
    pallas_call x0 -> x3, Pallas kernels: none -> 4.41 us  [the longest x1 2.24 us: on_device(): pl.pallas_call(deliver, out_shape=jax.ShapeDtypeStruct((BACK, TILES, CELL...]
    unnamed x9 -> x21, local copies, waits for them, and re-layouts: 0.69 us -> 5.1 us
    dot_general x4 -> x0, matrix products: 4.24 us -> none  [the longest x1 2.38 us: on_device(): jnp.einsum('sq,sft->qft', select, arrived, precision=lax.Precision.HIGHEST)]
  transfers between devices with their start and end apart: 3 -> 1, of which waited for: 3 -> 1; matrix products, arithmetic and copies ran while one was open for 3% -> 1% of each run, Pallas kernels for 0% -> 0%
where the time goes in v1:
time: 60.3 us; the launch traced here: 60 us
  blocking collectives  29.2 us (48%)
  waiting for transfers between devices  14.5 us (24%)
  local copies, waits for them, and re-layouts  6.66 us (11%)
  Pallas kernels  4.41 us (7%)
  starting transfers between devices  4.38 us (7%)
  between operations  0.76 us (1%)
    all_to_all x1, blocking collectives, swap(): lax.all_to_all(x.reshape(devices, ROWS_DEST, width), ('gx', 'gy'), split_...  29.2 us
    all_to_all x1, waiting for transfers between devices, swap(): lax.all_to_all(x.reshape(devices, ROWS_DEST, width), ('gx', 'gy'), split_...  14.5 us
    unnamed x21, local copies, waits for them, and re-layouts  5.1 us
    all_to_all x1, starting transfers between devices, swap(): lax.all_to_all(x.reshape(devices, ROWS_DEST, width), ('gx', 'gy'), split_...  4.38 us
    pallas_call x1, Pallas kernels, on_device(): pl.pallas_call(deliver, out_shape=jax.ShapeDtypeStruct((BACK, TILES, CELL...  2.24 us
    pallas_call x1, Pallas kernels, on_device(): pl.pallas_call(contribute, out_shape=jax.ShapeDtypeStruct((rows, SENT * H...  1.37 us
  transfers between devices with their start and end apart: 1, of which 1 were waited for; matrix products, arithmetic and copies ran while one was open for 1% of the time, Pallas kernels for 0%

profile of v1, /device:TPU:1, one launch (start us, length us, event | category | flops | bytes accessed | tf_op | source)
XLA Modules:
  0.0 60.0 jit_solution(13701613732390646895)
XLA Ops:
  0.6 0.0 copy-start
  0.6 1.6 %copy-done = bf16[16,256,256]{2,1,0:T(8,128)(2,1)S(1)} copy-done((bf16[16,256,256]{2,1,0:T(8,128)(2,1)S(1)}, bf16[16,256,256]{2,1,0:T(8,128)(2,1)}, u32[]{:S(2)}) %copy-start) | copy-done | bytes 2097176
  2.2 0.8 %copy-done.2 = bf16[16,8,256]{2,1,0:T(8,128)(2,1)S(1)} copy-done((bf16[16,8,256]{2,1,0:T(8,128)(2,1)S(1)}, bf16[16,8,256]{2,1,0:T(8,128)(2,1)}, u32[]{:S(2)}) %copy-start.2) | copy-done | bytes 65560
  3.1 0.7 %copy-done.5 = s32[16]{0:T(128)S(1)} copy-done((s32[16]{0:T(128)S(1)}, s32[16]{0:T(128)}, u32[]{:S(2)}) %copy-start.5) | copy-done | bytes 88
  3.7 0.7 %copy-done.7 = s32[16,1]{0,1:T(1,128)S(1)} copy-done((s32[16,1]{0,1:T(1,128)S(1)}, s32[16,1]{0,1:T(1,128)}, u32[]{:S(2)}) %copy-start.7) | copy-done | bytes 88
  4.4 0.7 %copy-done.9 = s32[16]{0:T(128)S(1)} copy-done((s32[16]{0:T(128)S(1)}, s32[16]{0:T(128)}, u32[]{:S(2)}) %copy-start.9) | copy-done | bytes 88
  5.0 1.4 %shard_map.86 = bf16[512,896]{1,0:T(8,128)(2,1)S(1)} custom-call(s32[16]{0:T(128)S(1)} %copy-done.5, s32[1,16]{1,0:T(1,128)S(1)} %bitcast.5, s32[1,16]{1,0:T(1,128)S(1)} %bitcast.7, bf16[16,8,256]{2,1,0:T(8,128)(2,1)S(1)} %copy-done.2, bf16[16,256,256]{2,1,0:T(8,128)(2,1)S(1)} %copy-done), custom_call_target="tpu_custom_call" | custom-call | tf_op jit(solution)/shard_map/pallas_call | solution.py:145
  6.4 0.2 reshape.24
  6.6 0.0 copy-start.3
  6.6 0.0 copy-start.4
  6.6 29.2 %all_to_all.10 = bf16[128,4,896]{2,1,0:T(4,128)(2,1)S(1)} all-to-all(bf16[128,4,896]{2,1,0:T(4,128)(2,1)S(1)} %reshape.24), channel_id=1, replica_groups=mesh['gx'=16,'gy'=8] {'gx','gy'}, dimensions={0} | all-to-all | bytes 1835008 | tf_op jit(solution)/shard_map/all_to_all | solution.py:136
  35.9 0.2 reshape.25.arrived
  36.1 0.0 copy-done.3
  36.1 0.0 copy-done.4
  36.1 0.8 %shard_map.87 = (f32[4,16,256]{2,1,0:T(8,128)S(1)}, bf16[512,640]{1,0:T(8,128)(2,1)S(1)}) custom-call(bf16[512,896]{1,0:T(8,128)(2,1)S(1)} %reshape.25.arrived, f32[16,256]{1,0:T(8,128)S(1)} %copy-done.3, s32[16,256]{1,0:T(8,128)S(1)} %copy-done.4), custom_call_target="tpu_custom_call" | custom-call | tf_op jit(solution)/shard_map/pallas_call | solution.py:153
  36.9 0.0 copy-start.1
  36.9 0.0 copy-start.6
  37.0 0.0 copy-start.8
  37.0 1.0 %reshape.26 = bf16[128,4,640]{2,1,0:T(4,128)(2,1)} reshape(bf16[512,640]{1,0:T(8,128)(2,1)S(1)} %get-tuple-element.5) | data formatting | bytes 1310720 | tf_op jit(solution)/shard_map/reshape | solution.py:137
  38.0 4.4 %all-to-all-start.1 = ((bf16[128,4,640]{2,1,0:T(4,128)(2,1)}), bf16[128,4,640]{2,1,0:T(4,128)(2,1)S(1)}, u32[]{:S(2)}, u32[]{:S(2)}) async-start(bf16[128,4,640]{2,1,0:T(4,128)(2,1)} %reshape.26), calls=%async_computation.1 | async-start | bytes 1310720 | tf_op jit(solution)/shard_map/all_to_all | solution.py:136
  42.4 0.7 %copy.9 = f32[16,4,256]{2,1,0:T(4,128)} copy(f32[16,4,256]{2,0,1:T(8,128)S(1)} %bitcast.4) | data formatting | bytes 131072
  43.0 14.5 %all-to-all-done.1 = bf16[128,4,640]{2,1,0:T(4,128)(2,1)S(1)} async-done(((bf16[128,4,640]{2,1,0:T(4,128)(2,1)}), bf16[128,4,640]{2,1,0:T(4,128)(2,1)S(1)}, u32[]{:S(2)}, u32[]{:S(2)}) %all-to-all-start.1) | async-done | bytes 655392 | tf_op jit(solution)/shard_map/all_to_all | solution.py:136
  57.5 0.1 reshape.27.returned
  57.7 2.2 %shard_map.88 = f32[5,16,256]{2,1,0:T(8,128)} custom-call(s32[16]{0:T(128)S(1)} %copy-done.6, s32[1,16]{1,0:T(1,128)S(1)} %bitcast.6, bf16[512,640]{1,0:T(8,128)(2,1)S(1)} %reshape.27.returned, bf16[16,256,256]{2,1,0:T(8,128)(2,1)S(1)} %copy-done.1), custom_call_target="tpu_custom_call" | custom-call | tf_op jit(solution)/shard_map/pallas_call | solution.py:163
  (7 shorter events, 0.0 us)
Async XLA Ops:
  0.6 1.6 %copy-start = (bf16[16,256,256]{2,1,0:T(8,128)(2,1)S(1)}, bf16[16,256,256]{2,1,0:T(8,128)(2,1)}, u32[]{:S(2)}) copy-start(bf16[16,256,256]{2,1,0:T(8,128)(2,1)} %weights.3) | copy-start | bytes 6291460
  2.2 0.8 %copy-start.2 = (bf16[16,8,256]{2,1,0:T(8,128)(2,1)S(1)}, bf16[16,8,256]{2,1,0:T(8,128)(2,1)}, u32[]{:S(2)}) copy-start(bf16[16,8,256]{2,1,0:T(8,128)(2,1)} %sky.1) | copy-start | bytes 196612
  3.1 0.7 %copy-start.5 = (s32[16]{0:T(128)S(1)}, s32[16]{0:T(128)}, u32[]{:S(2)}) copy-start(s32[16]{0:T(128)} %src.3) | copy-start | bytes 196
  3.7 0.7 %copy-start.7 = (s32[16,1]{0,1:T(1,128)S(1)}, s32[16,1]{0,1:T(1,128)}, u32[]{:S(2)}) copy-start(s32[16,1]{0,1:T(1,128)} %param.10) | copy-start | bytes 196
  4.4 0.7 %copy-start.9 = (s32[16]{0:T(128)S(1)}, s32[16]{0:T(128)}, u32[]{:S(2)}) copy-start(s32[16]{0:T(128)} %param.11) | copy-start | bytes 196
  6.6 29.5 %copy-start.3 = (f32[16,256]{1,0:T(8,128)S(1)}, f32[16,256]{1,0:T(8,128)}, u32[]{:S(2)}) copy-start(f32[16,256]{1,0:T(8,128)} %sst.1) | copy-start | bytes 49156
  6.6 29.5 %copy-start.4 = (s32[16,256]{1,0:T(8,128)S(1)}, s32[16,256]{1,0:T(8,128)}, u32[]{:S(2)}) copy-start(s32[16,256]{1,0:T(8,128)} %marine.1) | copy-start | bytes 49156
  36.9 20.8 %copy-start.1 = (bf16[16,256,256]{2,1,0:T(8,128)(2,1)S(1)}, bf16[16,256,256]{2,1,0:T(8,128)(2,1)}, u32[]{:S(2)}) copy-start(bf16[16,256,256]{2,1,0:T(8,128)(2,1)} %weights.3) | copy-start | bytes 6291460
  36.9 20.8 %copy-start.6 = (s32[16]{0:T(128)S(1)}, s32[16]{0:T(128)}, u32[]{:S(2)}) copy-start(s32[16]{0:T(128)} %src.3) | copy-start | bytes 196
  37.0 20.8 %copy-start.8 = (s32[16,1]{0,1:T(1,128)S(1)}, s32[16,1]{0,1:T(1,128)}, u32[]{:S(2)}) copy-start(s32[16,1]{0,1:T(1,128)} %param.10) | copy-start | bytes 196
  38.0 19.6 %all-to-all-start.1 = ((bf16[128,4,640]{2,1,0:T(4,128)(2,1)}), bf16[128,4,640]{2,1,0:T(4,128)(2,1)S(1)}, u32[]{:S(2)}, u32[]{:S(2)}) async-start(bf16[128,4,640]{2,1,0:T(4,128)(2,1)} %reshape.26), calls=%async_computation.1 | async-start | bytes 1310720 | tf_op jit(solution)/shard_map/all_to_all | solution.py:136

commit v2 on v1

--- a/solution.py
+++ b/solution.py
@@ -13,7 +13,9 @@
 SLOTS = 2
 SENT = 7
 BACK = 5
-ROWS_DEST = 2 * SLOTS
+CORES = 2
+CHIP_ROWS = CORES * 2 * TILES
+GROUP = 4
 BF = jnp.bfloat16
 F32 = jnp.float32
 VMEM_LIMIT = 24 * 1024 * 1024
@@ -40,9 +42,26 @@
     return SLOTS * column + jnp.sum(earlier, axis=1, keepdims=True)
 
 
-def contribute(src, target, sea, sky, weights, out, scratch):
+def contribute(
+    src_hbm, target_hbm, sea_hbm, sky_hbm, weights_hbm, out,
+    src, target, sea, sky, weights, scratch, sems,
+):
     rows = out.shape[0]
+    small = ((src_hbm, src), (sky_hbm, sky), (target_hbm, target), (sea_hbm, sea))
+    copies = [pltpu.make_async_copy(a, b, sems.at[i]) for i, (a, b) in enumerate(small)]
+    for i in range(PAIRS // GROUP):
+        part = pl.ds(i * GROUP, GROUP)
+        copies.append(
+            pltpu.make_async_copy(weights_hbm.at[part], weights.at[part], sems.at[len(small) + i])
+        )
+    for copy in copies:
+        copy.start()
+    for copy in copies[: len(small)]:
+        copy.wait()
+    core = lax.axis_index("gy") % CORES
     for p in range(PAIRS):
+        if p % GROUP == 0:
+            copies[len(small) + p // GROUP].wait()
         term = jnp.dot(sky[src[p]], weights[p], preferred_element_type=F32)
         for h in range(2):
             scratch[h, p * FIELDS : (p + 1) * FIELDS, :] = term[:, h * HALF : (h + 1) * HALF]
@@ -51,7 +70,9 @@
     both = 2 * PAIRS
     mine = (iota((both, PAIRS), 0) % PAIRS) == iota((both, PAIRS), 1)
     tile = jnp.sum(jnp.where(mine, sea[...].astype(F32), 0.0), axis=1, keepdims=True)
-    label = tile + (iota((both, 1), 0) // PAIRS * TILES + 1).astype(F32)
+    owner = jnp.sum(jnp.where(mine, target[...].astype(F32), 0.0), axis=1, keepdims=True)
+    other = (owner.astype(jnp.int32) + core) % CORES * (2 * TILES)
+    label = tile + (other + iota((both, 1), 0) // PAIRS * TILES + 1).astype(F32)
     rest = u - sent[0].astype(F32)
     sent.append(jnp.where(iota((both, HALF), 1) == 0, label, rest).astype(BF))
     slot = slot_column(target[...])
@@ -62,18 +83,26 @@
     out[...] = jnp.dot(chosen, jnp.concatenate(sent, axis=1), preferred_element_type=F32).astype(BF)
 
 
-def exchange(arrived, sst, marine, fluxes, out):
+def combine(arrived, partial, chosen):
     rows = arrived.shape[0]
+    label = arrived[:, (SENT - 1) * HALF :].astype(F32)[:, :1].astype(jnp.int32)
+    chosen[...] = jnp.where(label == iota((rows, CHIP_ROWS), 1) + 1, 1.0, 0.0).astype(BF)
+    total = lax.dot_general(
+        chosen[...], arrived[...], (((0,), (0,)), ((), ())), preferred_element_type=F32
+    )
+    partial[...] = total[:, : (SENT - 1) * HALF]
+    rest = total[:, (SENT - 1) * HALF :]
+    partial[:, :HALF] += jnp.where(iota((CHIP_ROWS, HALF), 1) == 0, 0.0, rest)
+
+
+def exchange(own, swapped, chosen, sst, sst_other, marine, marine_other, fluxes, out):
     both = 2 * TILES
-    label = arrived[:, (SENT - 1) * HALF :].astype(F32)[:, :1].astype(jnp.int32)
-    chosen = jnp.where(label == iota((rows, both), 1) + 1, 1.0, 0.0).astype(BF)
-    total = lax.dot_general(
-        chosen, arrived[...], (((0,), (0,)), ((), ())), preferred_element_type=F32
+    total = own[...] + jnp.concatenate([swapped[both:], swapped[:both]], axis=0)
+    u, v, ta, q, rad, pr = (total[:, f * HALF : (f + 1) * HALF] for f in range(SENT - 1))
+    sst_rows = jnp.concatenate([halves_to_rows(x[...]) for x in (sst, sst_other)], axis=0)
+    w = jnp.concatenate(
+        [halves_to_rows(x[...].astype(F32)) for x in (marine, marine_other)], axis=0
     )
-    u, v, ta, q, rad, pr, rest = (total[:, f * HALF : (f + 1) * HALF] for f in range(SENT))
-    u = u + jnp.where(iota((both, HALF), 1) == 0, 0.0, rest)
-    sst_rows = halves_to_rows(sst[...])
-    w = halves_to_rows(marine[...].astype(F32))
     square = u * u + v * v + 0.25
     speed = jnp.sqrt(square)
     dth = sst_rows - ta
@@ -86,9 +115,9 @@
     found = (k * u * w, k * v * w, (rad - k * dth - k * dq) * w, (pr - 0.5 * k * dq) * w)
     for f, x in enumerate(found):
         fluxes[f, :, :HALF] = x[:TILES]
-        fluxes[f, :, HALF:] = x[TILES:]
+        fluxes[f, :, HALF:] = x[TILES:both]
     back = jnp.concatenate([x.astype(BF) for x in found + (sst_rows * w,)], axis=1)
-    out[...] = jnp.dot(chosen, back, preferred_element_type=F32).astype(BF)
+    out[...] = jnp.dot(chosen[...], back, preferred_element_type=F32).astype(BF)
 
 
 def deliver(src, target, returned, weights, out, values, sums):
@@ -122,44 +151,70 @@
 
 SMEM = pl.BlockSpec(memory_space=pltpu.SMEM)
 VMEM = pl.BlockSpec(memory_space=pltpu.VMEM)
+HBM = pl.BlockSpec(memory_space=pltpu.HBM)
 
 
 def on_device(sky, weights, sky_block, target_device, sea_block, sst, marine):
     devices = lax.axis_size(("gx", "gy"))
-    rows = devices * ROWS_DEST
+    chips = devices // CORES
+    rows = devices * SLOTS * 2
     params = pltpu.CompilerParams(vmem_limit_bytes=VMEM_LIMIT)
     target = target_device.reshape(1, PAIRS)
     sea = sea_block.reshape(1, PAIRS)
+    same_core = [list(range(core, devices, CORES)) for core in range(CORES)]
 
     def swap(x):
         width = x.shape[1]
         y = lax.all_to_all(
-            x.reshape(devices, ROWS_DEST, width),
+            x.reshape(chips, rows // chips, width),
             ("gx", "gy"),
             split_axis=0,
             concat_axis=0,
+            axis_index_groups=same_core,
             tiled=True,
         )
         return y.reshape(rows, width)
 
+    def other_core(x):
+        return lax.ppermute(x, ("gx", "gy"), [(d, d ^ 1) for d in range(devices)])
+
     outgoing = pl.pallas_call(
         contribute,
         out_shape=jax.ShapeDtypeStruct((rows, SENT * HALF), BF),
-        in_specs=[SMEM] + [VMEM] * 4,
+        in_specs=[HBM] * 5,
         out_specs=VMEM,
-        scratch_shapes=[pltpu.VMEM((2, PAIRS * FIELDS, HALF), F32)],
+        scratch_shapes=[
+            pltpu.SMEM((PAIRS,), jnp.int32),
+            pltpu.VMEM((1, PAIRS), jnp.int32),
+            pltpu.VMEM((1, PAIRS), jnp.int32),
+            pltpu.VMEM((TILES, FIELDS, CELLS), BF),
+            pltpu.VMEM((PAIRS, CELLS, CELLS), BF),
+            pltpu.VMEM((2, PAIRS * FIELDS, HALF), F32),
+            pltpu.SemaphoreType.DMA((4 + PAIRS // GROUP,)),
+        ],
         compiler_params=params,
     )(sky_block, target, sea, sky, weights)
+    sst_other, marine_other = other_core(sst), other_core(marine)
+    partial, chosen = pl.pallas_call(
+        combine,
+        out_shape=(
+            jax.ShapeDtypeStruct((CHIP_ROWS, (SENT - 1) * HALF), F32),
+            jax.ShapeDtypeStruct((rows, CHIP_ROWS), BF),
+        ),
+        in_specs=[VMEM],
+        out_specs=(VMEM, VMEM),
+        compiler_params=params,
+    )(swap(outgoing))
     fluxes, back = pl.pallas_call(
         exchange,
         out_shape=(
             jax.ShapeDtypeStruct((4, TILES, CELLS), F32),
             jax.ShapeDtypeStruct((rows, BACK * HALF), BF),
         ),
-        in_specs=[VMEM] * 3,
+        in_specs=[VMEM] * 7,
         out_specs=(VMEM, VMEM),
         compiler_params=params,
-    )(swap(outgoing), sst, marine)
+    )(partial, other_core(partial), chosen, sst, sst_other, marine, marine_other)
     atm_back = pl.pallas_call(
         deliver,
         out_shape=jax.ShapeDtypeStruct((BACK, TILES, CELLS), F32),

time: 60.3 us -> 61.9 us (1.027)
  starting transfers between devices: 4.38 us -> 7.44 us
  local copies, waits for them, and re-layouts: 6.66 us -> 5.1 us
  Pallas kernels: 4.41 us -> 5.71 us
  blocking collectives: 29.2 us -> 28.1 us
    ppermute x0 -> x3, starting transfers between devices: none -> 2.8 us  [other_core(): return lax.ppermute(x, ('gx', 'gy'), [(d, d ^ 1) for d in range(devices)])]
    reshape x4 -> x0, local copies, waits for them, and re-layouts: 1.56 us -> none  [the longest x2 1.2 us: swap(): x.reshape(devices, ROWS_DEST, width)]
    all_to_all x1, waiting for transfers between devices: 14.5 us -> 13.4 us  [swap(): lax.all_to_all(x.reshape(chips, rows // chips, width), ('gx', 'gy'), spli...]
    all_to_all x1, blocking collectives: 29.2 us -> 28.1 us  [swap(): lax.all_to_all(x.reshape(chips, rows // chips, width), ('gx', 'gy'), spli...]
    ppermute x0 -> x3, waiting for transfers between devices: none -> 0.84 us  [other_core(): return lax.ppermute(x, ('gx', 'gy'), [(d, d ^ 1) for d in range(devices)])]
  transfers between devices with their start and end apart: 1 -> 4, of which waited for: 1 -> 3; matrix products, arithmetic and copies ran while one was open for 1% -> 1% of each run, Pallas kernels for 0% -> 0%
where the time goes in v2:
time: 61.9 us; the launch traced here: 61.3 us
  blocking collectives  28.1 us (45%)
  waiting for transfers between devices  14.2 us (23%)
  starting transfers between devices  7.44 us (12%)
  Pallas kernels  5.71 us (9%)
  local copies, waits for them, and re-layouts  5.1 us (8%)
  between operations  0.72 us (1%)
    all_to_all x1, blocking collectives, swap(): lax.all_to_all(x.reshape(chips, rows // chips, width), ('gx', 'gy'), spli...  28.1 us
    all_to_all x1, waiting for transfers between devices, swap(): lax.all_to_all(x.reshape(chips, rows // chips, width), ('gx', 'gy'), spli...  13.4 us
    unnamed x21, local copies, waits for them, and re-layouts  5.1 us
    all_to_all x1, starting transfers between devices, swap(): lax.all_to_all(x.reshape(chips, rows // chips, width), ('gx', 'gy'), spli...  4.64 us
    ppermute x3, starting transfers between devices, other_core(): return lax.ppermute(x, ('gx', 'gy'), [(d, d ^ 1) for d in range(devices)])  2.8 us
    pallas_call x1, Pallas kernels, on_device(): pl.pallas_call(deliver, out_shape=jax.ShapeDtypeStruct((BACK, TILES, CELL...  2.24 us
    pallas_call x1, Pallas kernels, on_device(): pl.pallas_call(contribute, out_shape=jax.ShapeDtypeStruct((rows, SENT * H...  1.81 us
  transfers between devices with their start and end apart: 4, of which 3 were waited for; matrix products, arithmetic and copies ran while one was open for 1% of the time, Pallas kernels for 0%

profile of v2, /device:TPU:1, one launch (start us, length us, event | category | flops | bytes accessed | tf_op | source)
XLA Modules:
  0.0 61.3 jit_solution(12074044736669886773)
XLA Ops:
  0.6 0.0 copy-start
  0.6 1.6 %copy-done = bf16[16,256,256]{2,1,0:T(8,128)(2,1)S(1)} copy-done((bf16[16,256,256]{2,1,0:T(8,128)(2,1)S(1)}, bf16[16,256,256]{2,1,0:T(8,128)(2,1)}, u32[]{:S(2)}) %copy-start) | copy-done | bytes 2097176
  2.2 0.8 %copy-done.2 = bf16[16,8,256]{2,1,0:T(8,128)(2,1)S(1)} copy-done((bf16[16,8,256]{2,1,0:T(8,128)(2,1)S(1)}, bf16[16,8,256]{2,1,0:T(8,128)(2,1)}, u32[]{:S(2)}) %copy-start.2) | copy-done | bytes 65560
  3.1 0.7 %copy-done.5 = s32[16]{0:T(128)S(1)} copy-done((s32[16]{0:T(128)S(1)}, s32[16]{0:T(128)}, u32[]{:S(2)}) %copy-start.5) | copy-done | bytes 88
  3.7 0.7 %copy-done.7 = s32[16,1]{0,1:T(1,128)S(1)} copy-done((s32[16,1]{0,1:T(1,128)S(1)}, s32[16,1]{0,1:T(1,128)}, u32[]{:S(2)}) %copy-start.7) | copy-done | bytes 88
  4.4 0.7 %copy-done.9 = s32[16]{0:T(128)S(1)} copy-done((s32[16]{0:T(128)S(1)}, s32[16]{0:T(128)}, u32[]{:S(2)}) %copy-start.9) | copy-done | bytes 88
  5.0 1.8 %shard_map.86 = bf16[512,896]{1,0:T(8,128)(2,1)S(1)} custom-call(s32[16]{0:T(128)S(1)} %copy-done.5, s32[1,16]{1,0:T(1,128)S(1)} %bitcast.12, s32[1,16]{1,0:T(1,128)S(1)} %bitcast.14, bf16[16,8,256]{2,1,0:T(8,128)(2,1)S(1)} %copy-done.2, bf16[16,256,256]{2,1,0:T(8,128)(2,1)S(1)} %copy-done), custom_call_target="tpu_custom_call" | custom-call | tf_op jit(solution)/shard_map/pallas_call | solution.py:181
  6.9 0.0 copy-start.3
  6.9 0.0 copy-start.4
  6.9 0.0 copy-start.1
  6.9 0.0 copy-start.6
  6.9 0.0 copy-start.8
  6.9 28.1 %all_to_all.10 = bf16[64,8,896]{2,1,0:T(8,128)(2,1)S(1)} all-to-all(bf16[64,8,896]{2,1,0:T(8,128)(2,1)S(1)} %bitcast.9), channel_id=1, replica_groups={{0,2,4,6,8,10,12,14,16,18,20,22,24,26,28,30,32,34,36,38,40,42,44,46,48,..., dimensions={0} | all-to-all | bytes 1835008 | tf_op jit(solution)/shard_map/all_to_all | solution.py:168
  35.1 0.4 shard_map.87
  35.5 2.3 %collective-permute-start = (f32[64,768]{1,0:T(8,128)S(1)}, f32[64,768]{1,0:T(8,128)S(1)}, u32[]{:S(2)}, u32[]{:S(2)}) collective-permute-start(f32[64,768]{1,0:T(8,128)S(1)} %get-tuple-element.6.own), channel_id=1, source_target_pairs={{0,1},{1,0},{2,3},{3,2},{4,5},{5,4},{6,7},{7,6},{8,9},{9,8},{10,11... | collective-permute-start | bytes 589832 | tf_op jit(solution)/shard_map/ppermute | solution.py:179
  37.8 0.1 collective-permute-start.1
  37.9 0.4 collective-permute-start.2
  38.3 0.7 %collective-permute-done.1.sst_other = f32[16,256]{1,0:T(8,128)S(1)} collective-permute-done((f32[16,256]{1,0:T(8,128)S(1)}, f32[16,256]{1,0:T(8,128)S(1)}, u32[]{:S(2)}, u32[]{:S(2)}) %collective-permute-start.1) | collective-permute-done | bytes 16416 | tf_op jit(solution)/shard_map/ppermute | solution.py:179
  39.0 0.2 collective-permute-done.2.marine_other
  39.1 1.2 %shard_map.88 = (f32[4,16,256]{2,1,0:T(8,128)S(1)}, bf16[512,640]{1,0:T(8,128)(2,1)}) custom-call(f32[64,768]{1,0:T(8,128)S(1)} %get-tuple-element.6.own, f32[64,768]{1,0:T(8,128)S(1)} %collective-permute-done.swapped, bf16[512,64]{1,0:T(8,128)(2,1)S(1)} %get-tuple-element.7.chosen, f32[16,256]{1,0:T(8,128)S(1)} %copy-done.3, ...), custom_call_target="tpu_custom_call" | custom-call | tf_op jit(solution)/shard_map/pallas_call | solution.py:208
  40.4 4.6 %all-to-all-start.1 = ((bf16[64,8,640]{2,1,0:T(8,128)(2,1)}), bf16[64,8,640]{2,1,0:T(8,128)(2,1)S(1)}, u32[]{:S(2)}, u32[]{:S(2)}) async-start(bf16[64,8,640]{2,1,0:T(8,128)(2,1)} %bitcast.5), calls=%async_computation.1 | async-start | bytes 1310720 | tf_op jit(solution)/shard_map/all_to_all | solution.py:168
  45.0 0.7 %copy.9 = f32[16,4,256]{2,1,0:T(4,128)} copy(f32[16,4,256]{2,0,1:T(8,128)S(1)} %bitcast.11) | data formatting | bytes 131072
  45.7 13.4 %all-to-all-done.1 = bf16[64,8,640]{2,1,0:T(8,128)(2,1)S(1)} async-done(((bf16[64,8,640]{2,1,0:T(8,128)(2,1)}), bf16[64,8,640]{2,1,0:T(8,128)(2,1)S(1)}, u32[]{:S(2)}, u32[]{:S(2)}) %all-to-all-start.1) | async-done | bytes 655392 | tf_op jit(solution)/shard_map/all_to_all | solution.py:168
  59.1 2.2 %shard_map.89 = f32[5,16,256]{2,1,0:T(8,128)} custom-call(s32[16]{0:T(128)S(1)} %copy-done.6, s32[1,16]{1,0:T(1,128)S(1)} %bitcast.13, bf16[512,640]{1,0:T(8,128)(2,1)S(1)} %bitcast.10, bf16[16,256,256]{2,1,0:T(8,128)(2,1)S(1)} %copy-done.1), custom_call_target="tpu_custom_call" | custom-call | tf_op jit(solution)/shard_map/pallas_call | solution.py:218
  (10 shorter events, 0.0 us)
Async XLA Ops:
  0.6 1.6 %copy-start = (bf16[16,256,256]{2,1,0:T(8,128)(2,1)S(1)}, bf16[16,256,256]{2,1,0:T(8,128)(2,1)}, u32[]{:S(2)}) copy-start(bf16[16,256,256]{2,1,0:T(8,128)(2,1)} %weights.1) | copy-start | bytes 6291460
  2.2 0.8 %copy-start.2 = (bf16[16,8,256]{2,1,0:T(8,128)(2,1)S(1)}, bf16[16,8,256]{2,1,0:T(8,128)(2,1)}, u32[]{:S(2)}) copy-start(bf16[16,8,256]{2,1,0:T(8,128)(2,1)} %sky_hbm.1) | copy-start | bytes 196612
  3.1 0.7 %copy-start.5 = (s32[16]{0:T(128)S(1)}, s32[16]{0:T(128)}, u32[]{:S(2)}) copy-start(s32[16]{0:T(128)} %src.1) | copy-start | bytes 196
  3.7 0.7 %copy-start.7 = (s32[16,1]{0,1:T(1,128)S(1)}, s32[16,1]{0,1:T(1,128)}, u32[]{:S(2)}) copy-start(s32[16,1]{0,1:T(1,128)} %param.10) | copy-start | bytes 196
  4.4 0.7 %copy-start.9 = (s32[16]{0:T(128)S(1)}, s32[16]{0:T(128)}, u32[]{:S(2)}) copy-start(s32[16]{0:T(128)} %param.11) | copy-start | bytes 196
  6.9 30.9 %copy-start.3 = (f32[16,256]{1,0:T(8,128)S(1)}, f32[16,256]{1,0:T(8,128)}, u32[]{:S(2)}) copy-start(f32[16,256]{1,0:T(8,128)} %sst.1) | copy-start | bytes 49156
  6.9 31.0 %copy-start.4 = (s32[16,256]{1,0:T(8,128)S(1)}, s32[16,256]{1,0:T(8,128)}, u32[]{:S(2)}) copy-start(s32[16,256]{1,0:T(8,128)} %marine.1) | copy-start | bytes 49156
  6.9 52.2 %copy-start.1 = (bf16[16,256,256]{2,1,0:T(8,128)(2,1)S(1)}, bf16[16,256,256]{2,1,0:T(8,128)(2,1)}, u32[]{:S(2)}) copy-start(bf16[16,256,256]{2,1,0:T(8,128)(2,1)} %weights.1) | copy-start | bytes 6291460
  6.9 52.2 %copy-start.6 = (s32[16]{0:T(128)S(1)}, s32[16]{0:T(128)}, u32[]{:S(2)}) copy-start(s32[16]{0:T(128)} %src.1) | copy-start | bytes 196
  6.9 52.2 %copy-start.8 = (s32[16,1]{0,1:T(1,128)S(1)}, s32[16,1]{0,1:T(1,128)}, u32[]{:S(2)}) copy-start(s32[16,1]{0,1:T(1,128)} %param.10) | copy-start | bytes 196
  35.5 3.6 %collective-permute-start = (f32[64,768]{1,0:T(8,128)S(1)}, f32[64,768]{1,0:T(8,128)S(1)}, u32[]{:S(2)}, u32[]{:S(2)}) collective-permute-start(f32[64,768]{1,0:T(8,128)S(1)} %get-tuple-element.6.own), channel_id=1, source_target_pairs={{0,1},{1,0},{2,3},{3,2},{4,5},{5,4},{6,7},{7,6},{8,9},{9,8},{10,11... | collective-permute-start | bytes 589832 | tf_op jit(solution)/shard_map/ppermute | solution.py:179
  37.8 1.2 %collective-permute-start.1 = (f32[16,256]{1,0:T(8,128)S(1)}, f32[16,256]{1,0:T(8,128)S(1)}, u32[]{:S(2)}, u32[]{:S(2)}) collective-permute-start(f32[16,256]{1,0:T(8,128)S(1)} %copy-done.3), channel_id=1, source_target_pairs={{0,1},{1,0},{2,3},{3,2},{4,5},{5,4},{6,7},{7,6},{8,9},{9,8},{10,11... | collective-permute-start | bytes 49160 | tf_op jit(solution)/shard_map/ppermute | solution.py:179
  37.9 1.2 %collective-permute-start.2 = (s32[16,256]{1,0:T(8,128)S(1)}, s32[16,256]{1,0:T(8,128)S(1)}, u32[]{:S(2)}, u32[]{:S(2)}) collective-permute-start(s32[16,256]{1,0:T(8,128)S(1)} %copy-done.4), channel_id=1, source_target_pairs={{0,1},{1,0},{2,3},{3,2},{4,5},{5,4},{6,7},{7,6},{8,9},{9,8},{10,11... | collective-permute-start | bytes 49160 | tf_op jit(solution)/shard_map/ppermute | solution.py:179
  40.4 18.7 %all-to-all-start.1 = ((bf16[64,8,640]{2,1,0:T(8,128)(2,1)}), bf16[64,8,640]{2,1,0:T(8,128)(2,1)S(1)}, u32[]{:S(2)}, u32[]{:S(2)}) async-start(bf16[64,8,640]{2,1,0:T(8,128)(2,1)} %bitcast.5), calls=%async_computation.1 | async-start | bytes 1310720 | tf_op jit(solution)/shard_map/all_to_all | solution.py:168

commit v3 on v2

--- a/solution.py
+++ b/solution.py
@@ -83,26 +83,27 @@
     out[...] = jnp.dot(chosen, jnp.concatenate(sent, axis=1), preferred_element_type=F32).astype(BF)
 
 
-def combine(arrived, partial, chosen):
+def combine(arrived, sst, marine, partial, chosen):
     rows = arrived.shape[0]
     label = arrived[:, (SENT - 1) * HALF :].astype(F32)[:, :1].astype(jnp.int32)
     chosen[...] = jnp.where(label == iota((rows, CHIP_ROWS), 1) + 1, 1.0, 0.0).astype(BF)
     total = lax.dot_general(
         chosen[...], arrived[...], (((0,), (0,)), ((), ())), preferred_element_type=F32
     )
-    partial[...] = total[:, : (SENT - 1) * HALF]
+    partial[:, : (SENT - 1) * HALF] = total[:, : (SENT - 1) * HALF]
+    partial[: CHIP_ROWS // CORES, (SENT - 1) * HALF :] = halves_to_rows(sst[...])
+    partial[CHIP_ROWS // CORES :, (SENT - 1) * HALF :] = halves_to_rows(marine[...].astype(F32))
     rest = total[:, (SENT - 1) * HALF :]
     partial[:, :HALF] += jnp.where(iota((CHIP_ROWS, HALF), 1) == 0, 0.0, rest)
 
 
-def exchange(own, swapped, chosen, sst, sst_other, marine, marine_other, fluxes, out):
+def exchange(own, swapped, chosen, fluxes, out):
     both = 2 * TILES
-    total = own[...] + jnp.concatenate([swapped[both:], swapped[:both]], axis=0)
+    sums = (SENT - 1) * HALF
+    total = own[:, :sums] + jnp.concatenate([swapped[both:, :sums], swapped[:both, :sums]], axis=0)
     u, v, ta, q, rad, pr = (total[:, f * HALF : (f + 1) * HALF] for f in range(SENT - 1))
-    sst_rows = jnp.concatenate([halves_to_rows(x[...]) for x in (sst, sst_other)], axis=0)
-    w = jnp.concatenate(
-        [halves_to_rows(x[...].astype(F32)) for x in (marine, marine_other)], axis=0
-    )
+    sst_rows = jnp.concatenate([own[:both, sums:], swapped[:both, sums:]], axis=0)
+    w = jnp.concatenate([own[both:, sums:], swapped[both:, sums:]], axis=0)
     square = u * u + v * v + 0.25
     speed = jnp.sqrt(square)
     dth = sst_rows - ta
@@ -114,8 +115,8 @@
     k = c * speed
     found = (k * u * w, k * v * w, (rad - k * dth - k * dq) * w, (pr - 0.5 * k * dq) * w)
     for f, x in enumerate(found):
-        fluxes[f, :, :HALF] = x[:TILES]
-        fluxes[f, :, HALF:] = x[TILES:both]
+        fluxes[:, f, :HALF] = x[:TILES]
+        fluxes[:, f, HALF:] = x[TILES:both]
     back = jnp.concatenate([x.astype(BF) for x in found + (sst_rows * w,)], axis=1)
     out[...] = jnp.dot(chosen[...], back, preferred_element_type=F32).astype(BF)
 
@@ -161,6 +162,7 @@
     params = pltpu.CompilerParams(vmem_limit_bytes=VMEM_LIMIT)
     target = target_device.reshape(1, PAIRS)
     sea = sea_block.reshape(1, PAIRS)
+    inputs = (sky_block, target, sea, sky, weights)
     same_core = [list(range(core, devices, CORES)) for core in range(CORES)]
 
     def swap(x):
@@ -193,28 +195,27 @@
             pltpu.SemaphoreType.DMA((4 + PAIRS // GROUP,)),
         ],
         compiler_params=params,
-    )(sky_block, target, sea, sky, weights)
-    sst_other, marine_other = other_core(sst), other_core(marine)
+    )(*(pltpu.with_memory_space_constraint(x, pltpu.HBM) for x in inputs))
     partial, chosen = pl.pallas_call(
         combine,
         out_shape=(
-            jax.ShapeDtypeStruct((CHIP_ROWS, (SENT - 1) * HALF), F32),
+            jax.ShapeDtypeStruct((CHIP_ROWS, SENT * HALF), F32),
             jax.ShapeDtypeStruct((rows, CHIP_ROWS), BF),
         ),
-        in_specs=[VMEM],
+        in_specs=[VMEM] * 3,
         out_specs=(VMEM, VMEM),
         compiler_params=params,
-    )(swap(outgoing))
+    )(swap(outgoing), sst, marine)
     fluxes, back = pl.pallas_call(
         exchange,
         out_shape=(
-            jax.ShapeDtypeStruct((4, TILES, CELLS), F32),
+            jax.ShapeDtypeStruct((TILES, 4, CELLS), F32),
             jax.ShapeDtypeStruct((rows, BACK * HALF), BF),
         ),
-        in_specs=[VMEM] * 7,
+        in_specs=[VMEM] * 3,
         out_specs=(VMEM, VMEM),
         compiler_params=params,
-    )(partial, other_core(partial), chosen, sst, sst_other, marine, marine_other)
+    )(partial, other_core(partial), chosen)
     atm_back = pl.pallas_call(
         deliver,
         out_shape=jax.ShapeDtypeStruct((BACK, TILES, CELLS), F32),
@@ -226,7 +227,7 @@
         ],
         compiler_params=params,
     )(sky_block, target, swap(back), weights)
-    return jnp.transpose(fluxes, (1, 0, 2)), jnp.transpose(atm_back, (1, 0, 2))
+    return fluxes, jnp.transpose(atm_back, (1, 0, 2))
 
 
 def solution(mesh):

time: 61.9 us -> 56.8 us (0.918)
  blocking collectives: 28.1 us -> 46.2 us
  waiting for transfers between devices: 14.2 us -> 1.12 us
  starting transfers between devices: 7.44 us -> 2.29 us
  local copies, waits for them, and re-layouts: 5.1 us -> 0.03 us
    all_to_all x1 -> x2, blocking collectives: 28.1 us -> 46.2 us  [swap(): lax.all_to_all(x.reshape(chips, rows // chips, width), ('gx', 'gy'), spli...]
    all_to_all x1 -> x0, waiting for transfers between devices: 13.4 us -> none  [swap(): lax.all_to_all(x.reshape(chips, rows // chips, width), ('gx', 'gy'), spli...]
    unnamed x21 -> x10, local copies, waits for them, and re-layouts: 5.1 us -> 0.03 us
    all_to_all x1 -> x0, starting transfers between devices: 4.64 us -> none  [swap(): lax.all_to_all(x.reshape(chips, rows // chips, width), ('gx', 'gy'), spli...]
    ppermute x3 -> x1, starting transfers between devices: 2.8 us -> 2.29 us  [other_core(): return lax.ppermute(x, ('gx', 'gy'), [(d, d ^ 1) for d in range(devices)])]
  transfers between devices with their start and end apart: 4 -> 1, of which waited for: 3 -> 1; matrix products, arithmetic and copies ran while one was open for 1% -> 0% of each run, Pallas kernels for 0% -> 0%
where the time goes in v3:
time: 56.8 us; the launch traced here: 56.1 us
  blocking collectives  46.2 us (81%)
  Pallas kernels  5.81 us (10%)
  starting transfers between devices  2.29 us (4%)
  waiting for transfers between devices  1.12 us (2%)
  between operations  0.69 us (1%)
    all_to_all x2, blocking collectives, swap(): lax.all_to_all(x.reshape(chips, rows // chips, width), ('gx', 'gy'), spli...  46.2 us
    pallas_call x1, Pallas kernels, on_device(): pl.pallas_call(contribute, out_shape=jax.ShapeDtypeStruct((rows, SENT * H...  2.38 us
    ppermute x1, starting transfers between devices, other_core(): return lax.ppermute(x, ('gx', 'gy'), [(d, d ^ 1) for d in range(devices)])  2.29 us
    pallas_call x1, Pallas kernels, on_device(): pl.pallas_call(deliver, out_shape=jax.ShapeDtypeStruct((BACK, TILES, CELL...  2.24 us
  transfers between devices with their start and end apart: 1, of which 1 were waited for; matrix products, arithmetic and copies ran while one was open for 0% of the time, Pallas kernels for 0%

profile of v3, /device:TPU:1, one launch (start us, length us, event | category | flops | bytes accessed | tf_op | source)
XLA Modules:
  0.0 56.1 jit_solution(4662113692184324035)
XLA Ops:
  0.6 0.0 copy-start.1
  0.6 0.0 copy-start.2
  0.7 2.4 %shard_map.86 = bf16[512,896]{1,0:T(8,128)(2,1)S(1)} custom-call(s32[16]{0:T(128)} %src.1, s32[1,16]{1,0:T(1,128)} %bitcast.11, s32[1,16]{1,0:T(1,128)} %bitcast.14, bf16[16,8,256]{2,1,0:T(8,128)(2,1)} %sky_hbm.1, bf16[16,256,256]{2,1,0:T(8,128)(2,1)} %weights.1), custom_call_target="tpu_custom_call" | custom-call | tf_op jit(solution)/shard_map/pallas_call | solution.py:183
  3.0 0.0 copy-start
  3.1 0.0 copy-start.3
  3.1 0.0 copy-start.4
  3.1 28.1 %all_to_all.10 = bf16[64,8,896]{2,1,0:T(8,128)(2,1)S(1)} all-to-all(bf16[64,8,896]{2,1,0:T(8,128)(2,1)S(1)} %bitcast.8), channel_id=1, replica_groups={{0,2,4,6,8,10,12,14,16,18,20,22,24,26,28,30,32,34,36,38,40,42,44,46,48,..., dimensions={0} | all-to-all | bytes 1835008 | tf_op jit(solution)/shard_map/all_to_all | solution.py:170
  31.2 0.0 copy-done.1
  31.2 0.0 copy-done.2
  31.2 0.4 shard_map.87
  31.7 2.3 %collective-permute-start = (f32[64,896]{1,0:T(8,128)S(1)}, f32[64,896]{1,0:T(8,128)S(1)}, u32[]{:S(2)}, u32[]{:S(2)}) collective-permute-start(f32[64,896]{1,0:T(8,128)S(1)} %get-tuple-element.6.own), channel_id=1, source_target_pairs={{0,1},{1,0},{2,3},{3,2},{4,5},{5,4},{6,7},{7,6},{8,9},{9,8},{10,11... | collective-permute-start | bytes 688136 | tf_op jit(solution)/shard_map/ppermute | solution.py:181
  34.0 1.1 %collective-permute-done.swapped = f32[64,896]{1,0:T(8,128)S(1)} collective-permute-done((f32[64,896]{1,0:T(8,128)S(1)}, f32[64,896]{1,0:T(8,128)S(1)}, u32[]{:S(2)}, u32[]{:S(2)}) %collective-permute-start) | collective-permute-done | bytes 229408 | tf_op jit(solution)/shard_map/ppermute | solution.py:181
  35.1 0.8 %shard_map.88 = (f32[16,4,256]{2,1,0:T(4,128)}, bf16[512,640]{1,0:T(8,128)(2,1)S(1)}) custom-call(f32[64,896]{1,0:T(8,128)S(1)} %get-tuple-element.6.own, f32[64,896]{1,0:T(8,128)S(1)} %collective-permute-done.swapped, bf16[512,64]{1,0:T(8,128)(2,1)S(1)} %get-tuple-element.7.chosen), custom_call_target="tpu_custom_call" | custom-call | tf_op jit(solution)/shard_map/pallas_call | solution.py:209
  35.8 18.1 %all_to_all.11 = bf16[64,8,640]{2,1,0:T(8,128)(2,1)S(1)} all-to-all(bf16[64,8,640]{2,1,0:T(8,128)(2,1)S(1)} %bitcast.10), channel_id=1, replica_groups={{0,2,4,6,8,10,12,14,16,18,20,22,24,26,28,30,32,34,36,38,40,42,44,46,48,..., dimensions={0} | all-to-all | bytes 1310720 | tf_op jit(solution)/shard_map/all_to_all | solution.py:170
  53.9 0.0 copy-done
  53.9 0.0 copy-done.3
  53.9 0.0 copy-done.4
  53.9 2.2 %shard_map.89 = f32[5,16,256]{2,1,0:T(8,128)} custom-call(s32[16]{0:T(128)S(1)} %copy-done.3, s32[1,16]{1,0:T(1,128)S(1)} %bitcast.12, bf16[512,640]{1,0:T(8,128)(2,1)S(1)} %bitcast.9, bf16[16,256,256]{2,1,0:T(8,128)(2,1)S(1)} %copy-done), custom_call_target="tpu_custom_call" | custom-call | tf_op jit(solution)/shard_map/pallas_call | solution.py:219
Async XLA Ops:
  0.6 30.6 %copy-start.1 = (f32[16,256]{1,0:T(8,128)S(1)}, f32[16,256]{1,0:T(8,128)}, u32[]{:S(2)}) copy-start(f32[16,256]{1,0:T(8,128)} %sst.1) | copy-start | bytes 49156
  0.6 30.6 %copy-start.2 = (s32[16,256]{1,0:T(8,128)S(1)}, s32[16,256]{1,0:T(8,128)}, u32[]{:S(2)}) copy-start(s32[16,256]{1,0:T(8,128)} %marine.1) | copy-start | bytes 49156
  3.0 50.9 %copy-start = (bf16[16,256,256]{2,1,0:T(8,128)(2,1)S(1)}, bf16[16,256,256]{2,1,0:T(8,128)(2,1)}, u32[]{:S(2)}) copy-start(bf16[16,256,256]{2,1,0:T(8,128)(2,1)} %weights.1) | copy-start | bytes 6291460
  3.1 50.8 %copy-start.3 = (s32[16]{0:T(128)S(1)}, s32[16]{0:T(128)}, u32[]{:S(2)}) copy-start(s32[16]{0:T(128)} %src.1) | copy-start | bytes 196
  3.1 50.8 %copy-start.4 = (s32[16,1]{0,1:T(1,128)S(1)}, s32[16,1]{0,1:T(1,128)}, u32[]{:S(2)}) copy-start(s32[16,1]{0,1:T(1,128)} %param.10) | copy-start | bytes 196
  31.7 3.4 %collective-permute-start = (f32[64,896]{1,0:T(8,128)S(1)}, f32[64,896]{1,0:T(8,128)S(1)}, u32[]{:S(2)}, u32[]{:S(2)}) collective-permute-start(f32[64,896]{1,0:T(8,128)S(1)} %get-tuple-element.6.own), channel_id=1, source_target_pairs={{0,1},{1,0},{2,3},{3,2},{4,5},{5,4},{6,7},{7,6},{8,9},{9,8},{10,11... | collective-permute-start | bytes 688136 | tf_op jit(solution)/shard_map/ppermute | solution.py:181

commit v4 on v1

--- a/solution.py
+++ b/solution.py
@@ -14,6 +14,7 @@
 SENT = 7
 BACK = 5
 ROWS_DEST = 2 * SLOTS
+GROUP = 4
 BF = jnp.bfloat16
 F32 = jnp.float32
 VMEM_LIMIT = 24 * 1024 * 1024
@@ -40,9 +41,25 @@
     return SLOTS * column + jnp.sum(earlier, axis=1, keepdims=True)
 
 
-def contribute(src, target, sea, sky, weights, out, scratch):
-    rows = out.shape[0]
+def contribute(
+    src_hbm, target_hbm, sea_hbm, sky_hbm, weights_hbm, out,
+    src, target, sea, sky, weights, scratch, sems,
+):
+    rows = out.shape[0] * out.shape[1]
+    small = ((src_hbm, src), (sky_hbm, sky), (target_hbm, target), (sea_hbm, sea))
+    copies = [pltpu.make_async_copy(a, b, sems.at[i]) for i, (a, b) in enumerate(small)]
+    for i in range(PAIRS // GROUP):
+        part = pl.ds(i * GROUP, GROUP)
+        copies.append(
+            pltpu.make_async_copy(weights_hbm.at[part], weights.at[part], sems.at[len(small) + i])
+        )
+    for copy in copies:
+        copy.start()
+    for copy in copies[: len(small)]:
+        copy.wait()
     for p in range(PAIRS):
+        if p % GROUP == 0:
+            copies[len(small) + p // GROUP].wait()
         term = jnp.dot(sky[src[p]], weights[p], preferred_element_type=F32)
         for h in range(2):
             scratch[h, p * FIELDS : (p + 1) * FIELDS, :] = term[:, h * HALF : (h + 1) * HALF]
@@ -59,17 +76,17 @@
     place = 2.0 * jnp.sum(jnp.where(pair, slot, 0.0), axis=0, keepdims=True)
     place = place.astype(jnp.int32) + iota((1, both), 1) // PAIRS
     chosen = jnp.where(iota((rows, both), 0) == place, 1.0, 0.0).astype(BF)
-    out[...] = jnp.dot(chosen, jnp.concatenate(sent, axis=1), preferred_element_type=F32).astype(BF)
+    filled = jnp.dot(chosen, jnp.concatenate(sent, axis=1), preferred_element_type=F32)
+    out[...] = filled.astype(BF).reshape(out.shape)
 
 
 def exchange(arrived, sst, marine, fluxes, out):
-    rows = arrived.shape[0]
+    rows = arrived.shape[0] * arrived.shape[1]
     both = 2 * TILES
-    label = arrived[:, (SENT - 1) * HALF :].astype(F32)[:, :1].astype(jnp.int32)
+    slots = arrived[...].reshape(rows, SENT * HALF)
+    label = slots[:, (SENT - 1) * HALF :].astype(F32)[:, :1].astype(jnp.int32)
     chosen = jnp.where(label == iota((rows, both), 1) + 1, 1.0, 0.0).astype(BF)
-    total = lax.dot_general(
-        chosen, arrived[...], (((0,), (0,)), ((), ())), preferred_element_type=F32
-    )
+    total = lax.dot_general(chosen, slots, (((0,), (0,)), ((), ())), preferred_element_type=F32)
     u, v, ta, q, rad, pr, rest = (total[:, f * HALF : (f + 1) * HALF] for f in range(SENT))
     u = u + jnp.where(iota((both, HALF), 1) == 0, 0.0, rest)
     sst_rows = halves_to_rows(sst[...])
@@ -85,25 +102,30 @@
     k = c * speed
     found = (k * u * w, k * v * w, (rad - k * dth - k * dq) * w, (pr - 0.5 * k * dq) * w)
     for f, x in enumerate(found):
-        fluxes[f, :, :HALF] = x[:TILES]
-        fluxes[f, :, HALF:] = x[TILES:]
+        fluxes[:, f, :HALF] = x[:TILES]
+        fluxes[:, f, HALF:] = x[TILES:]
     back = jnp.concatenate([x.astype(BF) for x in found + (sst_rows * w,)], axis=1)
-    out[...] = jnp.dot(chosen, back, preferred_element_type=F32).astype(BF)
-
-
-def deliver(src, target, returned, weights, out, values, sums):
-    rows = returned.shape[0]
+    out[...] = jnp.dot(chosen, back, preferred_element_type=F32).astype(BF).reshape(out.shape)
+
+
+def deliver(src_hbm, target, returned, weights, fluxes, fluxes_out, out, src, values, sums, sem):
+    copy = pltpu.make_async_copy(src_hbm, src, sem)
+    copy.start()
+    fluxes_out[...] = fluxes[...]
+    rows = returned.shape[0] * returned.shape[1]
     both = 2 * PAIRS
     slot = slot_column(target[...])
     place = jnp.concatenate([2.0 * slot, 2.0 * slot + 1.0], axis=0).astype(jnp.int32)
     chosen = jnp.where(iota((both, rows), 1) == place, 1.0, 0.0).astype(BF)
-    picked = jnp.dot(chosen, returned[...], preferred_element_type=F32)
+    slots = returned[...].reshape(rows, BACK * HALF)
+    picked = jnp.dot(chosen, slots, preferred_element_type=F32)
     values[...] = jnp.zeros_like(values)
     for f in range(BACK):
         for h in range(2):
             part = picked[h * PAIRS : (h + 1) * PAIRS, f * HALF : (f + 1) * HALF]
             values[h, pl.ds(f, PAIRS, stride=FIELDS), :] = part
     sums[...] = jnp.zeros_like(sums)
+    copy.wait()
     for p in range(PAIRS):
         block = pl.ds(p * FIELDS, FIELDS)
         term = lax.dot_general(
@@ -120,58 +142,63 @@
             out[f, :, h * HALF : (h + 1) * HALF] = sums[h, pl.ds(f, TILES, stride=FIELDS), :]
 
 
-SMEM = pl.BlockSpec(memory_space=pltpu.SMEM)
 VMEM = pl.BlockSpec(memory_space=pltpu.VMEM)
+HBM = pl.BlockSpec(memory_space=pltpu.HBM)
 
 
 def on_device(sky, weights, sky_block, target_device, sea_block, sst, marine):
     devices = lax.axis_size(("gx", "gy"))
-    rows = devices * ROWS_DEST
     params = pltpu.CompilerParams(vmem_limit_bytes=VMEM_LIMIT)
     target = target_device.reshape(1, PAIRS)
     sea = sea_block.reshape(1, PAIRS)
+    flux_shape = jax.ShapeDtypeStruct((TILES, 4, CELLS), F32)
+
+    def wire(width):
+        return jax.ShapeDtypeStruct((devices, ROWS_DEST, width), BF)
 
     def swap(x):
-        width = x.shape[1]
-        y = lax.all_to_all(
-            x.reshape(devices, ROWS_DEST, width),
-            ("gx", "gy"),
-            split_axis=0,
-            concat_axis=0,
-            tiled=True,
-        )
-        return y.reshape(rows, width)
+        return lax.all_to_all(x, ("gx", "gy"), split_axis=0, concat_axis=0, tiled=True)
+
+    def stay(*arrays):
+        return tuple(pltpu.with_memory_space_constraint(x, pltpu.HBM) for x in arrays)
 
     outgoing = pl.pallas_call(
         contribute,
-        out_shape=jax.ShapeDtypeStruct((rows, SENT * HALF), BF),
-        in_specs=[SMEM] + [VMEM] * 4,
+        out_shape=wire(SENT * HALF),
+        in_specs=[HBM] * 5,
         out_specs=VMEM,
-        scratch_shapes=[pltpu.VMEM((2, PAIRS * FIELDS, HALF), F32)],
+        scratch_shapes=[
+            pltpu.SMEM((PAIRS,), jnp.int32),
+            pltpu.VMEM((1, PAIRS), jnp.int32),
+            pltpu.VMEM((1, PAIRS), jnp.int32),
+            pltpu.VMEM((TILES, FIELDS, CELLS), BF),
+            pltpu.VMEM((PAIRS, CELLS, CELLS), BF),
+            pltpu.VMEM((2, PAIRS * FIELDS, HALF), F32),
+            pltpu.SemaphoreType.DMA((4 + PAIRS // GROUP,)),
+        ],
         compiler_params=params,
-    )(sky_block, target, sea, sky, weights)
+    )(*stay(sky_block, target, sea, sky, weights))
     fluxes, back = pl.pallas_call(
         exchange,
-        out_shape=(
-            jax.ShapeDtypeStruct((4, TILES, CELLS), F32),
-            jax.ShapeDtypeStruct((rows, BACK * HALF), BF),
-        ),
+        out_shape=(flux_shape, wire(BACK * HALF)),
         in_specs=[VMEM] * 3,
         out_specs=(VMEM, VMEM),
         compiler_params=params,
     )(swap(outgoing), sst, marine)
-    atm_back = pl.pallas_call(
+    fluxes, atm_back = pl.pallas_call(
         deliver,
-        out_shape=jax.ShapeDtypeStruct((BACK, TILES, CELLS), F32),
-        in_specs=[SMEM] + [VMEM] * 3,
-        out_specs=VMEM,
+        out_shape=(flux_shape, jax.ShapeDtypeStruct((BACK, TILES, CELLS), F32)),
+        in_specs=[HBM] + [VMEM] * 4,
+        out_specs=(VMEM, VMEM),
         scratch_shapes=[
+            pltpu.SMEM((PAIRS,), jnp.int32),
             pltpu.VMEM((2, PAIRS * FIELDS, HALF), F32),
             pltpu.VMEM((2, TILES * FIELDS, HALF), F32),
+            pltpu.SemaphoreType.DMA,
         ],
         compiler_params=params,
-    )(sky_block, target, swap(back), weights)
-    return jnp.transpose(fluxes, (1, 0, 2)), jnp.transpose(atm_back, (1, 0, 2))
+    )(*stay(sky_block), target, swap(back), weights, fluxes)
+    return fluxes, jnp.transpose(atm_back, (1, 0, 2))
 
 
 def solution(mesh):

time: 60.3 us -> 55 us (0.912)
  blocking collectives: 29.2 us -> 48.6 us
  waiting for transfers between devices: 14.5 us -> 0 us
  local copies, waits for them, and re-layouts: 6.66 us -> 0.02 us
  starting transfers between devices: 4.38 us -> 0 us
  Pallas kernels: 4.41 us -> 5.57 us
    all_to_all x1 -> x2, blocking collectives: 29.2 us -> 48.6 us  [swap(): lax.all_to_all(x, ('gx', 'gy'), split_axis=0, concat_axis=0, tiled=True)]
    all_to_all x1 -> x0, waiting for transfers between devices: 14.5 us -> none  [swap(): lax.all_to_all(x.reshape(devices, ROWS_DEST, width), ('gx', 'gy'), split_...]
    unnamed x21 -> x8, local copies, waits for them, and re-layouts: 5.1 us -> 0.02 us
    all_to_all x1 -> x0, starting transfers between devices: 4.38 us -> none  [swap(): lax.all_to_all(x.reshape(devices, ROWS_DEST, width), ('gx', 'gy'), split_...]
    reshape x4 -> x0, local copies, waits for them, and re-layouts: 1.56 us -> none  [the longest x2 1.2 us: swap(): x.reshape(devices, ROWS_DEST, width)]
    pallas_call x3, Pallas kernels: 4.41 us -> 5.57 us  [the longest x1 2.38 us: on_device(): pl.pallas_call(contribute, out_shape=wire(SENT * HALF), in_specs=[HBM] *...]
  transfers between devices with their start and end apart: 1 -> 0, of which waited for: 1 -> 0; matrix products, arithmetic and copies ran while one was open for 1% -> 0% of each run, Pallas kernels for 0% -> 0%
where the time goes in v4:
time: 55 us; the launch traced here: 54.8 us
  blocking collectives  48.6 us (88%)
  Pallas kernels  5.57 us (10%)
  between operations  0.68 us (1%)
    all_to_all x2, blocking collectives, swap(): lax.all_to_all(x, ('gx', 'gy'), split_axis=0, concat_axis=0, tiled=True)  48.6 us
    pallas_call x1, Pallas kernels, on_device(): pl.pallas_call(contribute, out_shape=wire(SENT * HALF), in_specs=[HBM] *...  2.38 us
    pallas_call x1, Pallas kernels, on_device(): pl.pallas_call(deliver, out_shape=(flux_shape, jax.ShapeDtypeStruct((BACK...  2.27 us

profile of v4, /device:TPU:1, one launch (start us, length us, event | category | flops | bytes accessed | tf_op | source)
XLA Modules:
  0.0 54.8 jit_solution(5672718335731095471)
XLA Ops:
  0.6 0.0 copy-start.1
  0.6 0.0 copy-start.2
  0.7 2.4 %shard_map.86 = bf16[128,4,896]{2,1,0:T(4,128)(2,1)S(1)} custom-call(s32[16]{0:T(128)} %src_hbm.3, s32[1,16]{1,0:T(1,128)} %bitcast.3, s32[1,16]{1,0:T(1,128)} %bitcast.5, bf16[16,8,256]{2,1,0:T(8,128)(2,1)} %sky_hbm.1, bf16[16,256,256]{2,1,0:T(8,128)(2,1)} %weights.1), custom_call_target="tpu_custom_call" | custom-call | tf_op jit(solution)/shard_map/pallas_call | solution.py:165
  3.0 0.0 copy-start
  3.1 0.0 copy-start.3
  3.1 29.2 %all_to_all.10.arrived = bf16[128,4,896]{2,1,0:T(4,128)(2,1)S(1)} all-to-all(bf16[128,4,896]{2,1,0:T(4,128)(2,1)S(1)} %shard_map.86), channel_id=1, replica_groups=mesh['gx'=16,'gy'=8] {'gx','gy'}, dimensions={0} | all-to-all | bytes 1835008 | tf_op jit(solution)/shard_map/all_to_all | solution.py:160
  32.3 0.0 copy-done.1
  32.3 0.0 copy-done.2
  32.3 0.9 %shard_map.87 = (f32[16,4,256]{2,1,0:T(4,128)S(1)}, bf16[128,4,640]{2,1,0:T(4,128)(2,1)S(1)}) custom-call(bf16[128,4,896]{2,1,0:T(4,128)(2,1)S(1)} %all_to_all.10.arrived, f32[16,256]{1,0:T(8,128)S(1)} %copy-done.1, s32[16,256]{1,0:T(8,128)S(1)} %copy-done.2), custom_call_target="tpu_custom_call" | custom-call | tf_op jit(solution)/shard_map/pallas_call | solution.py:181
  33.2 19.3 %all_to_all.11.returned = bf16[128,4,640]{2,1,0:T(4,128)(2,1)S(1)} all-to-all(bf16[128,4,640]{2,1,0:T(4,128)(2,1)S(1)} %get-tuple-element.6), channel_id=1, replica_groups=mesh['gx'=16,'gy'=8] {'gx','gy'}, dimensions={0} | all-to-all | bytes 1310720 | tf_op jit(solution)/shard_map/all_to_all | solution.py:160
  52.6 0.0 copy-done
  52.6 0.0 copy-done.3
  52.6 2.3 %shard_map.88 = (f32[16,4,256]{2,1,0:T(4,128)}, f32[5,16,256]{2,1,0:T(8,128)}) custom-call(s32[16]{0:T(128)} %src_hbm.3, s32[1,16]{1,0:T(1,128)S(1)} %bitcast.4, bf16[128,4,640]{2,1,0:T(4,128)(2,1)S(1)} %all_to_all.11.returned, bf16[16,256,256]{2,1,0:T(8,128)(2,1)S(1)} %copy-done, f32[16,4,256]{2,1,0:T(4,128)S(1)} %get-tuple-element.7.fluxes), custom_call_target="tpu_custom_call" | custom-call | tf_op jit(solution)/shard_map/pallas_call | solution.py:188
Async XLA Ops:
  0.6 31.7 %copy-start.1 = (f32[16,256]{1,0:T(8,128)S(1)}, f32[16,256]{1,0:T(8,128)}, u32[]{:S(2)}) copy-start(f32[16,256]{1,0:T(8,128)} %sst.1) | copy-start | bytes 49156
  0.6 31.7 %copy-start.2 = (s32[16,256]{1,0:T(8,128)S(1)}, s32[16,256]{1,0:T(8,128)}, u32[]{:S(2)}) copy-start(s32[16,256]{1,0:T(8,128)} %marine.1) | copy-start | bytes 49156
  3.0 49.5 %copy-start = (bf16[16,256,256]{2,1,0:T(8,128)(2,1)S(1)}, bf16[16,256,256]{2,1,0:T(8,128)(2,1)}, u32[]{:S(2)}) copy-start(bf16[16,256,256]{2,1,0:T(8,128)(2,1)} %weights.1) | copy-start | bytes 6291460
  3.1 49.5 %copy-start.3 = (s32[16,1]{0,1:T(1,128)S(1)}, s32[16,1]{0,1:T(1,128)}, u32[]{:S(2)}) copy-start(s32[16,1]{0,1:T(1,128)} %param.10) | copy-start | bytes 196

commit v5 on v4

v5 whole, which is shorter than its diff:
```python
import jax
import jax.numpy as jnp
from jax import lax
from jax.experimental import pallas as pl
from jax.experimental.pallas import tpu as pltpu
from jax.sharding import PartitionSpec as P

PAIRS = 16
TILES = 16
FIELDS = 8
SENT = 6
BACK = 5
CELLS = 256
LANES = 128
SLOTS = 2
GROUP = 4
OUT_WIDTH = SENT * CELLS + LANES
BACK_WIDTH = BACK * CELLS
BF = jnp.bfloat16
F32 = jnp.float32
VMEM_LIMIT = 24 * 1024 * 1024


def iota(shape, dim):
    return lax.broadcasted_iota(jnp.int32, shape, dim)


def to_column(row):
    same = iota((PAIRS, PAIRS), 0) == iota((PAIRS, PAIRS), 1)
    return jnp.sum(jnp.where(same, row, 0.0), axis=1, keepdims=True)


def to_row(column):
    same = iota((PAIRS, PAIRS), 0) == iota((PAIRS, PAIRS), 1)
    return jnp.sum(jnp.where(same, column, 0.0), axis=0, keepdims=True)


def slot_column(target):
    row = target.astype(F32)
    column = to_column(row)
    later, other = iota((PAIRS, PAIRS), 0), iota((PAIRS, PAIRS), 1)
    earlier = jnp.where((column == row) & (other < later), 1.0, 0.0)
    return SLOTS * column + jnp.sum(earlier, axis=1, keepdims=True)


def contribute(
    src_hbm, target_hbm, sea_hbm, sky_hbm, weights_hbm, out,
    src, target, sea, sky, weights, scratch, sems,
):
    rows = out.shape[0] * out.shape[1]
    small = ((target_hbm, target), (sea_hbm, sea), (src_hbm, src), (sky_hbm, sky))
    copies = [pltpu.make_async_copy(a, b, sems.at[i]) for i, (a, b) in enumerate(small)]
    for i in range(PAIRS // GROUP):
        part = pl.ds(i * GROUP, GROUP)
        copies.append(
            pltpu.make_async_copy(weights_hbm.at[part], weights.at[part], sems.at[len(small) + i])
        )
    for copy in copies:
        copy.start()
    for copy in copies[:2]:
        copy.wait()
    place = to_row(slot_column(target[...])).astype(jnp.int32)
    chosen = jnp.where(iota((rows, PAIRS), 0) == place, 1.0, 0.0).astype(BF)
    label = to_column(sea[...].astype(F32)) + 1.0
    for copy in copies[2 : len(small)]:
        copy.wait()
    for p in range(PAIRS):
        if p % GROUP == 0:
            copies[len(small) + p // GROUP].wait()
        term = jnp.dot(sky[src[p]], weights[p], preferred_element_type=F32)
        for h in range(2):
            scratch[h, p * FIELDS : (p + 1) * FIELDS, :] = term[:, h * LANES : (h + 1) * LANES]

    def field(f):
        parts = [scratch[h, pl.ds(f, PAIRS, stride=FIELDS), :] for h in range(2)]
        return jnp.concatenate(parts, axis=1)

    u, v, ta, qa, sw, lw, pr, ps = (field(f) for f in range(FIELDS))
    sent = [x.astype(BF) for x in (u, v, ta, qa - 0.3 * ps, 0.5 * sw + 0.3 * lw, pr)]
    rest = (u - sent[0].astype(F32))[:, :LANES]
    sent.append(jnp.where(iota((PAIRS, LANES), 1) == 0, label, rest).astype(BF))
    filled = jnp.dot(chosen, jnp.concatenate(sent, axis=1), preferred_element_type=F32)
    out[...] = filled.astype(BF).reshape(out.shape)


def exchange(arrived, sst, marine, fluxes, out):
    rows = arrived.shape[0] * arrived.shape[1]
    slots = arrived[...].reshape(rows, OUT_WIDTH)
    label = slots[:, SENT * CELLS :].astype(F32)[:, :1].astype(jnp.int32)
    chosen = jnp.where(label == iota((rows, TILES), 1) + 1, 1.0, 0.0).astype(BF)
    total = lax.dot_general(chosen, slots, (((0,), (0,)), ((), ())), preferred_element_type=F32)
    u, v, ta, q, rad, pr = (total[:, f * CELLS : (f + 1) * CELLS] for f in range(SENT))
    rest = jnp.where(iota((TILES, LANES), 1) == 0, 0.0, total[:, SENT * CELLS :])
    u = jnp.concatenate([u[:, :LANES] + rest, u[:, LANES:]], axis=1)
    warmth = sst[...]
    w = marine[...].astype(F32)
    speed = jnp.sqrt(u * u + v * v + 0.25)
    dth = warmth - ta
    dq = 0.4 * warmth - q
    lift = 2.0 * (dth + 0.5 * dq)
    c = jnp.ones_like(speed)
    for _ in range(3):
        c = 1.0 + 0.5 * jnp.tanh(lift / (1.0 + c * speed * speed))
    k = c * speed
    found = (k * u * w, k * v * w, (rad - k * dth - k * dq) * w, (pr - 0.5 * k * dq) * w)
    for f, x in enumerate(found):
        fluxes[:, f, :] = x
    back = jnp.concatenate([x.astype(BF) for x in found + (warmth * w,)], axis=1)
    out[...] = jnp.dot(chosen, back, preferred_element_type=F32).astype(BF).reshape(out.shape)


def deliver(
    src_hbm, target, returned, weights, fluxes, fluxes_hbm, out, src, values, sums, sems
):
    copies = [
        pltpu.make_async_copy(src_hbm, src, sems.at[0]),
        pltpu.make_async_copy(fluxes, fluxes_hbm, sems.at[1]),
    ]
    for copy in copies:
        copy.start()
    rows = returned.shape[0] * returned.shape[1]
    place = slot_column(target[...]).astype(jnp.int32)
    chosen = jnp.where(iota((PAIRS, rows), 1) == place, 1.0, 0.0).astype(BF)
    slots = returned[...].reshape(rows, BACK_WIDTH)
    picked = jnp.dot(chosen, slots, preferred_element_type=F32)
    values[...] = jnp.zeros_like(values)
    for f in range(BACK):
        for h in range(2):
            start = f * CELLS + h * LANES
            values[h, pl.ds(f, PAIRS, stride=FIELDS), :] = picked[:, start : start + LANES]
    sums[...] = jnp.zeros_like(sums)
    copies[0].wait()
    for p in range(PAIRS):
        block = pl.ds(p * FIELDS, FIELDS)
        term = lax.dot_general(
            jnp.concatenate([values[h, block, :] for h in range(2)], axis=1).astype(BF),
            weights[p],
            (((1,), (1,)), ((), ())),
            preferred_element_type=F32,
        )
        at = pl.ds(pl.multiple_of(src[p] * FIELDS, FIELDS), FIELDS)
        for h in range(2):
            sums[h, at, :] += term[:, h * LANES : (h + 1) * LANES]
    for f in range(BACK):
        for h in range(2):
            out[f, :, h * LANES : (h + 1) * LANES] = sums[h, pl.ds(f, TILES, stride=FIELDS), :]
    copies[1].wait()


VMEM = pl.BlockSpec(memory_space=pltpu.VMEM)
HBM = pl.BlockSpec(memory_space=pltpu.HBM)


def on_device(sky, weights, sky_block, target_device, sea_block, sst, marine):
    devices = lax.axis_size(("gx", "gy"))
    params = pltpu.CompilerParams(vmem_limit_bytes=VMEM_LIMIT)
    target = target_device.reshape(1, PAIRS)
    sea = sea_block.reshape(1, PAIRS)
    flux_shape = jax.ShapeDtypeStruct((TILES, 4, CELLS), F32)

    def wire(width):
        return jax.ShapeDtypeStruct((devices, SLOTS, width), BF)

    def swap(x):
        return lax.all_to_all(x, ("gx", "gy"), split_axis=0, concat_axis=0, tiled=True)

    def stay(*arrays):
        return tuple(pltpu.with_memory_space_constraint(x, pltpu.HBM) for x in arrays)

    outgoing = pl.pallas_call(
        contribute,
        out_shape=wire(OUT_WIDTH),
        in_specs=[HBM] * 5,
        out_specs=VMEM,
        scratch_shapes=[
            pltpu.SMEM((PAIRS,), jnp.int32),
            pltpu.VMEM((1, PAIRS), jnp.int32),
            pltpu.VMEM((1, PAIRS), jnp.int32),
            pltpu.VMEM((TILES, FIELDS, CELLS), BF),
            pltpu.VMEM((PAIRS, CELLS, CELLS), BF),
            pltpu.VMEM((2, PAIRS * FIELDS, LANES), F32),
            pltpu.SemaphoreType.DMA((4 + PAIRS // GROUP,)),
        ],
        compiler_params=params,
    )(*stay(sky_block, target, sea, sky, weights))
    fluxes, back = pl.pallas_call(
        exchange,
        out_shape=(flux_shape, wire(BACK_WIDTH)),
        in_specs=[VMEM] * 3,
        out_specs=(VMEM, VMEM),
        compiler_params=params,
    )(swap(outgoing), sst, marine)
    fluxes, atm_back = pl.pallas_call(
        deliver,
        out_shape=(flux_shape, jax.ShapeDtypeStruct((BACK, TILES, CELLS), F32)),
        in_specs=[HBM] + [VMEM] * 4,
        out_specs=(HBM, VMEM),
        scratch_shapes=[
            pltpu.SMEM((PAIRS,), jnp.int32),
            pltpu.VMEM((2, PAIRS * FIELDS, LANES), F32),
            pltpu.VMEM((2, TILES * FIELDS, LANES), F32),
            pltpu.SemaphoreType.DMA((2,)),
        ],
        compiler_params=params,
    )(*stay(sky_block), target, swap(back), weights, fluxes)
    return fluxes, jnp.transpose(atm_back, (1, 0, 2))


def solution(mesh):
    tiles = P(("gx", "gy"), None, None)
    cells = P(("gx", "gy"), None)
    flat = P(("gx", "gy"))
    return jax.shard_map(
        on_device,
        mesh=mesh,
        in_specs=(tiles, tiles, flat, cells, flat, cells, cells),
        out_specs=(tiles, tiles),
        check_vma=False,
    )
```

time: 55 us -> 54 us (0.982)
  blocking collectives: 48.6 us -> 47.9 us
    all_to_all x2, blocking collectives: 48.6 us -> 47.9 us  [swap(): lax.all_to_all(x, ('gx', 'gy'), split_axis=0, concat_axis=0, tiled=True)]
where the time goes in v5:
time: 54 us; the launch traced here: 53.8 us
  blocking collectives  47.9 us (89%)
  Pallas kernels  5.24 us (10%)
  between operations  0.68 us (1%)
    all_to_all x2, blocking collectives, swap(): lax.all_to_all(x, ('gx', 'gy'), split_axis=0, concat_axis=0, tiled=True)  47.9 us
    pallas_call x1, Pallas kernels, on_device(): pl.pallas_call(contribute, out_shape=wire(OUT_WIDTH), in_specs=[HBM] * 5,...  2.32 us
    pallas_call x1, Pallas kernels, on_device(): pl.pallas_call(deliver, out_shape=(flux_shape, jax.ShapeDtypeStruct((BACK...  2.04 us

profile of v5, /device:TPU:1, one launch (start us, length us, event | category | flops | bytes accessed | tf_op | source)
XLA Modules:
  0.0 53.8 jit_solution(307814008512290435)
XLA Ops:
  0.6 0.0 copy-start.1
  0.6 0.0 copy-start.2
  0.7 2.3 %shard_map.86 = bf16[128,2,1664]{2,1,0:T(2,128)(2,1)S(1)} custom-call(s32[16]{0:T(128)} %src_hbm.3, s32[1,16]{1,0:T(1,128)} %bitcast.3, s32[1,16]{1,0:T(1,128)} %bitcast.5, bf16[16,8,256]{2,1,0:T(8,128)(2,1)} %sky_hbm.1, bf16[16,256,256]{2,1,0:T(8,128)(2,1)} %weights.1), custom_call_target="tpu_custom_call" | custom-call | tf_op jit(solution)/shard_map/pallas_call | solution.py:170
  3.0 0.0 copy-start
  3.0 0.0 copy-start.3
  3.0 28.5 %all_to_all.10.arrived = bf16[128,2,1664]{2,1,0:T(2,128)(2,1)S(1)} all-to-all(bf16[128,2,1664]{2,1,0:T(2,128)(2,1)S(1)} %shard_map.86), channel_id=1, replica_groups=mesh['gx'=16,'gy'=8] {'gx','gy'}, dimensions={0} | all-to-all | bytes 1703936 | tf_op jit(solution)/shard_map/all_to_all | solution.py:165
  31.5 0.0 copy-done.1
  31.5 0.0 copy-done.2
  31.5 0.9 %shard_map.87 = (f32[16,4,256]{2,1,0:T(4,128)S(1)}, bf16[128,2,1280]{2,1,0:T(2,128)(2,1)S(1)}) custom-call(bf16[128,2,1664]{2,1,0:T(2,128)(2,1)S(1)} %all_to_all.10.arrived, f32[16,256]{1,0:T(8,128)S(1)} %copy-done.1, s32[16,256]{1,0:T(8,128)S(1)} %copy-done.2), custom_call_target="tpu_custom_call" | custom-call | tf_op jit(solution)/shard_map/pallas_call | solution.py:186
  32.4 19.3 %all_to_all.11.returned = bf16[128,2,1280]{2,1,0:T(2,128)(2,1)S(1)} all-to-all(bf16[128,2,1280]{2,1,0:T(2,128)(2,1)S(1)} %get-tuple-element.6), channel_id=1, replica_groups=mesh['gx'=16,'gy'=8] {'gx','gy'}, dimensions={0} | all-to-all | bytes 1310720 | tf_op jit(solution)/shard_map/all_to_all | solution.py:165
  51.8 0.0 copy-done
  51.8 0.0 copy-done.3
  51.8 2.0 %shard_map.88 = (f32[16,4,256]{2,1,0:T(4,128)}, f32[5,16,256]{2,1,0:T(8,128)}) custom-call(s32[16]{0:T(128)} %src_hbm.3, s32[1,16]{1,0:T(1,128)S(1)} %bitcast.4, bf16[128,2,1280]{2,1,0:T(2,128)(2,1)S(1)} %all_to_all.11.returned, bf16[16,256,256]{2,1,0:T(8,128)(2,1)S(1)} %copy-done, f32[16,4,256]{2,1,0:T(4,128)S(1)} %get-tuple-element.7.fluxes), custom_call_target="tpu_custom_call" | custom-call | tf_op jit(solution)/shard_map/pallas_call | solution.py:193
Async XLA Ops:
  0.6 30.9 %copy-start.1 = (f32[16,256]{1,0:T(8,128)S(1)}, f32[16,256]{1,0:T(8,128)}, u32[]{:S(2)}) copy-start(f32[16,256]{1,0:T(8,128)} %sst.1) | copy-start | bytes 49156
  0.6 30.9 %copy-start.2 = (s32[16,256]{1,0:T(8,128)S(1)}, s32[16,256]{1,0:T(8,128)}, u32[]{:S(2)}) copy-start(s32[16,256]{1,0:T(8,128)} %marine.1) | copy-start | bytes 49156
  3.0 48.8 %copy-start = (bf16[16,256,256]{2,1,0:T(8,128)(2,1)S(1)}, bf16[16,256,256]{2,1,0:T(8,128)(2,1)}, u32[]{:S(2)}) copy-start(bf16[16,256,256]{2,1,0:T(8,128)(2,1)} %weights.1) | copy-start | bytes 6291460
  3.0 48.8 %copy-start.3 = (s32[16,1]{0,1:T(1,128)S(1)}, s32[16,1]{0,1:T(1,128)}, u32[]{:S(2)}) copy-start(s32[16,1]{0,1:T(1,128)} %param.10) | copy-start | bytes 196

commit v6 on v5

--- a/solution.py
+++ b/solution.py
@@ -13,7 +13,7 @@
 CELLS = 256
 LANES = 128
 SLOTS = 2
-GROUP = 4
+STRIP = 16
 OUT_WIDTH = SENT * CELLS + LANES
 BACK_WIDTH = BACK * CELLS
 BF = jnp.bfloat16
@@ -44,30 +44,61 @@
 
 
 def contribute(
-    src_hbm, target_hbm, sea_hbm, sky_hbm, weights_hbm, out,
-    src, target, sea, sky, weights, scratch, sems,
+    src_hbm, owner_hbm, sea_hbm, sky_hbm, weights_hbm, sst_hbm, marine_hbm, out, sst, marine,
+    src, owner, sea, sky, blocks, top, middle, bottom, scratch, sems,
 ):
-    rows = out.shape[0] * out.shape[1]
-    small = ((target_hbm, target), (sea_hbm, sea), (src_hbm, src), (sky_hbm, sky))
-    copies = [pltpu.make_async_copy(a, b, sems.at[i]) for i, (a, b) in enumerate(small)]
-    for i in range(PAIRS // GROUP):
-        part = pl.ds(i * GROUP, GROUP)
-        copies.append(
-            pltpu.make_async_copy(weights_hbm.at[part], weights.at[part], sems.at[len(small) + i])
+    copies = {}
+
+    def fetch(name, source, held):
+        copies[name] = pltpu.make_async_copy(source, held, sems.at[len(copies)])
+        copies[name].start()
+
+    left, right = pl.ds(0, LANES), pl.ds(LANES, LANES)
+    every = pl.ds(0, PAIRS)
+    fetch("upper", weights_hbm.at[every, left, left], blocks.at[0])
+    fetch("lower", weights_hbm.at[every, right, right], blocks.at[1])
+    fetch("top", weights_hbm.at[every, pl.ds(0, STRIP), right], top)
+    fetch("middle", weights_hbm.at[every, pl.ds(LANES - STRIP, 2 * STRIP)], middle)
+    fetch("bottom", weights_hbm.at[every, pl.ds(CELLS - STRIP, STRIP), left], bottom)
+    fetch("owner", owner_hbm, owner)
+    fetch("sea", sea_hbm, sea)
+    fetch("src", src_hbm, src)
+    fetch("sky", sky_hbm, sky)
+    fetch("sst", sst_hbm, sst)
+    fetch("marine", marine_hbm, marine)
+    out[...] = jnp.zeros_like(out)
+    copies["owner"].wait()
+    copies["sea"].wait()
+    at = iota((PAIRS, PAIRS), 1)
+    row = jnp.zeros((PAIRS, PAIRS), jnp.int32)
+    tiles = jnp.zeros((PAIRS, LANES), jnp.int32)
+    for p in range(PAIRS):
+        row = jnp.where(at == p, owner[p], row)
+        tiles = jnp.where(iota((PAIRS, LANES), 0) == p, sea[p], tiles)
+    row = row[:1].astype(F32)
+    column = to_column(row)
+    before = at < iota((PAIRS, PAIRS), 0)
+    rank = jnp.sum(jnp.where((column == row) & before, 1.0, 0.0), axis=1, keepdims=True)
+    both = SLOTS * PAIRS
+    wanted, pair = iota((both, PAIRS), 0), iota((both, PAIRS), 1)
+    mine = jnp.sum(jnp.where(wanted // SLOTS == pair, row, 0.0), axis=1, keepdims=True)
+    fits = (mine == row) & ((wanted % SLOTS).astype(F32) == to_row(rank))
+    chosen = jnp.where(fits, 1.0, 0.0).astype(BF)
+    label = tiles.astype(F32) + 1.0
+    for name in ("src", "sky", "top", "middle", "bottom", "upper", "lower"):
+        copies[name].wait()
+    gap = jnp.zeros((LANES - 2 * STRIP, LANES), BF)
+    for p in range(PAIRS):
+        upper = jnp.concatenate([top[p], gap, middle[p, :STRIP, LANES:]], axis=0)
+        lower = jnp.concatenate([middle[p, STRIP:, :LANES], gap, bottom[p]], axis=0)
+        weights = jnp.concatenate(
+            [
+                jnp.concatenate([blocks[0, p], upper], axis=1),
+                jnp.concatenate([lower, blocks[1, p]], axis=1),
+            ],
+            axis=0,
         )
-    for copy in copies:
-        copy.start()
-    for copy in copies[:2]:
-        copy.wait()
-    place = to_row(slot_column(target[...])).astype(jnp.int32)
-    chosen = jnp.where(iota((rows, PAIRS), 0) == place, 1.0, 0.0).astype(BF)
-    label = to_column(sea[...].astype(F32)) + 1.0
-    for copy in copies[2 : len(small)]:
-        copy.wait()
-    for p in range(PAIRS):
-        if p % GROUP == 0:
-            copies[len(small) + p // GROUP].wait()
-        term = jnp.dot(sky[src[p]], weights[p], preferred_element_type=F32)
+        term = jnp.dot(sky[src[p]], weights, preferred_element_type=F32)
         for h in range(2):
             scratch[h, p * FIELDS : (p + 1) * FIELDS, :] = term[:, h * LANES : (h + 1) * LANES]
 
@@ -80,7 +111,11 @@
     rest = (u - sent[0].astype(F32))[:, :LANES]
     sent.append(jnp.where(iota((PAIRS, LANES), 1) == 0, label, rest).astype(BF))
     filled = jnp.dot(chosen, jnp.concatenate(sent, axis=1), preferred_element_type=F32)
-    out[...] = filled.astype(BF).reshape(out.shape)
+    filled = filled.astype(BF).reshape(PAIRS, SLOTS, OUT_WIDTH)
+    for p in range(PAIRS):
+        out[owner[p]] = filled[p]
+    copies["sst"].wait()
+    copies["marine"].wait()
 
 
 def exchange(arrived, sst, marine, fluxes, out):
@@ -110,10 +145,10 @@
 
 
 def deliver(
-    src_hbm, target, returned, weights, fluxes, fluxes_hbm, out, src, values, sums, sems
+    src_row, target, returned, weights, fluxes, fluxes_hbm, out, src, values, terms, sums, sems
 ):
     copies = [
-        pltpu.make_async_copy(src_hbm, src, sems.at[0]),
+        pltpu.make_async_copy(src_row, src, sems.at[0]),
         pltpu.make_async_copy(fluxes, fluxes_hbm, sems.at[1]),
     ]
     for copy in copies:
@@ -129,7 +164,6 @@
             start = f * CELLS + h * LANES
             values[h, pl.ds(f, PAIRS, stride=FIELDS), :] = picked[:, start : start + LANES]
     sums[...] = jnp.zeros_like(sums)
-    copies[0].wait()
     for p in range(PAIRS):
         block = pl.ds(p * FIELDS, FIELDS)
         term = lax.dot_general(
@@ -138,9 +172,14 @@
             (((1,), (1,)), ((), ())),
             preferred_element_type=F32,
         )
+        for h in range(2):
+            terms[h, block, :] = term[:, h * LANES : (h + 1) * LANES]
+    copies[0].wait()
+    for p in range(PAIRS):
+        block = pl.ds(p * FIELDS, FIELDS)
         at = pl.ds(pl.multiple_of(src[p] * FIELDS, FIELDS), FIELDS)
         for h in range(2):
-            sums[h, at, :] += term[:, h * LANES : (h + 1) * LANES]
+            sums[h, at, :] += terms[h, block, :]
     for f in range(BACK):
         for h in range(2):
             out[f, :, h * LANES : (h + 1) * LANES] = sums[h, pl.ds(f, TILES, stride=FIELDS), :]
@@ -155,7 +194,6 @@
     devices = lax.axis_size(("gx", "gy"))
     params = pltpu.CompilerParams(vmem_limit_bytes=VMEM_LIMIT)
     target = target_device.reshape(1, PAIRS)
-    sea = sea_block.reshape(1, PAIRS)
     flux_shape = jax.ShapeDtypeStruct((TILES, 4, CELLS), F32)
 
     def wire(width):
@@ -167,22 +205,29 @@
     def stay(*arrays):
         return tuple(pltpu.with_memory_space_constraint(x, pltpu.HBM) for x in arrays)
 
-    outgoing = pl.pallas_call(
+    outgoing, sst, marine = pl.pallas_call(
         contribute,
-        out_shape=wire(OUT_WIDTH),
-        in_specs=[HBM] * 5,
-        out_specs=VMEM,
+        out_shape=(
+            wire(OUT_WIDTH),
+            jax.ShapeDtypeStruct((TILES, CELLS), F32),
+            jax.ShapeDtypeStruct((TILES, CELLS), jnp.int32),
+        ),
+        in_specs=[HBM] * 7,
+        out_specs=(VMEM,) * 3,
         scratch_shapes=[
             pltpu.SMEM((PAIRS,), jnp.int32),
-            pltpu.VMEM((1, PAIRS), jnp.int32),
-            pltpu.VMEM((1, PAIRS), jnp.int32),
+            pltpu.SMEM((PAIRS,), jnp.int32),
+            pltpu.SMEM((PAIRS,), jnp.int32),
             pltpu.VMEM((TILES, FIELDS, CELLS), BF),
-            pltpu.VMEM((PAIRS, CELLS, CELLS), BF),
+            pltpu.VMEM((2, PAIRS, LANES, LANES), BF),
+            pltpu.VMEM((PAIRS, STRIP, LANES), BF),
+            pltpu.VMEM((PAIRS, 2 * STRIP, CELLS), BF),
+            pltpu.VMEM((PAIRS, STRIP, LANES), BF),
             pltpu.VMEM((2, PAIRS * FIELDS, LANES), F32),
-            pltpu.SemaphoreType.DMA((4 + PAIRS // GROUP,)),
+            pltpu.SemaphoreType.DMA((11,)),
         ],
         compiler_params=params,
-    )(*stay(sky_block, target, sea, sky, weights))
+    )(*stay(sky_block, target_device.reshape(PAIRS), sea_block, sky, weights, sst, marine))
     fluxes, back = pl.pallas_call(
         exchange,
         out_shape=(flux_shape, wire(BACK_WIDTH)),
@@ -193,16 +238,17 @@
     fluxes, atm_back = pl.pallas_call(
         deliver,
         out_shape=(flux_shape, jax.ShapeDtypeStruct((BACK, TILES, CELLS), F32)),
-        in_specs=[HBM] + [VMEM] * 4,
+        in_specs=[VMEM] * 5,
         out_specs=(HBM, VMEM),
         scratch_shapes=[
             pltpu.SMEM((PAIRS,), jnp.int32),
+            pltpu.VMEM((2, PAIRS * FIELDS, LANES), F32),
             pltpu.VMEM((2, PAIRS * FIELDS, LANES), F32),
             pltpu.VMEM((2, TILES * FIELDS, LANES), F32),
             pltpu.SemaphoreType.DMA((2,)),
         ],
         compiler_params=params,
-    )(*stay(sky_block), target, swap(back), weights, fluxes)
+    )(sky_block, target, swap(back), weights, fluxes)
     return fluxes, jnp.transpose(atm_back, (1, 0, 2))
 
 

time: 54 us -> 53.7 us (level)
  no operation moved by 1% of the time
where the time goes in v6:
time: 53.7 us; the launch traced here: 53.5 us
  blocking collectives  47.9 us (89%)
  Pallas kernels  4.95 us (9%)
  between operations  0.67 us (1%)
    all_to_all x2, blocking collectives, swap(): lax.all_to_all(x, ('gx', 'gy'), split_axis=0, concat_axis=0, tiled=True)  47.9 us
    pallas_call x1, Pallas kernels, on_device(): pl.pallas_call(deliver, out_shape=(flux_shape, jax.ShapeDtypeStruct((BACK...  2.07 us
    pallas_call x1, Pallas kernels, on_device(): pl.pallas_call(contribute, out_shape=(wire(OUT_WIDTH), jax.ShapeDtypeStru...  2 us

profile of v6, /device:TPU:1, one launch (start us, length us, event | category | flops | bytes accessed | tf_op | source)
XLA Modules:
  0.0 53.5 jit_solution(9151036143108132704)
XLA Ops:
  0.6 2.0 %shard_map.86 = (bf16[128,2,1664]{2,1,0:T(2,128)(2,1)S(1)}, f32[16,256]{1,0:T(8,128)S(1)}, s32[16,256]{1,0:T(8,128)S(1)}) custom-call(s32[16]{0:T(128)} %src_row.1, s32[16]{0:T(128)} %bitcast.3, s32[16]{0:T(128)} %sea_hbm.1, bf16[16,8,256]{2,1,0:T(8,128)(2,1)} %sky_hbm.1, bf16[16,256,256]{2,1,0:T(8,128)(2,1)} %weights.1, f32[16,256]{1,0:T(8,128)} %sst_hbm.1, ...), custom_call_target="tpu_custom_call" | custom-call | tf_op jit(solution)/shard_map/pallas_call | solution.py:208
  2.6 0.0 copy-start
  2.7 0.0 copy-start.1
  2.7 0.0 copy-start.2
  2.7 28.5 %all_to_all.10.arrived = bf16[128,2,1664]{2,1,0:T(2,128)(2,1)S(1)} all-to-all(bf16[128,2,1664]{2,1,0:T(2,128)(2,1)S(1)} %get-tuple-element.9), channel_id=1, replica_groups=mesh['gx'=16,'gy'=8] {'gx','gy'}, dimensions={0} | all-to-all | bytes 1703936 | tf_op jit(solution)/shard_map/all_to_all | solution.py:203
  31.2 0.9 %shard_map.87 = (f32[16,4,256]{2,1,0:T(4,128)S(1)}, bf16[128,2,1280]{2,1,0:T(2,128)(2,1)S(1)}) custom-call(bf16[128,2,1664]{2,1,0:T(2,128)(2,1)S(1)} %all_to_all.10.arrived, f32[16,256]{1,0:T(8,128)S(1)} %get-tuple-element.10.sst, s32[16,256]{1,0:T(8,128)S(1)} %get-tuple-element.11.marine), custom_call_target="tpu_custom_call" | custom-call | tf_op jit(solution)/shard_map/pallas_call | solution.py:231
  32.1 19.3 %all_to_all.11.returned = bf16[128,2,1280]{2,1,0:T(2,128)(2,1)S(1)} all-to-all(bf16[128,2,1280]{2,1,0:T(2,128)(2,1)S(1)} %get-tuple-element.12), channel_id=1, replica_groups=mesh['gx'=16,'gy'=8] {'gx','gy'}, dimensions={0} | all-to-all | bytes 1310720 | tf_op jit(solution)/shard_map/all_to_all | solution.py:203
  51.4 0.0 copy-done
  51.4 0.0 copy-done.1
  51.4 0.0 copy-done.2
  51.5 2.1 %shard_map.88 = (f32[16,4,256]{2,1,0:T(4,128)}, f32[5,16,256]{2,1,0:T(8,128)}) custom-call(s32[16]{0:T(128)S(1)} %copy-done.1, s32[1,16]{1,0:T(1,128)S(1)} %bitcast.4, bf16[128,2,1280]{2,1,0:T(2,128)(2,1)S(1)} %all_to_all.11.returned, bf16[16,256,256]{2,1,0:T(8,128)(2,1)S(1)} %copy-done, f32[16,4,256]{2,1,0:T(4,128)S(1)} %get-tuple-element.13.fluxes), custom_call_target="tpu_custom_call" | custom-call | tf_op jit(solution)/shard_map/pallas_call | solution.py:238
Async XLA Ops:
  2.6 48.8 %copy-start = (bf16[16,256,256]{2,1,0:T(8,128)(2,1)S(1)}, bf16[16,256,256]{2,1,0:T(8,128)(2,1)}, u32[]{:S(2)}) copy-start(bf16[16,256,256]{2,1,0:T(8,128)(2,1)} %weights.1) | copy-start | bytes 6291460
  2.7 48.8 %copy-start.1 = (s32[16]{0:T(128)S(1)}, s32[16]{0:T(128)}, u32[]{:S(2)}) copy-start(s32[16]{0:T(128)} %src_row.1) | copy-start | bytes 196
  2.7 48.8 %copy-start.2 = (s32[16,1]{0,1:T(1,128)S(1)}, s32[16,1]{0,1:T(1,128)}, u32[]{:S(2)}) copy-start(s32[16,1]{0,1:T(1,128)} %param.10) | copy-start | bytes 196

commit v7 on v6

--- a/solution.py
+++ b/solution.py
@@ -1,3 +1,5 @@
+import functools
+
 import jax
 import jax.numpy as jnp
 from jax import lax
@@ -121,8 +123,10 @@
 def exchange(arrived, sst, marine, fluxes, out):
     rows = arrived.shape[0] * arrived.shape[1]
     slots = arrived[...].reshape(rows, OUT_WIDTH)
-    label = slots[:, SENT * CELLS :].astype(F32)[:, :1].astype(jnp.int32)
-    chosen = jnp.where(label == iota((rows, TILES), 1) + 1, 1.0, 0.0).astype(BF)
+    first = jnp.where(iota((LANES, TILES), 0) == 0, 1.0, 0.0).astype(BF)
+    label = jnp.dot(slots[:, SENT * CELLS :], first, preferred_element_type=F32)
+    tile = (iota((rows, TILES), 1) + 1).astype(F32)
+    chosen = jnp.where(label == tile, 1.0, 0.0).astype(BF)
     total = lax.dot_general(chosen, slots, (((0,), (0,)), ((), ())), preferred_element_type=F32)
     u, v, ta, q, rad, pr = (total[:, f * CELLS : (f + 1) * CELLS] for f in range(SENT))
     rest = jnp.where(iota((TILES, LANES), 1) == 0, 0.0, total[:, SENT * CELLS :])
@@ -145,24 +149,22 @@
 
 
 def deliver(
-    src_row, target, returned, weights, fluxes, fluxes_hbm, out, src, values, terms, sums, sems
+    src_row, target, returned, weights, fluxes, fluxes_hbm, out, values, terms, sums, sem
 ):
-    copies = [
-        pltpu.make_async_copy(src_row, src, sems.at[0]),
-        pltpu.make_async_copy(fluxes, fluxes_hbm, sems.at[1]),
-    ]
-    for copy in copies:
-        copy.start()
-    rows = returned.shape[0] * returned.shape[1]
-    place = slot_column(target[...]).astype(jnp.int32)
-    chosen = jnp.where(iota((PAIRS, rows), 1) == place, 1.0, 0.0).astype(BF)
-    slots = returned[...].reshape(rows, BACK_WIDTH)
-    picked = jnp.dot(chosen, slots, preferred_element_type=F32)
+    copy = pltpu.make_async_copy(fluxes, fluxes_hbm, sem)
+    copy.start()
+    owners, sources = target[...], src_row[...]
+    owner = [owners[0, p] for p in range(PAIRS)]
+    src = [sources[0, p] for p in range(PAIRS)]
     values[...] = jnp.zeros_like(values)
-    for f in range(BACK):
-        for h in range(2):
-            start = f * CELLS + h * LANES
-            values[h, pl.ds(f, PAIRS, stride=FIELDS), :] = picked[:, start : start + LANES]
+    for p in range(PAIRS):
+        second = functools.reduce(jnp.logical_or, [owner[q] == owner[p] for q in range(p)], False)
+        slots = returned[owner[p]].astype(F32)
+        slot = jnp.where(second, slots[1:], slots[:1])
+        for f in range(BACK):
+            for h in range(2):
+                start = f * CELLS + h * LANES
+                values[h, p * FIELDS + f : p * FIELDS + f + 1, :] = slot[:, start : start + LANES]
     sums[...] = jnp.zeros_like(sums)
     for p in range(PAIRS):
         block = pl.ds(p * FIELDS, FIELDS)
@@ -174,7 +176,6 @@
         )
         for h in range(2):
             terms[h, block, :] = term[:, h * LANES : (h + 1) * LANES]
-    copies[0].wait()
     for p in range(PAIRS):
         block = pl.ds(p * FIELDS, FIELDS)
         at = pl.ds(pl.multiple_of(src[p] * FIELDS, FIELDS), FIELDS)
@@ -183,7 +184,7 @@
     for f in range(BACK):
         for h in range(2):
             out[f, :, h * LANES : (h + 1) * LANES] = sums[h, pl.ds(f, TILES, stride=FIELDS), :]
-    copies[1].wait()
+    copy.wait()
 
 
 VMEM = pl.BlockSpec(memory_space=pltpu.VMEM)
@@ -241,14 +242,13 @@
         in_specs=[VMEM] * 5,
         out_specs=(HBM, VMEM),
         scratch_shapes=[
-            pltpu.SMEM((PAIRS,), jnp.int32),
             pltpu.VMEM((2, PAIRS * FIELDS, LANES), F32),
             pltpu.VMEM((2, PAIRS * FIELDS, LANES), F32),
             pltpu.VMEM((2, TILES * FIELDS, LANES), F32),
-            pltpu.SemaphoreType.DMA((2,)),
+            pltpu.SemaphoreType.DMA,
         ],
         compiler_params=params,
-    )(sky_block, target, swap(back), weights, fluxes)
+    )(sky_block.reshape(1, PAIRS), target, swap(back), weights, fluxes)
     return fluxes, jnp.transpose(atm_back, (1, 0, 2))
 
 

time: 53.7 us -> 53.3 us (level)
  no operation moved by 1% of the time
where the time goes in v7:
time: 53.3 us; the launch traced here: 53.1 us
  blocking collectives  47.9 us (90%)
  Pallas kernels  4.52 us (8%)
  between operations  0.68 us (1%)
    all_to_all x2, blocking collectives, swap(): lax.all_to_all(x, ('gx', 'gy'), split_axis=0, concat_axis=0, tiled=True)  47.9 us
    pallas_call x1, Pallas kernels, on_device(): pl.pallas_call(contribute, out_shape=(wire(OUT_WIDTH), jax.ShapeDtypeStru...  2 us
    pallas_call x1, Pallas kernels, on_device(): pl.pallas_call(deliver, out_shape=(flux_shape, jax.ShapeDtypeStruct((BACK...  1.72 us

profile of v7, /device:TPU:1, one launch (start us, length us, event | category | flops | bytes accessed | tf_op | source)
XLA Modules:
  0.0 53.1 jit_solution(12859140094398111639)
XLA Ops:
  0.6 2.0 %shard_map.86 = (bf16[128,2,1664]{2,1,0:T(2,128)(2,1)S(1)}, f32[16,256]{1,0:T(8,128)S(1)}, s32[16,256]{1,0:T(8,128)S(1)}) custom-call(s32[16]{0:T(128)} %src_hbm.1, s32[16]{0:T(128)} %bitcast.5, s32[16]{0:T(128)} %sea_hbm.1, bf16[16,8,256]{2,1,0:T(8,128)(2,1)} %sky_hbm.1, bf16[16,256,256]{2,1,0:T(8,128)(2,1)} %weights.1, f32[16,256]{1,0:T(8,128)} %sst_hbm.1, ...), custom_call_target="tpu_custom_call" | custom-call | tf_op jit(solution)/shard_map/pallas_call | solution.py:209
  2.6 0.0 copy-start
  2.6 0.0 copy-start.1
  2.7 0.0 copy-start.2
  2.7 28.5 %all_to_all.10.arrived = bf16[128,2,1664]{2,1,0:T(2,128)(2,1)S(1)} all-to-all(bf16[128,2,1664]{2,1,0:T(2,128)(2,1)S(1)} %get-tuple-element.9), channel_id=1, replica_groups=mesh['gx'=16,'gy'=8] {'gx','gy'}, dimensions={0} | all-to-all | bytes 1703936 | tf_op jit(solution)/shard_map/all_to_all | solution.py:204
  31.2 0.8 %shard_map.87 = (f32[16,4,256]{2,1,0:T(4,128)S(1)}, bf16[128,2,1280]{2,1,0:T(2,128)(2,1)S(1)}) custom-call(bf16[128,2,1664]{2,1,0:T(2,128)(2,1)S(1)} %all_to_all.10.arrived, f32[16,256]{1,0:T(8,128)S(1)} %get-tuple-element.10.sst, s32[16,256]{1,0:T(8,128)S(1)} %get-tuple-element.11.marine), custom_call_target="tpu_custom_call" | custom-call | tf_op jit(solution)/shard_map/pallas_call | solution.py:232
  32.0 19.3 %all_to_all.11.returned = bf16[128,2,1280]{2,1,0:T(2,128)(2,1)S(1)} all-to-all(bf16[128,2,1280]{2,1,0:T(2,128)(2,1)S(1)} %get-tuple-element.12), channel_id=1, replica_groups=mesh['gx'=16,'gy'=8] {'gx','gy'}, dimensions={0} | all-to-all | bytes 1310720 | tf_op jit(solution)/shard_map/all_to_all | solution.py:204
  51.4 0.0 copy-done
  51.4 0.0 copy-done.1
  51.4 0.0 copy-done.2
  51.4 1.7 %shard_map.88 = (f32[16,4,256]{2,1,0:T(4,128)}, f32[5,16,256]{2,1,0:T(8,128)}) custom-call(s32[1,16]{1,0:T(1,128)S(1)} %bitcast.4, s32[1,16]{1,0:T(1,128)S(1)} %bitcast.6, bf16[128,2,1280]{2,1,0:T(2,128)(2,1)S(1)} %all_to_all.11.returned, bf16[16,256,256]{2,1,0:T(8,128)(2,1)S(1)} %copy-done, f32[16,4,256]{2,1,0:T(4,128)S(1)} %get-tuple-element.13.fluxes), custom_call_target="tpu_custom_call" | custom-call | tf_op jit(solution)/shard_map/pallas_call | solution.py:239
Async XLA Ops:
  2.6 48.7 %copy-start = (bf16[16,256,256]{2,1,0:T(8,128)(2,1)S(1)}, bf16[16,256,256]{2,1,0:T(8,128)(2,1)}, u32[]{:S(2)}) copy-start(bf16[16,256,256]{2,1,0:T(8,128)(2,1)} %weights.1) | copy-start | bytes 6291460
  2.6 48.7 %copy-start.1 = (s32[16]{0:T(128)S(1)}, s32[16]{0:T(128)}, u32[]{:S(2)}) copy-start(s32[16]{0:T(128)} %src_hbm.1) | copy-start | bytes 196
  2.7 48.7 %copy-start.2 = (s32[16,1]{0,1:T(1,128)S(1)}, s32[16,1]{0,1:T(1,128)}, u32[]{:S(2)}) copy-start(s32[16,1]{0,1:T(1,128)} %param.10) | copy-start | bytes 196

commit v8 on v7

--- a/solution.py
+++ b/solution.py
@@ -16,6 +16,7 @@
 LANES = 128
 SLOTS = 2
 STRIP = 16
+STRIDE = 37
 OUT_WIDTH = SENT * CELLS + LANES
 BACK_WIDTH = BACK * CELLS
 BF = jnp.bfloat16
@@ -25,6 +26,10 @@
 
 def iota(shape, dim):
     return lax.broadcasted_iota(jnp.int32, shape, dim)
+
+
+def block_of(device, devices):
+    return lax.rem(device * pow(STRIDE, -1, devices), devices)
 
 
 def to_column(row):
@@ -58,14 +63,14 @@
     left, right = pl.ds(0, LANES), pl.ds(LANES, LANES)
     every = pl.ds(0, PAIRS)
     fetch("upper", weights_hbm.at[every, left, left], blocks.at[0])
-    fetch("lower", weights_hbm.at[every, right, right], blocks.at[1])
-    fetch("top", weights_hbm.at[every, pl.ds(0, STRIP), right], top)
     fetch("middle", weights_hbm.at[every, pl.ds(LANES - STRIP, 2 * STRIP)], middle)
     fetch("bottom", weights_hbm.at[every, pl.ds(CELLS - STRIP, STRIP), left], bottom)
     fetch("owner", owner_hbm, owner)
     fetch("sea", sea_hbm, sea)
     fetch("src", src_hbm, src)
     fetch("sky", sky_hbm, sky)
+    fetch("lower", weights_hbm.at[every, right, right], blocks.at[1])
+    fetch("top", weights_hbm.at[every, pl.ds(0, STRIP), right], top)
     fetch("sst", sst_hbm, sst)
     fetch("marine", marine_hbm, marine)
     out[...] = jnp.zeros_like(out)
@@ -87,22 +92,18 @@
     fits = (mine == row) & ((wanted % SLOTS).astype(F32) == to_row(rank))
     chosen = jnp.where(fits, 1.0, 0.0).astype(BF)
     label = tiles.astype(F32) + 1.0
-    for name in ("src", "sky", "top", "middle", "bottom", "upper", "lower"):
-        copies[name].wait()
     gap = jnp.zeros((LANES - 2 * STRIP, LANES), BF)
-    for p in range(PAIRS):
-        upper = jnp.concatenate([top[p], gap, middle[p, :STRIP, LANES:]], axis=0)
-        lower = jnp.concatenate([middle[p, STRIP:, :LANES], gap, bottom[p]], axis=0)
-        weights = jnp.concatenate(
-            [
-                jnp.concatenate([blocks[0, p], upper], axis=1),
-                jnp.concatenate([lower, blocks[1, p]], axis=1),
-            ],
-            axis=0,
-        )
-        term = jnp.dot(sky[src[p]], weights, preferred_element_type=F32)
-        for h in range(2):
-            scratch[h, p * FIELDS : (p + 1) * FIELDS, :] = term[:, h * LANES : (h + 1) * LANES]
+    for h, needed in enumerate((("src", "sky", "upper", "middle", "bottom"), ("lower", "top"))):
+        for name in needed:
+            copies[name].wait()
+        for p in range(PAIRS):
+            if h == 0:
+                parts = [blocks[0, p], middle[p, STRIP:, :LANES], gap, bottom[p]]
+            else:
+                parts = [top[p], gap, middle[p, :STRIP, LANES:], blocks[1, p]]
+            scratch[h, p * FIELDS : (p + 1) * FIELDS, :] = jnp.dot(
+                sky[src[p]], jnp.concatenate(parts, axis=0), preferred_element_type=F32
+            )
 
     def field(f):
         parts = [scratch[h, pl.ds(f, PAIRS, stride=FIELDS), :] for h in range(2)]
@@ -115,7 +116,7 @@
     filled = jnp.dot(chosen, jnp.concatenate(sent, axis=1), preferred_element_type=F32)
     filled = filled.astype(BF).reshape(PAIRS, SLOTS, OUT_WIDTH)
     for p in range(PAIRS):
-        out[owner[p]] = filled[p]
+        out[block_of(owner[p], out.shape[0])] = filled[p]
     copies["sst"].wait()
     copies["marine"].wait()
 
@@ -159,7 +160,7 @@
     values[...] = jnp.zeros_like(values)
     for p in range(PAIRS):
         second = functools.reduce(jnp.logical_or, [owner[q] == owner[p] for q in range(p)], False)
-        slots = returned[owner[p]].astype(F32)
+        slots = returned[block_of(owner[p], returned.shape[0])].astype(F32)
         slot = jnp.where(second, slots[1:], slots[:1])
         for f in range(BACK):
             for h in range(2):
@@ -201,7 +202,15 @@
         return jax.ShapeDtypeStruct((devices, SLOTS, width), BF)
 
     def swap(x):
-        return lax.all_to_all(x, ("gx", "gy"), split_axis=0, concat_axis=0, tiled=True)
+        order = [STRIDE * j % devices for j in range(devices)]
+        return lax.all_to_all(
+            x,
+            ("gx", "gy"),
+            split_axis=0,
+            concat_axis=0,
+            axis_index_groups=[order],
+            tiled=True,
+        )
 
     def stay(*arrays):
         return tuple(pltpu.with_memory_space_constraint(x, pltpu.HBM) for x in arrays)

time: 53.3 us -> 53.4 us (level)
  no operation moved by 1% of the time
where the time goes in v8:
time: 53.4 us; the launch traced here: 53.2 us
  blocking collectives  47.9 us (90%)
  Pallas kernels  4.66 us (9%)
  between operations  0.68 us (1%)
    all_to_all x2, blocking collectives, swap(): lax.all_to_all(x, ('gx', 'gy'), split_axis=0, concat_axis=0, axis_index_g...  47.9 us
    pallas_call x1, Pallas kernels, on_device(): pl.pallas_call(contribute, out_shape=(wire(OUT_WIDTH), jax.ShapeDtypeStru...  1.93 us
    pallas_call x1, Pallas kernels, on_device(): pl.pallas_call(deliver, out_shape=(flux_shape, jax.ShapeDtypeStruct((BACK...  1.93 us

profile of v8, /device:TPU:1, one launch (start us, length us, event | category | flops | bytes accessed | tf_op | source)
XLA Modules:
  0.0 53.2 jit_solution(8021480625404657873)
XLA Ops:
  0.6 1.9 %shard_map.86 = (bf16[128,2,1664]{2,1,0:T(2,128)(2,1)S(1)}, f32[16,256]{1,0:T(8,128)S(1)}, s32[16,256]{1,0:T(8,128)S(1)}) custom-call(s32[16]{0:T(128)} %src_hbm.1, s32[16]{0:T(128)} %bitcast.5, s32[16]{0:T(128)} %sea_hbm.1, bf16[16,8,256]{2,1,0:T(8,128)(2,1)} %sky_hbm.1, bf16[16,256,256]{2,1,0:T(8,128)(2,1)} %weights.1, f32[16,256]{1,0:T(8,128)} %sst_hbm.1, ...), custom_call_target="tpu_custom_call" | custom-call | tf_op jit(solution)/shard_map/pallas_call | solution.py:218
  2.6 0.0 copy-start
  2.6 0.0 copy-start.1
  2.6 0.0 copy-start.2
  2.6 28.8 %all_to_all.10.arrived = bf16[128,2,1664]{2,1,0:T(2,128)(2,1)S(1)} all-to-all(bf16[128,2,1664]{2,1,0:T(2,128)(2,1)S(1)} %get-tuple-element.9), channel_id=1, replica_groups={{0,37,74,111,20,57,94,3,40,77,114,23,60,97,6,43,80,117,26,63,100,9,46,8..., dimensions={0} | all-to-all | bytes 1703936 | tf_op jit(solution)/shard_map/all_to_all | solution.py:206
  31.4 0.8 %shard_map.87 = (f32[16,4,256]{2,1,0:T(4,128)S(1)}, bf16[128,2,1280]{2,1,0:T(2,128)(2,1)S(1)}) custom-call(bf16[128,2,1664]{2,1,0:T(2,128)(2,1)S(1)} %all_to_all.10.arrived, f32[16,256]{1,0:T(8,128)S(1)} %get-tuple-element.10.sst, s32[16,256]{1,0:T(8,128)S(1)} %get-tuple-element.11.marine), custom_call_target="tpu_custom_call" | custom-call | tf_op jit(solution)/shard_map/pallas_call | solution.py:241
  32.2 19.0 %all_to_all.11.returned = bf16[128,2,1280]{2,1,0:T(2,128)(2,1)S(1)} all-to-all(bf16[128,2,1280]{2,1,0:T(2,128)(2,1)S(1)} %get-tuple-element.12), channel_id=1, replica_groups={{0,37,74,111,20,57,94,3,40,77,114,23,60,97,6,43,80,117,26,63,100,9,46,8..., dimensions={0} | all-to-all | bytes 1310720 | tf_op jit(solution)/shard_map/all_to_all | solution.py:206
  51.3 0.0 copy-done
  51.3 0.0 copy-done.1
  51.3 0.0 copy-done.2
  51.3 1.9 %shard_map.88 = (f32[16,4,256]{2,1,0:T(4,128)}, f32[5,16,256]{2,1,0:T(8,128)}) custom-call(s32[1,16]{1,0:T(1,128)S(1)} %bitcast.4, s32[1,16]{1,0:T(1,128)S(1)} %bitcast.6, bf16[128,2,1280]{2,1,0:T(2,128)(2,1)S(1)} %all_to_all.11.returned, bf16[16,256,256]{2,1,0:T(8,128)(2,1)S(1)} %copy-done, f32[16,4,256]{2,1,0:T(4,128)S(1)} %get-tuple-element.13.fluxes), custom_call_target="tpu_custom_call" | custom-call | tf_op jit(solution)/shard_map/pallas_call | solution.py:248
Async XLA Ops:
  2.6 48.7 %copy-start = (bf16[16,256,256]{2,1,0:T(8,128)(2,1)S(1)}, bf16[16,256,256]{2,1,0:T(8,128)(2,1)}, u32[]{:S(2)}) copy-start(bf16[16,256,256]{2,1,0:T(8,128)(2,1)} %weights.1) | copy-start | bytes 6291460
  2.6 48.7 %copy-start.1 = (s32[16]{0:T(128)S(1)}, s32[16]{0:T(128)}, u32[]{:S(2)}) copy-start(s32[16]{0:T(128)} %src_hbm.1) | copy-start | bytes 196
  2.6 48.7 %copy-start.2 = (s32[16,1]{0,1:T(1,128)S(1)}, s32[16,1]{0,1:T(1,128)}, u32[]{:S(2)}) copy-start(s32[16,1]{0,1:T(1,128)} %param.10) | copy-start | bytes 196

commit v9 on v8

--- a/solution.py
+++ b/solution.py
@@ -29,7 +29,7 @@
 
 
 def block_of(device, devices):
-    return lax.rem(device * pow(STRIDE, -1, devices), devices)
+    return (device * pow(STRIDE, -1, devices)) & (devices - 1)
 
 
 def to_column(row):

time: 53.4 us -> 53.2 us (level)
  no operation moved by 1% of the time
where the time goes in v9:
time: 53.2 us; the launch traced here: 53 us
  blocking collectives  47.9 us (90%)
  Pallas kernels  4.45 us (8%)
  between operations  0.68 us (1%)
    all_to_all x2, blocking collectives, swap(): lax.all_to_all(x, ('gx', 'gy'), split_axis=0, concat_axis=0, axis_index_g...  47.9 us
    pallas_call x1, Pallas kernels, on_device(): pl.pallas_call(contribute, out_shape=(wire(OUT_WIDTH), jax.ShapeDtypeStru...  1.93 us
    pallas_call x1, Pallas kernels, on_device(): pl.pallas_call(deliver, out_shape=(flux_shape, jax.ShapeDtypeStruct((BACK...  1.72 us

profile of v9, /device:TPU:1, one launch (start us, length us, event | category | flops | bytes accessed | tf_op | source)
XLA Modules:
  0.0 53.0 jit_solution(16467778558259414908)
XLA Ops:
  0.6 1.9 %shard_map.86 = (bf16[128,2,1664]{2,1,0:T(2,128)(2,1)S(1)}, f32[16,256]{1,0:T(8,128)S(1)}, s32[16,256]{1,0:T(8,128)S(1)}) custom-call(s32[16]{0:T(128)} %src_hbm.1, s32[16]{0:T(128)} %bitcast.5, s32[16]{0:T(128)} %sea_hbm.1, bf16[16,8,256]{2,1,0:T(8,128)(2,1)} %sky_hbm.1, bf16[16,256,256]{2,1,0:T(8,128)(2,1)} %weights.1, f32[16,256]{1,0:T(8,128)} %sst_hbm.1, ...), custom_call_target="tpu_custom_call" | custom-call | tf_op jit(solution)/shard_map/pallas_call | solution.py:218
  2.6 0.0 copy-start
  2.6 0.0 copy-start.1
  2.6 0.0 copy-start.2
  2.6 28.8 %all_to_all.10.arrived = bf16[128,2,1664]{2,1,0:T(2,128)(2,1)S(1)} all-to-all(bf16[128,2,1664]{2,1,0:T(2,128)(2,1)S(1)} %get-tuple-element.9), channel_id=1, replica_groups={{0,37,74,111,20,57,94,3,40,77,114,23,60,97,6,43,80,117,26,63,100,9,46,8..., dimensions={0} | all-to-all | bytes 1703936 | tf_op jit(solution)/shard_map/all_to_all | solution.py:206
  31.4 0.8 %shard_map.87 = (f32[16,4,256]{2,1,0:T(4,128)S(1)}, bf16[128,2,1280]{2,1,0:T(2,128)(2,1)S(1)}) custom-call(bf16[128,2,1664]{2,1,0:T(2,128)(2,1)S(1)} %all_to_all.10.arrived, f32[16,256]{1,0:T(8,128)S(1)} %get-tuple-element.10.sst, s32[16,256]{1,0:T(8,128)S(1)} %get-tuple-element.11.marine), custom_call_target="tpu_custom_call" | custom-call | tf_op jit(solution)/shard_map/pallas_call | solution.py:241
  32.2 19.0 %all_to_all.11.returned = bf16[128,2,1280]{2,1,0:T(2,128)(2,1)S(1)} all-to-all(bf16[128,2,1280]{2,1,0:T(2,128)(2,1)S(1)} %get-tuple-element.12), channel_id=1, replica_groups={{0,37,74,111,20,57,94,3,40,77,114,23,60,97,6,43,80,117,26,63,100,9,46,8..., dimensions={0} | all-to-all | bytes 1310720 | tf_op jit(solution)/shard_map/all_to_all | solution.py:206
  51.3 0.0 copy-done
  51.3 0.0 copy-done.1
  51.3 0.0 copy-done.2
  51.3 1.7 %shard_map.88 = (f32[16,4,256]{2,1,0:T(4,128)}, f32[5,16,256]{2,1,0:T(8,128)}) custom-call(s32[1,16]{1,0:T(1,128)S(1)} %bitcast.4, s32[1,16]{1,0:T(1,128)S(1)} %bitcast.6, bf16[128,2,1280]{2,1,0:T(2,128)(2,1)S(1)} %all_to_all.11.returned, bf16[16,256,256]{2,1,0:T(8,128)(2,1)S(1)} %copy-done, f32[16,4,256]{2,1,0:T(4,128)S(1)} %get-tuple-element.13.fluxes), custom_call_target="tpu_custom_call" | custom-call | tf_op jit(solution)/shard_map/pallas_call | solution.py:248
Async XLA Ops:
  2.6 48.7 %copy-start = (bf16[16,256,256]{2,1,0:T(8,128)(2,1)S(1)}, bf16[16,256,256]{2,1,0:T(8,128)(2,1)}, u32[]{:S(2)}) copy-start(bf16[16,256,256]{2,1,0:T(8,128)(2,1)} %weights.1) | copy-start | bytes 6291460
  2.6 48.7 %copy-start.1 = (s32[16]{0:T(128)S(1)}, s32[16]{0:T(128)}, u32[]{:S(2)}) copy-start(s32[16]{0:T(128)} %src_hbm.1) | copy-start | bytes 196
  2.6 48.7 %copy-start.2 = (s32[16,1]{0,1:T(1,128)S(1)}, s32[16,1]{0,1:T(1,128)}, u32[]{:S(2)}) copy-start(s32[16,1]{0,1:T(1,128)} %param.10) | copy-start | bytes 196

commit v10 on v9

--- a/solution.py
+++ b/solution.py
@@ -16,7 +16,6 @@
 LANES = 128
 SLOTS = 2
 STRIP = 16
-STRIDE = 37
 OUT_WIDTH = SENT * CELLS + LANES
 BACK_WIDTH = BACK * CELLS
 BF = jnp.bfloat16
@@ -28,8 +27,14 @@
     return lax.broadcasted_iota(jnp.int32, shape, dim)
 
 
-def block_of(device, devices):
-    return (device * pow(STRIDE, -1, devices)) & (devices - 1)
+def key_of(device):
+    return ((device >> 5) + ((device >> 3) & 3) + ((device >> 1) & 3)) * 128 + device
+
+
+def places_of(column, devices):
+    others = key_of(iota((PAIRS, devices), 1))
+    ahead = jnp.where(others < key_of(column.astype(jnp.int32)), 1.0, 0.0)
+    return to_row(jnp.sum(ahead, axis=1, keepdims=True)).astype(jnp.int32)
 
 
 def to_column(row):
@@ -42,16 +47,8 @@
     return jnp.sum(jnp.where(same, column, 0.0), axis=0, keepdims=True)
 
 
-def slot_column(target):
-    row = target.astype(F32)
-    column = to_column(row)
-    later, other = iota((PAIRS, PAIRS), 0), iota((PAIRS, PAIRS), 1)
-    earlier = jnp.where((column == row) & (other < later), 1.0, 0.0)
-    return SLOTS * column + jnp.sum(earlier, axis=1, keepdims=True)
-
-
 def contribute(
-    src_hbm, owner_hbm, sea_hbm, sky_hbm, weights_hbm, sst_hbm, marine_hbm, out, sst, marine,
+    src_hbm, owner_hbm, sea_hbm, sky_hbm, weights_hbm, sst_hbm, marine_hbm, out, sst, marine, places,
     src, owner, sea, sky, blocks, top, middle, bottom, scratch, sems,
 ):
     copies = {}
@@ -92,6 +89,9 @@
     fits = (mine == row) & ((wanted % SLOTS).astype(F32) == to_row(rank))
     chosen = jnp.where(fits, 1.0, 0.0).astype(BF)
     label = tiles.astype(F32) + 1.0
+    row_of_places = places_of(column, out.shape[0])
+    places[...] = row_of_places
+    place = [row_of_places[0, p] for p in range(PAIRS)]
     gap = jnp.zeros((LANES - 2 * STRIP, LANES), BF)
     for h, needed in enumerate((("src", "sky", "upper", "middle", "bottom"), ("lower", "top"))):
         for name in needed:
@@ -116,7 +116,7 @@
     filled = jnp.dot(chosen, jnp.concatenate(sent, axis=1), preferred_element_type=F32)
     filled = filled.astype(BF).reshape(PAIRS, SLOTS, OUT_WIDTH)
     for p in range(PAIRS):
-        out[block_of(owner[p], out.shape[0])] = filled[p]
+        out[place[p]] = filled[p]
     copies["sst"].wait()
     copies["marine"].wait()
 
@@ -150,17 +150,17 @@
 
 
 def deliver(
-    src_row, target, returned, weights, fluxes, fluxes_hbm, out, values, terms, sums, sem
+    src_row, places, returned, weights, fluxes, fluxes_hbm, out, values, terms, sums, sem
 ):
     copy = pltpu.make_async_copy(fluxes, fluxes_hbm, sem)
     copy.start()
-    owners, sources = target[...], src_row[...]
-    owner = [owners[0, p] for p in range(PAIRS)]
+    row_of_places, sources = places[...], src_row[...]
+    place = [row_of_places[0, p] for p in range(PAIRS)]
     src = [sources[0, p] for p in range(PAIRS)]
     values[...] = jnp.zeros_like(values)
     for p in range(PAIRS):
-        second = functools.reduce(jnp.logical_or, [owner[q] == owner[p] for q in range(p)], False)
-        slots = returned[block_of(owner[p], returned.shape[0])].astype(F32)
+        second = functools.reduce(jnp.logical_or, [place[q] == place[p] for q in range(p)], False)
+        slots = returned[place[p]].astype(F32)
         slot = jnp.where(second, slots[1:], slots[:1])
         for f in range(BACK):
             for h in range(2):
@@ -195,14 +195,13 @@
 def on_device(sky, weights, sky_block, target_device, sea_block, sst, marine):
     devices = lax.axis_size(("gx", "gy"))
     params = pltpu.CompilerParams(vmem_limit_bytes=VMEM_LIMIT)
-    target = target_device.reshape(1, PAIRS)
     flux_shape = jax.ShapeDtypeStruct((TILES, 4, CELLS), F32)
 
     def wire(width):
         return jax.ShapeDtypeStruct((devices, SLOTS, width), BF)
 
     def swap(x):
-        order = [STRIDE * j % devices for j in range(devices)]
+        order = sorted(range(devices), key=key_of)
         return lax.all_to_all(
             x,
             ("gx", "gy"),
@@ -215,15 +214,16 @@
     def stay(*arrays):
         return tuple(pltpu.with_memory_space_constraint(x, pltpu.HBM) for x in arrays)
 
-    outgoing, sst, marine = pl.pallas_call(
+    outgoing, sst, marine, places = pl.pallas_call(
         contribute,
         out_shape=(
             wire(OUT_WIDTH),
             jax.ShapeDtypeStruct((TILES, CELLS), F32),
             jax.ShapeDtypeStruct((TILES, CELLS), jnp.int32),
+            jax.ShapeDtypeStruct((1, PAIRS), jnp.int32),
         ),
         in_specs=[HBM] * 7,
-        out_specs=(VMEM,) * 3,
+        out_specs=(VMEM,) * 4,
         scratch_shapes=[
             pltpu.SMEM((PAIRS,), jnp.int32),
             pltpu.SMEM((PAIRS,), jnp.int32),
@@ -257,7 +257,7 @@
             pltpu.SemaphoreType.DMA,
         ],
         compiler_params=params,
-    )(sky_block.reshape(1, PAIRS), target, swap(back), weights, fluxes)
+    )(sky_block.reshape(1, PAIRS), places, swap(back), weights, fluxes)
     return fluxes, jnp.transpose(atm_back, (1, 0, 2))
 
 

time: 53.2 us -> 52.9 us (level)
  no operation moved by 1% of the time
where the time goes in v10:
time: 52.9 us; the launch traced here: 52.7 us
  blocking collectives  47.6 us (90%)
  Pallas kernels  4.45 us (8%)
  between operations  0.66 us (1%)
    all_to_all x2, blocking collectives, swap(): lax.all_to_all(x, ('gx', 'gy'), split_axis=0, concat_axis=0, axis_index_g...  47.6 us
    pallas_call x1, Pallas kernels, on_device(): pl.pallas_call(contribute, out_shape=(wire(OUT_WIDTH), jax.ShapeDtypeStru...  1.93 us
    pallas_call x1, Pallas kernels, on_device(): pl.pallas_call(deliver, out_shape=(flux_shape, jax.ShapeDtypeStruct((BACK...  1.72 us

profile of v10, /device:TPU:1, one launch (start us, length us, event | category | flops | bytes accessed | tf_op | source)
XLA Modules:
  0.0 52.7 jit_solution(11011753549144527124)
XLA Ops:
  0.6 1.9 %shard_map.86 = (bf16[128,2,1664]{2,1,0:T(2,128)(2,1)S(1)}, f32[16,256]{1,0:T(8,128)S(1)}, s32[16,256]{1,0:T(8,128)S(1)}, s32[1,16]{1,0:T(1,128)S(1)}) custom-call(s32[16]{0:T(128)} %src_hbm.1, s32[16]{0:T(128)} %bitcast.4, s32[16]{0:T(128)} %sea_hbm.1, bf16[16,8,256]{2,1,0:T(8,128)(2,1)} %sky_hbm.1, bf16[16,256,256]{2,1,0:T(8,128)(2,1)} %weights.1, ...), custom_call_target="tpu_custom_call" | custom-call | tf_op jit(solution)/shard_map/pallas_call | solution.py:217
  2.6 0.0 copy-start
  2.6 0.0 copy-start.1
  2.6 28.5 %all_to_all.10.arrived = bf16[128,2,1664]{2,1,0:T(2,128)(2,1)S(1)} all-to-all(bf16[128,2,1664]{2,1,0:T(2,128)(2,1)S(1)} %get-tuple-element.11), channel_id=1, replica_groups={{0,1,2,3,8,9,32,33,4,5,10,11,16,17,34,35,40,41,64,65,6,7,12,13,18,19,24..., dimensions={0} | all-to-all | bytes 1703936 | tf_op jit(solution)/shard_map/all_to_all | solution.py:205
  31.1 0.8 %shard_map.87 = (f32[16,4,256]{2,1,0:T(4,128)S(1)}, bf16[128,2,1280]{2,1,0:T(2,128)(2,1)S(1)}) custom-call(bf16[128,2,1664]{2,1,0:T(2,128)(2,1)S(1)} %all_to_all.10.arrived, f32[16,256]{1,0:T(8,128)S(1)} %get-tuple-element.12.sst, s32[16,256]{1,0:T(8,128)S(1)} %get-tuple-element.13.marine), custom_call_target="tpu_custom_call" | custom-call | tf_op jit(solution)/shard_map/pallas_call | solution.py:241
  31.9 19.1 %all_to_all.11.returned = bf16[128,2,1280]{2,1,0:T(2,128)(2,1)S(1)} all-to-all(bf16[128,2,1280]{2,1,0:T(2,128)(2,1)S(1)} %get-tuple-element.14), channel_id=1, replica_groups={{0,1,2,3,8,9,32,33,4,5,10,11,16,17,34,35,40,41,64,65,6,7,12,13,18,19,24..., dimensions={0} | all-to-all | bytes 1310720 | tf_op jit(solution)/shard_map/all_to_all | solution.py:205
  51.0 0.0 copy-done
  51.0 0.0 copy-done.1
  51.0 1.7 %shard_map.88 = (f32[16,4,256]{2,1,0:T(4,128)}, f32[5,16,256]{2,1,0:T(8,128)}) custom-call(s32[1,16]{1,0:T(1,128)S(1)} %bitcast.3, s32[1,16]{1,0:T(1,128)S(1)} %get-tuple-element.10.places, bf16[128,2,1280]{2,1,0:T(2,128)(2,1)S(1)} %all_to_all.11.returned, bf16[16,256,256]{2,1,0:T(8,128)(2,1)S(1)} %copy-done, f32[16,4,256]{2,1,0:T(4,128)S(1)} %get-tuple-element.15.fluxes), custom_call_target="tpu_custom_call" | custom-call | tf_op jit(solution)/shard_map/pallas_call | solution.py:248
Async XLA Ops:
  2.6 48.5 %copy-start = (bf16[16,256,256]{2,1,0:T(8,128)(2,1)S(1)}, bf16[16,256,256]{2,1,0:T(8,128)(2,1)}, u32[]{:S(2)}) copy-start(bf16[16,256,256]{2,1,0:T(8,128)(2,1)} %weights.1) | copy-start | bytes 6291460
  2.6 48.4 %copy-start.1 = (s32[16]{0:T(128)S(1)}, s32[16]{0:T(128)}, u32[]{:S(2)}) copy-start(s32[16]{0:T(128)} %src_hbm.1) | copy-start | bytes 196

commit v11 on v10

--- a/solution.py
+++ b/solution.py
@@ -49,7 +49,7 @@
 
 def contribute(
     src_hbm, owner_hbm, sea_hbm, sky_hbm, weights_hbm, sst_hbm, marine_hbm, out, sst, marine, places,
-    src, owner, sea, sky, blocks, top, middle, bottom, scratch, sems,
+    src, owner, sea, sky, blocks, top, bottom, scratch, sems,
 ):
     copies = {}
 
@@ -59,14 +59,17 @@
 
     left, right = pl.ds(0, LANES), pl.ds(LANES, LANES)
     every = pl.ds(0, PAIRS)
-    fetch("upper", weights_hbm.at[every, left, left], blocks.at[0])
-    fetch("middle", weights_hbm.at[every, pl.ds(LANES - STRIP, 2 * STRIP)], middle)
+    fetch("upper", weights_hbm.at[every, pl.ds(0, LANES + STRIP), left], blocks.at[0])
     fetch("bottom", weights_hbm.at[every, pl.ds(CELLS - STRIP, STRIP), left], bottom)
     fetch("owner", owner_hbm, owner)
     fetch("sea", sea_hbm, sea)
     fetch("src", src_hbm, src)
     fetch("sky", sky_hbm, sky)
-    fetch("lower", weights_hbm.at[every, right, right], blocks.at[1])
+    fetch(
+        "lower",
+        weights_hbm.at[every, pl.ds(LANES - STRIP, LANES + STRIP), right],
+        blocks.at[1],
+    )
     fetch("top", weights_hbm.at[every, pl.ds(0, STRIP), right], top)
     fetch("sst", sst_hbm, sst)
     fetch("marine", marine_hbm, marine)
@@ -93,14 +96,14 @@
     places[...] = row_of_places
     place = [row_of_places[0, p] for p in range(PAIRS)]
     gap = jnp.zeros((LANES - 2 * STRIP, LANES), BF)
-    for h, needed in enumerate((("src", "sky", "upper", "middle", "bottom"), ("lower", "top"))):
+    for h, needed in enumerate((("src", "sky", "upper", "bottom"), ("lower", "top"))):
         for name in needed:
             copies[name].wait()
         for p in range(PAIRS):
             if h == 0:
-                parts = [blocks[0, p], middle[p, STRIP:, :LANES], gap, bottom[p]]
+                parts = [blocks[0, p], gap, bottom[p]]
             else:
-                parts = [top[p], gap, middle[p, :STRIP, LANES:], blocks[1, p]]
+                parts = [top[p], gap, blocks[1, p]]
             scratch[h, p * FIELDS : (p + 1) * FIELDS, :] = jnp.dot(
                 sky[src[p]], jnp.concatenate(parts, axis=0), preferred_element_type=F32
             )
@@ -229,12 +232,11 @@
             pltpu.SMEM((PAIRS,), jnp.int32),
             pltpu.SMEM((PAIRS,), jnp.int32),
             pltpu.VMEM((TILES, FIELDS, CELLS), BF),
-            pltpu.VMEM((2, PAIRS, LANES, LANES), BF),
+            pltpu.VMEM((2, PAIRS, LANES + STRIP, LANES), BF),
             pltpu.VMEM((PAIRS, STRIP, LANES), BF),
-            pltpu.VMEM((PAIRS, 2 * STRIP, CELLS), BF),
             pltpu.VMEM((PAIRS, STRIP, LANES), BF),
             pltpu.VMEM((2, PAIRS * FIELDS, LANES), F32),
-            pltpu.SemaphoreType.DMA((11,)),
+            pltpu.SemaphoreType.DMA((10,)),
         ],
         compiler_params=params,
     )(*stay(sky_block, target_device.reshape(PAIRS), sea_block, sky, weights, sst, marine))

time: 52.9 us -> 52.9 us (level)
  no operation moved by 1% of the time
where the time goes in v11:
time: 52.9 us; the launch traced here: 52.7 us
  blocking collectives  47.6 us (90%)
  Pallas kernels  4.43 us (8%)
  between operations  0.66 us (1%)
    all_to_all x2, blocking collectives, swap(): lax.all_to_all(x, ('gx', 'gy'), split_axis=0, concat_axis=0, axis_index_g...  47.6 us
    pallas_call x1, Pallas kernels, on_device(): pl.pallas_call(contribute, out_shape=(wire(OUT_WIDTH), jax.ShapeDtypeStru...  1.91 us
    pallas_call x1, Pallas kernels, on_device(): pl.pallas_call(deliver, out_shape=(flux_shape, jax.ShapeDtypeStruct((BACK...  1.72 us

profile of v11, /device:TPU:1, one launch (start us, length us, event | category | flops | bytes accessed | tf_op | source)
XLA Modules:
  0.0 52.7 jit_solution(14416289675789034871)
XLA Ops:
  0.6 1.9 %shard_map.86 = (bf16[128,2,1664]{2,1,0:T(2,128)(2,1)S(1)}, f32[16,256]{1,0:T(8,128)S(1)}, s32[16,256]{1,0:T(8,128)S(1)}, s32[1,16]{1,0:T(1,128)S(1)}) custom-call(s32[16]{0:T(128)} %src_hbm.1, s32[16]{0:T(128)} %bitcast.4, s32[16]{0:T(128)} %sea_hbm.1, bf16[16,8,256]{2,1,0:T(8,128)(2,1)} %sky_hbm.1, bf16[16,256,256]{2,1,0:T(8,128)(2,1)} %weights.1, ...), custom_call_target="tpu_custom_call" | custom-call | tf_op jit(solution)/shard_map/pallas_call | solution.py:220
  2.6 0.0 copy-start
  2.6 0.0 copy-start.1
  2.6 28.5 %all_to_all.10.arrived = bf16[128,2,1664]{2,1,0:T(2,128)(2,1)S(1)} all-to-all(bf16[128,2,1664]{2,1,0:T(2,128)(2,1)S(1)} %get-tuple-element.11), channel_id=1, replica_groups={{0,1,2,3,8,9,32,33,4,5,10,11,16,17,34,35,40,41,64,65,6,7,12,13,18,19,24..., dimensions={0} | all-to-all | bytes 1703936 | tf_op jit(solution)/shard_map/all_to_all | solution.py:208
  31.1 0.8 %shard_map.87 = (f32[16,4,256]{2,1,0:T(4,128)S(1)}, bf16[128,2,1280]{2,1,0:T(2,128)(2,1)S(1)}) custom-call(bf16[128,2,1664]{2,1,0:T(2,128)(2,1)S(1)} %all_to_all.10.arrived, f32[16,256]{1,0:T(8,128)S(1)} %get-tuple-element.12.sst, s32[16,256]{1,0:T(8,128)S(1)} %get-tuple-element.13.marine), custom_call_target="tpu_custom_call" | custom-call | tf_op jit(solution)/shard_map/pallas_call | solution.py:243
  31.9 19.1 %all_to_all.11.returned = bf16[128,2,1280]{2,1,0:T(2,128)(2,1)S(1)} all-to-all(bf16[128,2,1280]{2,1,0:T(2,128)(2,1)S(1)} %get-tuple-element.14), channel_id=1, replica_groups={{0,1,2,3,8,9,32,33,4,5,10,11,16,17,34,35,40,41,64,65,6,7,12,13,18,19,24..., dimensions={0} | all-to-all | bytes 1310720 | tf_op jit(solution)/shard_map/all_to_all | solution.py:208
  51.0 0.0 copy-done
  51.0 0.0 copy-done.1
  51.0 1.7 %shard_map.88 = (f32[16,4,256]{2,1,0:T(4,128)}, f32[5,16,256]{2,1,0:T(8,128)}) custom-call(s32[1,16]{1,0:T(1,128)S(1)} %bitcast.3, s32[1,16]{1,0:T(1,128)S(1)} %get-tuple-element.10.places, bf16[128,2,1280]{2,1,0:T(2,128)(2,1)S(1)} %all_to_all.11.returned, bf16[16,256,256]{2,1,0:T(8,128)(2,1)S(1)} %copy-done, f32[16,4,256]{2,1,0:T(4,128)S(1)} %get-tuple-element.15.fluxes), custom_call_target="tpu_custom_call" | custom-call | tf_op jit(solution)/shard_map/pallas_call | solution.py:250
Async XLA Ops:
  2.6 48.5 %copy-start = (bf16[16,256,256]{2,1,0:T(8,128)(2,1)S(1)}, bf16[16,256,256]{2,1,0:T(8,128)(2,1)}, u32[]{:S(2)}) copy-start(bf16[16,256,256]{2,1,0:T(8,128)(2,1)} %weights.1) | copy-start | bytes 6291460
  2.6 48.4 %copy-start.1 = (s32[16]{0:T(128)S(1)}, s32[16]{0:T(128)}, u32[]{:S(2)}) copy-start(s32[16]{0:T(128)} %src_hbm.1) | copy-start | bytes 196

commit v12 on v11

--- a/solution.py
+++ b/solution.py
@@ -49,7 +49,7 @@
 
 def contribute(
     src_hbm, owner_hbm, sea_hbm, sky_hbm, weights_hbm, sst_hbm, marine_hbm, out, sst, marine, places,
-    src, owner, sea, sky, blocks, top, bottom, scratch, sems,
+    src, owner, sea, sky, cells, blocks, top, bottom, scratch, sems,
 ):
     copies = {}
 
@@ -95,17 +95,27 @@
     row_of_places = places_of(column, out.shape[0])
     places[...] = row_of_places
     place = [row_of_places[0, p] for p in range(PAIRS)]
-    gap = jnp.zeros((LANES - 2 * STRIP, LANES), BF)
-    for h, needed in enumerate((("src", "sky", "upper", "bottom"), ("lower", "top"))):
+    for name in ("src", "sky"):
+        copies[name].wait()
+    wide = sky[...].astype(F32).reshape(TILES * FIELDS, CELLS)
+    sides = (wide[:, :LANES], wide[:, LANES:])
+    lane = iota((TILES * FIELDS, LANES), 1)
+    for h in range(2):
+        ends = jnp.where(lane < STRIP, sides[1 - h], pltpu.roll(sides[1 - h], 2 * STRIP, 1))
+        gathered = jnp.concatenate([sides[h], ends], axis=1).astype(BF)
+        cells[h] = gathered.reshape(TILES, FIELDS, CELLS)
+    for h, needed in enumerate((("upper", "bottom"), ("lower", "top"))):
         for name in needed:
             copies[name].wait()
         for p in range(PAIRS):
             if h == 0:
-                parts = [blocks[0, p], gap, bottom[p]]
+                parts = [blocks[0, p], bottom[p]]
             else:
-                parts = [top[p], gap, blocks[1, p]]
+                parts = [blocks[1, p, STRIP:], top[p], blocks[1, p, :STRIP]]
             scratch[h, p * FIELDS : (p + 1) * FIELDS, :] = jnp.dot(
-                sky[src[p]], jnp.concatenate(parts, axis=0), preferred_element_type=F32
+                cells[h, src[p]][:, : LANES + 2 * STRIP],
+                jnp.concatenate(parts, axis=0),
+                preferred_element_type=F32,
             )
 
     def field(f):
@@ -232,6 +242,7 @@
             pltpu.SMEM((PAIRS,), jnp.int32),
             pltpu.SMEM((PAIRS,), jnp.int32),
             pltpu.VMEM((TILES, FIELDS, CELLS), BF),
+            pltpu.VMEM((2, TILES, FIELDS, CELLS), BF),
             pltpu.VMEM((2, PAIRS, LANES + STRIP, LANES), BF),
             pltpu.VMEM((PAIRS, STRIP, LANES), BF),
             pltpu.VMEM((PAIRS, STRIP, LANES), BF),

time: 52.9 us -> 53.1 us (level)
  no operation moved by 1% of the time
where the time goes in v12:
time: 53.1 us; the launch traced here: 52.9 us
  blocking collectives  47.6 us (90%)
  Pallas kernels  4.6 us (9%)
  between operations  0.66 us (1%)
    all_to_all x2, blocking collectives, swap(): lax.all_to_all(x, ('gx', 'gy'), split_axis=0, concat_axis=0, axis_index_g...  47.6 us
    pallas_call x1, Pallas kernels, on_device(): pl.pallas_call(contribute, out_shape=(wire(OUT_WIDTH), jax.ShapeDtypeStru...  2.07 us
    pallas_call x1, Pallas kernels, on_device(): pl.pallas_call(deliver, out_shape=(flux_shape, jax.ShapeDtypeStruct((BACK...  1.72 us

profile of v12, /device:TPU:1, one launch (start us, length us, event | category | flops | bytes accessed | tf_op | source)
XLA Modules:
  0.0 52.9 jit_solution(4342053066985622232)
XLA Ops:
  0.6 2.1 %shard_map.86 = (bf16[128,2,1664]{2,1,0:T(2,128)(2,1)S(1)}, f32[16,256]{1,0:T(8,128)S(1)}, s32[16,256]{1,0:T(8,128)S(1)}, s32[1,16]{1,0:T(1,128)S(1)}) custom-call(s32[16]{0:T(128)} %src_hbm.1, s32[16]{0:T(128)} %bitcast.4, s32[16]{0:T(128)} %sea_hbm.1, bf16[16,8,256]{2,1,0:T(8,128)(2,1)} %sky_hbm.1, bf16[16,256,256]{2,1,0:T(8,128)(2,1)} %weights.1, ...), custom_call_target="tpu_custom_call" | custom-call | tf_op jit(solution)/shard_map/pallas_call | solution.py:230
  2.7 0.0 copy-start
  2.7 0.0 copy-start.1
  2.7 28.5 %all_to_all.10.arrived = bf16[128,2,1664]{2,1,0:T(2,128)(2,1)S(1)} all-to-all(bf16[128,2,1664]{2,1,0:T(2,128)(2,1)S(1)} %get-tuple-element.11), channel_id=1, replica_groups={{0,1,2,3,8,9,32,33,4,5,10,11,16,17,34,35,40,41,64,65,6,7,12,13,18,19,24..., dimensions={0} | all-to-all | bytes 1703936 | tf_op jit(solution)/shard_map/all_to_all | solution.py:218
  31.3 0.8 %shard_map.87 = (f32[16,4,256]{2,1,0:T(4,128)S(1)}, bf16[128,2,1280]{2,1,0:T(2,128)(2,1)S(1)}) custom-call(bf16[128,2,1664]{2,1,0:T(2,128)(2,1)S(1)} %all_to_all.10.arrived, f32[16,256]{1,0:T(8,128)S(1)} %get-tuple-element.12.sst, s32[16,256]{1,0:T(8,128)S(1)} %get-tuple-element.13.marine), custom_call_target="tpu_custom_call" | custom-call | tf_op jit(solution)/shard_map/pallas_call | solution.py:254
  32.1 19.1 %all_to_all.11.returned = bf16[128,2,1280]{2,1,0:T(2,128)(2,1)S(1)} all-to-all(bf16[128,2,1280]{2,1,0:T(2,128)(2,1)S(1)} %get-tuple-element.14), channel_id=1, replica_groups={{0,1,2,3,8,9,32,33,4,5,10,11,16,17,34,35,40,41,64,65,6,7,12,13,18,19,24..., dimensions={0} | all-to-all | bytes 1310720 | tf_op jit(solution)/shard_map/all_to_all | solution.py:218
  51.2 0.0 copy-done
  51.2 0.0 copy-done.1
  51.2 1.7 %shard_map.88 = (f32[16,4,256]{2,1,0:T(4,128)}, f32[5,16,256]{2,1,0:T(8,128)}) custom-call(s32[1,16]{1,0:T(1,128)S(1)} %bitcast.3, s32[1,16]{1,0:T(1,128)S(1)} %get-tuple-element.10.places, bf16[128,2,1280]{2,1,0:T(2,128)(2,1)S(1)} %all_to_all.11.returned, bf16[16,256,256]{2,1,0:T(8,128)(2,1)S(1)} %copy-done, f32[16,4,256]{2,1,0:T(4,128)S(1)} %get-tuple-element.15.fluxes), custom_call_target="tpu_custom_call" | custom-call | tf_op jit(solution)/shard_map/pallas_call | solution.py:261
Async XLA Ops:
  2.7 48.4 %copy-start = (bf16[16,256,256]{2,1,0:T(8,128)(2,1)S(1)}, bf16[16,256,256]{2,1,0:T(8,128)(2,1)}, u32[]{:S(2)}) copy-start(bf16[16,256,256]{2,1,0:T(8,128)(2,1)} %weights.1) | copy-start | bytes 6291460
  2.7 48.4 %copy-start.1 = (s32[16]{0:T(128)S(1)}, s32[16]{0:T(128)}, u32[]{:S(2)}) copy-start(s32[16]{0:T(128)} %src_hbm.1) | copy-start | bytes 196

commit v13 on v11

--- a/solution.py
+++ b/solution.py
@@ -74,8 +74,18 @@
     fetch("sst", sst_hbm, sst)
     fetch("marine", marine_hbm, marine)
     out[...] = jnp.zeros_like(out)
-    copies["owner"].wait()
-    copies["sea"].wait()
+    gap = jnp.zeros((LANES - 2 * STRIP, LANES), BF)
+
+    def product(h, p):
+        parts = [top[p], gap, blocks[1, p]] if h else [blocks[0, p], gap, bottom[p]]
+        scratch[h, p * FIELDS : (p + 1) * FIELDS, :] = jnp.dot(
+            sky[src[p]], jnp.concatenate(parts, axis=0), preferred_element_type=F32
+        )
+
+    for name in ("owner", "sea", "src", "sky", "upper", "bottom"):
+        copies[name].wait()
+    for p in range(PAIRS):
+        product(0, p)
     at = iota((PAIRS, PAIRS), 1)
     row = jnp.zeros((PAIRS, PAIRS), jnp.int32)
     tiles = jnp.zeros((PAIRS, LANES), jnp.int32)
@@ -95,18 +105,10 @@
     row_of_places = places_of(column, out.shape[0])
     places[...] = row_of_places
     place = [row_of_places[0, p] for p in range(PAIRS)]
-    gap = jnp.zeros((LANES - 2 * STRIP, LANES), BF)
-    for h, needed in enumerate((("src", "sky", "upper", "bottom"), ("lower", "top"))):
-        for name in needed:
-            copies[name].wait()
-        for p in range(PAIRS):
-            if h == 0:
-                parts = [blocks[0, p], gap, bottom[p]]
-            else:
-                parts = [top[p], gap, blocks[1, p]]
-            scratch[h, p * FIELDS : (p + 1) * FIELDS, :] = jnp.dot(
-                sky[src[p]], jnp.concatenate(parts, axis=0), preferred_element_type=F32
-            )
+    for name in ("lower", "top"):
+        copies[name].wait()
+    for p in range(PAIRS):
+        product(1, p)
 
     def field(f):
         parts = [scratch[h, pl.ds(f, PAIRS, stride=FIELDS), :] for h in range(2)]

time: 52.9 us -> 52.9 us (level)
  no operation moved by 1% of the time
where the time goes in v13:
time: 52.9 us; the launch traced here: 52.7 us
  blocking collectives  47.6 us (90%)
  Pallas kernels  4.43 us (8%)
  between operations  0.66 us (1%)
    all_to_all x2, blocking collectives, swap(): lax.all_to_all(x, ('gx', 'gy'), split_axis=0, concat_axis=0, axis_index_g...  47.6 us
    pallas_call x1, Pallas kernels, on_device(): pl.pallas_call(contribute, out_shape=(wire(OUT_WIDTH), jax.ShapeDtypeStru...  1.91 us
    pallas_call x1, Pallas kernels, on_device(): pl.pallas_call(deliver, out_shape=(flux_shape, jax.ShapeDtypeStruct((BACK...  1.72 us

profile of v13, /device:TPU:1, one launch (start us, length us, event | category | flops | bytes accessed | tf_op | source)
XLA Modules:
  0.0 52.7 jit_solution(1942076305105756761)
XLA Ops:
  0.6 1.9 %shard_map.86 = (bf16[128,2,1664]{2,1,0:T(2,128)(2,1)S(1)}, f32[16,256]{1,0:T(8,128)S(1)}, s32[16,256]{1,0:T(8,128)S(1)}, s32[1,16]{1,0:T(1,128)S(1)}) custom-call(s32[16]{0:T(128)} %src_hbm.1, s32[16]{0:T(128)} %bitcast.4, s32[16]{0:T(128)} %sea_hbm.1, bf16[16,8,256]{2,1,0:T(8,128)(2,1)} %sky_hbm.1, bf16[16,256,256]{2,1,0:T(8,128)(2,1)} %weights.1, ...), custom_call_target="tpu_custom_call" | custom-call | tf_op jit(solution)/shard_map/pallas_call | solution.py:222
  2.6 0.0 copy-start
  2.6 0.0 copy-start.1
  2.6 28.5 %all_to_all.10.arrived = bf16[128,2,1664]{2,1,0:T(2,128)(2,1)S(1)} all-to-all(bf16[128,2,1664]{2,1,0:T(2,128)(2,1)S(1)} %get-tuple-element.11), channel_id=1, replica_groups={{0,1,2,3,8,9,32,33,4,5,10,11,16,17,34,35,40,41,64,65,6,7,12,13,18,19,24..., dimensions={0} | all-to-all | bytes 1703936 | tf_op jit(solution)/shard_map/all_to_all | solution.py:210
  31.1 0.8 %shard_map.87 = (f32[16,4,256]{2,1,0:T(4,128)S(1)}, bf16[128,2,1280]{2,1,0:T(2,128)(2,1)S(1)}) custom-call(bf16[128,2,1664]{2,1,0:T(2,128)(2,1)S(1)} %all_to_all.10.arrived, f32[16,256]{1,0:T(8,128)S(1)} %get-tuple-element.12.sst, s32[16,256]{1,0:T(8,128)S(1)} %get-tuple-element.13.marine), custom_call_target="tpu_custom_call" | custom-call | tf_op jit(solution)/shard_map/pallas_call | solution.py:245
  31.9 19.1 %all_to_all.11.returned = bf16[128,2,1280]{2,1,0:T(2,128)(2,1)S(1)} all-to-all(bf16[128,2,1280]{2,1,0:T(2,128)(2,1)S(1)} %get-tuple-element.14), channel_id=1, replica_groups={{0,1,2,3,8,9,32,33,4,5,10,11,16,17,34,35,40,41,64,65,6,7,12,13,18,19,24..., dimensions={0} | all-to-all | bytes 1310720 | tf_op jit(solution)/shard_map/all_to_all | solution.py:210
  51.0 0.0 copy-done
  51.0 0.0 copy-done.1
  51.0 1.7 %shard_map.88 = (f32[16,4,256]{2,1,0:T(4,128)}, f32[5,16,256]{2,1,0:T(8,128)}) custom-call(s32[1,16]{1,0:T(1,128)S(1)} %bitcast.3, s32[1,16]{1,0:T(1,128)S(1)} %get-tuple-element.10.places, bf16[128,2,1280]{2,1,0:T(2,128)(2,1)S(1)} %all_to_all.11.returned, bf16[16,256,256]{2,1,0:T(8,128)(2,1)S(1)} %copy-done, f32[16,4,256]{2,1,0:T(4,128)S(1)} %get-tuple-element.15.fluxes), custom_call_target="tpu_custom_call" | custom-call | tf_op jit(solution)/shard_map/pallas_call | solution.py:252
Async XLA Ops:
  2.6 48.4 %copy-start = (bf16[16,256,256]{2,1,0:T(8,128)(2,1)S(1)}, bf16[16,256,256]{2,1,0:T(8,128)(2,1)}, u32[]{:S(2)}) copy-start(bf16[16,256,256]{2,1,0:T(8,128)(2,1)} %weights.1) | copy-start | bytes 6291460
  2.6 48.4 %copy-start.1 = (s32[16]{0:T(128)S(1)}, s32[16]{0:T(128)}, u32[]{:S(2)}) copy-start(s32[16]{0:T(128)} %src_hbm.1) | copy-start | bytes 196

commit v14 on v13

--- a/solution.py
+++ b/solution.py
@@ -155,7 +155,7 @@
 
 
 def deliver(
-    src_row, places, returned, weights, fluxes, fluxes_hbm, out, values, terms, sums, sem
+    src_row, places, returned, weights, fluxes, fluxes_hbm, out, values, sums, sem
 ):
     copy = pltpu.make_async_copy(fluxes, fluxes_hbm, sem)
     copy.start()
@@ -180,13 +180,9 @@
             (((1,), (1,)), ((), ())),
             preferred_element_type=F32,
         )
-        for h in range(2):
-            terms[h, block, :] = term[:, h * LANES : (h + 1) * LANES]
-    for p in range(PAIRS):
-        block = pl.ds(p * FIELDS, FIELDS)
         at = pl.ds(pl.multiple_of(src[p] * FIELDS, FIELDS), FIELDS)
         for h in range(2):
-            sums[h, at, :] += terms[h, block, :]
+            sums[h, at, :] += term[:, h * LANES : (h + 1) * LANES]
     for f in range(BACK):
         for h in range(2):
             out[f, :, h * LANES : (h + 1) * LANES] = sums[h, pl.ds(f, TILES, stride=FIELDS), :]
@@ -256,7 +252,6 @@
         out_specs=(HBM, VMEM),
         scratch_shapes=[
             pltpu.VMEM((2, PAIRS * FIELDS, LANES), F32),
-            pltpu.VMEM((2, PAIRS * FIELDS, LANES), F32),
             pltpu.VMEM((2, TILES * FIELDS, LANES), F32),
             pltpu.SemaphoreType.DMA,
         ],

time: 52.9 us -> 52.9 us (level)
  no operation moved by 1% of the time
where the time goes in v14:
time: 52.9 us; the launch traced here: 52.7 us
  blocking collectives  47.6 us (90%)
  Pallas kernels  4.43 us (8%)
  between operations  0.66 us (1%)
    all_to_all x2, blocking collectives, swap(): lax.all_to_all(x, ('gx', 'gy'), split_axis=0, concat_axis=0, axis_index_g...  47.6 us
    pallas_call x1, Pallas kernels, on_device(): pl.pallas_call(contribute, out_shape=(wire(OUT_WIDTH), jax.ShapeDtypeStru...  1.91 us
    pallas_call x1, Pallas kernels, on_device(): pl.pallas_call(deliver, out_shape=(flux_shape, jax.ShapeDtypeStruct((BACK...  1.72 us

profile of v14, /device:TPU:1, one launch (start us, length us, event | category | flops | bytes accessed | tf_op | source)
XLA Modules:
  0.0 52.7 jit_solution(1942076305105756761)
XLA Ops:
  0.6 1.9 %shard_map.86 = (bf16[128,2,1664]{2,1,0:T(2,128)(2,1)S(1)}, f32[16,256]{1,0:T(8,128)S(1)}, s32[16,256]{1,0:T(8,128)S(1)}, s32[1,16]{1,0:T(1,128)S(1)}) custom-call(s32[16]{0:T(128)} %src_hbm.1, s32[16]{0:T(128)} %bitcast.4, s32[16]{0:T(128)} %sea_hbm.1, bf16[16,8,256]{2,1,0:T(8,128)(2,1)} %sky_hbm.1, bf16[16,256,256]{2,1,0:T(8,128)(2,1)} %weights.1, ...), custom_call_target="tpu_custom_call" | custom-call | tf_op jit(solution)/shard_map/pallas_call | solution.py:218
  2.6 0.0 copy-start
  2.6 0.0 copy-start.1
  2.6 28.5 %all_to_all.10.arrived = bf16[128,2,1664]{2,1,0:T(2,128)(2,1)S(1)} all-to-all(bf16[128,2,1664]{2,1,0:T(2,128)(2,1)S(1)} %get-tuple-element.11), channel_id=1, replica_groups={{0,1,2,3,8,9,32,33,4,5,10,11,16,17,34,35,40,41,64,65,6,7,12,13,18,19,24..., dimensions={0} | all-to-all | bytes 1703936 | tf_op jit(solution)/shard_map/all_to_all | solution.py:206
  31.1 0.8 %shard_map.87 = (f32[16,4,256]{2,1,0:T(4,128)S(1)}, bf16[128,2,1280]{2,1,0:T(2,128)(2,1)S(1)}) custom-call(bf16[128,2,1664]{2,1,0:T(2,128)(2,1)S(1)} %all_to_all.10.arrived, f32[16,256]{1,0:T(8,128)S(1)} %get-tuple-element.12.sst, s32[16,256]{1,0:T(8,128)S(1)} %get-tuple-element.13.marine), custom_call_target="tpu_custom_call" | custom-call | tf_op jit(solution)/shard_map/pallas_call | solution.py:241
  31.9 19.1 %all_to_all.11.returned = bf16[128,2,1280]{2,1,0:T(2,128)(2,1)S(1)} all-to-all(bf16[128,2,1280]{2,1,0:T(2,128)(2,1)S(1)} %get-tuple-element.14), channel_id=1, replica_groups={{0,1,2,3,8,9,32,33,4,5,10,11,16,17,34,35,40,41,64,65,6,7,12,13,18,19,24..., dimensions={0} | all-to-all | bytes 1310720 | tf_op jit(solution)/shard_map/all_to_all | solution.py:206
  51.0 0.0 copy-done
  51.0 0.0 copy-done.1
  51.0 1.7 %shard_map.88 = (f32[16,4,256]{2,1,0:T(4,128)}, f32[5,16,256]{2,1,0:T(8,128)}) custom-call(s32[1,16]{1,0:T(1,128)S(1)} %bitcast.3, s32[1,16]{1,0:T(1,128)S(1)} %get-tuple-element.10.places, bf16[128,2,1280]{2,1,0:T(2,128)(2,1)S(1)} %all_to_all.11.returned, bf16[16,256,256]{2,1,0:T(8,128)(2,1)S(1)} %copy-done, f32[16,4,256]{2,1,0:T(4,128)S(1)} %get-tuple-element.15.fluxes), custom_call_target="tpu_custom_call" | custom-call | tf_op jit(solution)/shard_map/pallas_call | solution.py:248
Async XLA Ops:
  2.6 48.4 %copy-start = (bf16[16,256,256]{2,1,0:T(8,128)(2,1)S(1)}, bf16[16,256,256]{2,1,0:T(8,128)(2,1)}, u32[]{:S(2)}) copy-start(bf16[16,256,256]{2,1,0:T(8,128)(2,1)} %weights.1) | copy-start | bytes 6291460
  2.6 48.4 %copy-start.1 = (s32[16]{0:T(128)S(1)}, s32[16]{0:T(128)}, u32[]{:S(2)}) copy-start(s32[16]{0:T(128)} %src_hbm.1) | copy-start | bytes 196

commit v15 on v14

--- a/solution.py
+++ b/solution.py
@@ -129,11 +129,17 @@
 def exchange(arrived, sst, marine, fluxes, out):
     rows = arrived.shape[0] * arrived.shape[1]
     slots = arrived[...].reshape(rows, OUT_WIDTH)
-    first = jnp.where(iota((LANES, TILES), 0) == 0, 1.0, 0.0).astype(BF)
-    label = jnp.dot(slots[:, SENT * CELLS :], first, preferred_element_type=F32)
+    tail = slots[:, SENT * CELLS :]
+    first = jnp.where(iota((TILES, LANES), 1) == 0, 1.0, 0.0).astype(BF)
+
+    def against(a, b):
+        return lax.dot_general(a, b, (((1,), (1,)), ((), ())), preferred_element_type=F32)
+
+    wanted = (iota((TILES, rows), 0) + 1).astype(F32)
+    summed = jnp.where(against(first, tail) == wanted, 1.0, 0.0).astype(BF)
     tile = (iota((rows, TILES), 1) + 1).astype(F32)
-    chosen = jnp.where(label == tile, 1.0, 0.0).astype(BF)
-    total = lax.dot_general(chosen, slots, (((0,), (0,)), ((), ())), preferred_element_type=F32)
+    chosen = jnp.where(against(tail, first) == tile, 1.0, 0.0).astype(BF)
+    total = jnp.dot(summed, slots, preferred_element_type=F32)
     u, v, ta, q, rad, pr = (total[:, f * CELLS : (f + 1) * CELLS] for f in range(SENT))
     rest = jnp.where(iota((TILES, LANES), 1) == 0, 0.0, total[:, SENT * CELLS :])
     u = jnp.concatenate([u[:, :LANES] + rest, u[:, LANES:]], axis=1)

time: 52.9 us -> 52.9 us (level)
  no operation moved by 1% of the time
where the time goes in v15:
time: 52.9 us; the launch traced here: 52.7 us
  blocking collectives  47.6 us (90%)
  Pallas kernels  4.4 us (8%)
  between operations  0.66 us (1%)
    all_to_all x2, blocking collectives, swap(): lax.all_to_all(x, ('gx', 'gy'), split_axis=0, concat_axis=0, axis_index_g...  47.6 us
    pallas_call x1, Pallas kernels, on_device(): pl.pallas_call(contribute, out_shape=(wire(OUT_WIDTH), jax.ShapeDtypeStru...  1.91 us
    pallas_call x1, Pallas kernels, on_device(): pl.pallas_call(deliver, out_shape=(flux_shape, jax.ShapeDtypeStruct((BACK...  1.72 us

profile of v15, /device:TPU:1, one launch (start us, length us, event | category | flops | bytes accessed | tf_op | source)
XLA Modules:
  0.0 52.7 jit_solution(8544562046344896841)
XLA Ops:
  0.6 1.9 %shard_map.86 = (bf16[128,2,1664]{2,1,0:T(2,128)(2,1)S(1)}, f32[16,256]{1,0:T(8,128)S(1)}, s32[16,256]{1,0:T(8,128)S(1)}, s32[1,16]{1,0:T(1,128)S(1)}) custom-call(s32[16]{0:T(128)} %src_hbm.1, s32[16]{0:T(128)} %bitcast.4, s32[16]{0:T(128)} %sea_hbm.1, bf16[16,8,256]{2,1,0:T(8,128)(2,1)} %sky_hbm.1, bf16[16,256,256]{2,1,0:T(8,128)(2,1)} %weights.1, ...), custom_call_target="tpu_custom_call" | custom-call | tf_op jit(solution)/shard_map/pallas_call | solution.py:224
  2.5 0.0 copy-start
  2.6 0.0 copy-start.1
  2.6 28.5 %all_to_all.10.arrived = bf16[128,2,1664]{2,1,0:T(2,128)(2,1)S(1)} all-to-all(bf16[128,2,1664]{2,1,0:T(2,128)(2,1)S(1)} %get-tuple-element.11), channel_id=1, replica_groups={{0,1,2,3,8,9,32,33,4,5,10,11,16,17,34,35,40,41,64,65,6,7,12,13,18,19,24..., dimensions={0} | all-to-all | bytes 1703936 | tf_op jit(solution)/shard_map/all_to_all | solution.py:212
  31.1 0.8 %shard_map.87 = (f32[16,4,256]{2,1,0:T(4,128)S(1)}, bf16[128,2,1280]{2,1,0:T(2,128)(2,1)S(1)}) custom-call(bf16[128,2,1664]{2,1,0:T(2,128)(2,1)S(1)} %all_to_all.10.arrived, f32[16,256]{1,0:T(8,128)S(1)} %get-tuple-element.12.sst, s32[16,256]{1,0:T(8,128)S(1)} %get-tuple-element.13.marine), custom_call_target="tpu_custom_call" | custom-call | tf_op jit(solution)/shard_map/pallas_call | solution.py:247
  31.9 19.1 %all_to_all.11.returned = bf16[128,2,1280]{2,1,0:T(2,128)(2,1)S(1)} all-to-all(bf16[128,2,1280]{2,1,0:T(2,128)(2,1)S(1)} %get-tuple-element.14), channel_id=1, replica_groups={{0,1,2,3,8,9,32,33,4,5,10,11,16,17,34,35,40,41,64,65,6,7,12,13,18,19,24..., dimensions={0} | all-to-all | bytes 1310720 | tf_op jit(solution)/shard_map/all_to_all | solution.py:212
  51.0 0.0 copy-done
  51.0 0.0 copy-done.1
  51.0 1.7 %shard_map.88 = (f32[16,4,256]{2,1,0:T(4,128)}, f32[5,16,256]{2,1,0:T(8,128)}) custom-call(s32[1,16]{1,0:T(1,128)S(1)} %bitcast.3, s32[1,16]{1,0:T(1,128)S(1)} %get-tuple-element.10.places, bf16[128,2,1280]{2,1,0:T(2,128)(2,1)S(1)} %all_to_all.11.returned, bf16[16,256,256]{2,1,0:T(8,128)(2,1)S(1)} %copy-done, f32[16,4,256]{2,1,0:T(4,128)S(1)} %get-tuple-element.15.fluxes), custom_call_target="tpu_custom_call" | custom-call | tf_op jit(solution)/shard_map/pallas_call | solution.py:254
Async XLA Ops:
  2.5 48.4 %copy-start = (bf16[16,256,256]{2,1,0:T(8,128)(2,1)S(1)}, bf16[16,256,256]{2,1,0:T(8,128)(2,1)}, u32[]{:S(2)}) copy-start(bf16[16,256,256]{2,1,0:T(8,128)(2,1)} %weights.1) | copy-start | bytes 6291460
  2.6 48.4 %copy-start.1 = (s32[16]{0:T(128)S(1)}, s32[16]{0:T(128)}, u32[]{:S(2)}) copy-start(s32[16]{0:T(128)} %src_hbm.1) | copy-start | bytes 196

commit v16 on v15

--- a/solution.py
+++ b/solution.py
@@ -145,14 +145,14 @@
     u = jnp.concatenate([u[:, :LANES] + rest, u[:, LANES:]], axis=1)
     warmth = sst[...]
     w = marine[...].astype(F32)
-    speed = jnp.sqrt(u * u + v * v + 0.25)
+    square = u * u + v * v + 0.25
     dth = warmth - ta
     dq = 0.4 * warmth - q
     lift = 2.0 * (dth + 0.5 * dq)
-    c = jnp.ones_like(speed)
+    c = jnp.ones_like(square)
     for _ in range(3):
-        c = 1.0 + 0.5 * jnp.tanh(lift / (1.0 + c * speed * speed))
-    k = c * speed
+        c = 1.0 + 0.5 * jnp.tanh(lift / (1.0 + c * square))
+    k = c * jnp.sqrt(square)
     found = (k * u * w, k * v * w, (rad - k * dth - k * dq) * w, (pr - 0.5 * k * dq) * w)
     for f, x in enumerate(found):
         fluxes[:, f, :] = x

time: 52.9 us -> 52.9 us (level)
  no operation moved by 1% of the time
where the time goes in v16:
time: 52.9 us; the launch traced here: 52.7 us
  blocking collectives  47.6 us (90%)
  Pallas kernels  4.39 us (8%)
  between operations  0.66 us (1%)
    all_to_all x2, blocking collectives, swap(): lax.all_to_all(x, ('gx', 'gy'), split_axis=0, concat_axis=0, axis_index_g...  47.6 us
    pallas_call x1, Pallas kernels, on_device(): pl.pallas_call(contribute, out_shape=(wire(OUT_WIDTH), jax.ShapeDtypeStru...  1.91 us
    pallas_call x1, Pallas kernels, on_device(): pl.pallas_call(deliver, out_shape=(flux_shape, jax.ShapeDtypeStruct((BACK...  1.72 us

profile of v16, /device:TPU:1, one launch (start us, length us, event | category | flops | bytes accessed | tf_op | source)
XLA Modules:
  0.0 52.7 jit_solution(10606249011246984625)
XLA Ops:
  0.6 1.9 %shard_map.86 = (bf16[128,2,1664]{2,1,0:T(2,128)(2,1)S(1)}, f32[16,256]{1,0:T(8,128)S(1)}, s32[16,256]{1,0:T(8,128)S(1)}, s32[1,16]{1,0:T(1,128)S(1)}) custom-call(s32[16]{0:T(128)} %src_hbm.1, s32[16]{0:T(128)} %bitcast.4, s32[16]{0:T(128)} %sea_hbm.1, bf16[16,8,256]{2,1,0:T(8,128)(2,1)} %sky_hbm.1, bf16[16,256,256]{2,1,0:T(8,128)(2,1)} %weights.1, ...), custom_call_target="tpu_custom_call" | custom-call | tf_op jit(solution)/shard_map/pallas_call | solution.py:224
  2.6 0.0 copy-start
  2.6 0.0 copy-start.1
  2.6 28.5 %all_to_all.10.arrived = bf16[128,2,1664]{2,1,0:T(2,128)(2,1)S(1)} all-to-all(bf16[128,2,1664]{2,1,0:T(2,128)(2,1)S(1)} %get-tuple-element.11), channel_id=1, replica_groups={{0,1,2,3,8,9,32,33,4,5,10,11,16,17,34,35,40,41,64,65,6,7,12,13,18,19,24..., dimensions={0} | all-to-all | bytes 1703936 | tf_op jit(solution)/shard_map/all_to_all | solution.py:212
  31.1 0.8 %shard_map.87 = (f32[16,4,256]{2,1,0:T(4,128)S(1)}, bf16[128,2,1280]{2,1,0:T(2,128)(2,1)S(1)}) custom-call(bf16[128,2,1664]{2,1,0:T(2,128)(2,1)S(1)} %all_to_all.10.arrived, f32[16,256]{1,0:T(8,128)S(1)} %get-tuple-element.12.sst, s32[16,256]{1,0:T(8,128)S(1)} %get-tuple-element.13.marine), custom_call_target="tpu_custom_call" | custom-call | tf_op jit(solution)/shard_map/pallas_call | solution.py:247
  31.9 19.1 %all_to_all.11.returned = bf16[128,2,1280]{2,1,0:T(2,128)(2,1)S(1)} all-to-all(bf16[128,2,1280]{2,1,0:T(2,128)(2,1)S(1)} %get-tuple-element.14), channel_id=1, replica_groups={{0,1,2,3,8,9,32,33,4,5,10,11,16,17,34,35,40,41,64,65,6,7,12,13,18,19,24..., dimensions={0} | all-to-all | bytes 1310720 | tf_op jit(solution)/shard_map/all_to_all | solution.py:212
  51.0 0.0 copy-done
  51.0 0.0 copy-done.1
  51.0 1.7 %shard_map.88 = (f32[16,4,256]{2,1,0:T(4,128)}, f32[5,16,256]{2,1,0:T(8,128)}) custom-call(s32[1,16]{1,0:T(1,128)S(1)} %bitcast.3, s32[1,16]{1,0:T(1,128)S(1)} %get-tuple-element.10.places, bf16[128,2,1280]{2,1,0:T(2,128)(2,1)S(1)} %all_to_all.11.returned, bf16[16,256,256]{2,1,0:T(8,128)(2,1)S(1)} %copy-done, f32[16,4,256]{2,1,0:T(4,128)S(1)} %get-tuple-element.15.fluxes), custom_call_target="tpu_custom_call" | custom-call | tf_op jit(solution)/shard_map/pallas_call | solution.py:254
Async XLA Ops:
  2.6 48.4 %copy-start = (bf16[16,256,256]{2,1,0:T(8,128)(2,1)S(1)}, bf16[16,256,256]{2,1,0:T(8,128)(2,1)}, u32[]{:S(2)}) copy-start(bf16[16,256,256]{2,1,0:T(8,128)(2,1)} %weights.1) | copy-start | bytes 6291460
  2.6 48.4 %copy-start.1 = (s32[16]{0:T(128)S(1)}, s32[16]{0:T(128)}, u32[]{:S(2)}) copy-start(s32[16]{0:T(128)} %src_hbm.1) | copy-start | bytes 196
